TPU v7x, 32 devices: a whole 2x2x4 slice. The times are simulated.
32 devices in a mesh: tm: 8 (over z, y), roi: 4 (over x, core).
Axes of the slice: x: 2, y: 2, z: 4, core: 2. Of those that a mesh axis runs over, the one named last changes fastest.
Arguments:
- movie: bfloat16 [128, 128, 2048], P('tm', None, 'roi'), may hold values from -6 to 6
- coeffs: bfloat16 [5, 128, 2048], P(None, 'tm', 'roi'), may hold values from -3 to 3
- footprint_w: bfloat16 [512, 3, 512], P(('tm', 'roi')), may hold values from -0.15625 to 0.15625
- roi_blocks: int32 [512, 3], P('tm'), may hold values from 0 to 63, as said below
- roi_len: int32 [512], P('tm'), may hold values from 1 to 3
Outputs:
- delta_field: bfloat16 [128, 128, 2048], P(None, 'tm', 'roi')
- traces: float32 [512, 128], P(('tm', 'roi'))
Inputs may be any that keep to these rules, and one draw needn't show every extreme that they name: `roi_blocks`: entry m of ROI r names block slab * 16 + row: image row row of the group of r, inside column slab slab. The live entries of a ROI name distinct rows of one slab; entries past roi_len repeat the ROI's first entry. Over the 16 consecutive ROIs of one owner, the live entries from one slab name at most 3 distinct rows, and exactly 3 for some slab of every owner.
All inputs are finite; a program needn't handle non-finite values.
Results may differ from a plain program's by a relative error of at most 0.0049.
Values may be sent and summed in bfloat16 or wider, within the bound.
No kernel may reach another device: no remote copies, remote signals or barrier semaphores. Data moves between devices by JAX's collectives and lax.ppermute only.
A program may use at most 64 MiB of HBM per device.

v0:
```python
import jax
import jax.numpy as jnp
from jax import lax
from jax.sharding import PartitionSpec as P

BASE_WIN = 128


def temporal_filter(regrouped, coeffs):
    frames = regrouped.shape[0]
    tap_count = coeffs.shape[0]
    padded = jnp.pad(regrouped, ((tap_count - 1, 0), (0, 0), (0, 0)))
    filtered = jnp.zeros(regrouped.shape, jnp.float32)
    for delay_step in range(tap_count):
        lower = tap_count - 1 - delay_step
        filtered = filtered + coeffs[delay_step].astype(jnp.float32) * padded[
            lower : lower + frames
        ].astype(jnp.float32)
    return filtered.astype(jnp.bfloat16)


def local(movie, coeffs, footprint_w, roi_blocks, roi_len):
    regrouped = lax.all_to_all(movie, "tm", split_axis=1, concat_axis=0, tiled=True)
    frames, rows_here, slab_width = regrouped.shape
    filtered = temporal_filter(regrouped, coeffs)
    flat_filtered = filtered.reshape(frames, rows_here * slab_width)
    frame_later = lax.broadcasted_iota(jnp.int32, (frames, frames), 0)
    frame_earlier = lax.broadcasted_iota(jnp.int32, (frames, frames), 1)
    window_band = (
        (frame_earlier <= frame_later) & (frame_earlier > frame_later - BASE_WIN)
    ).astype(jnp.bfloat16)
    window_sum = jnp.dot(window_band, flat_filtered, preferred_element_type=jnp.float32)
    counts = jnp.minimum(jnp.arange(frames, dtype=jnp.int32) + 1, BASE_WIN).astype(jnp.float32)[
        :, None
    ]
    flat_delta = (flat_filtered.astype(jnp.float32) - window_sum / counts).astype(jnp.bfloat16)
    delta_field = flat_delta.reshape(frames, rows_here, slab_width)
    groups = lax.axis_size("roi")
    position = lax.axis_index("roi")
    roi_here = footprint_w.shape[0]
    slot_count = roi_blocks.shape[1]
    source = roi_blocks // rows_here
    local_row = roi_blocks % rows_here
    entry_used = jnp.arange(slot_count, dtype=jnp.int32)[None, :] < roi_len[:, None]
    own_source = lax.dynamic_slice_in_dim(source, position * roi_here, roi_here, 0)
    own_row = lax.dynamic_slice_in_dim(local_row, position * roi_here, roi_here, 0)
    own_used = lax.dynamic_slice_in_dim(entry_used, position * roi_here, roi_here, 0)
    row_ids = jnp.arange(rows_here, dtype=jnp.int32)
    slot_ids = jnp.arange(slot_count, dtype=jnp.int32)
    group_ids = jnp.arange(groups, dtype=jnp.int32)
    wanted = entry_used & (source == position)
    entry_hits = wanted[:, :, None] & (local_row[:, :, None] == row_ids)
    needed = jnp.any(entry_hits.reshape(groups, roi_here * slot_count, rows_here), axis=1)
    needed_count = needed.astype(jnp.int32)
    slot_order = jnp.cumsum(needed_count, axis=1) - needed_count
    picker = (needed[:, None, :] & (slot_order[:, None, :] == slot_ids[None, :, None])).astype(
        jnp.bfloat16
    )
    outgoing = jnp.einsum(
        "jcb,tbp->jctp", picker, delta_field, preferred_element_type=jnp.float32
    ).astype(jnp.bfloat16)
    incoming = lax.all_to_all(outgoing, "roi", split_axis=0, concat_axis=0, tiled=True)
    own_entries = (
        own_used[:, :, None, None]
        & (own_source[:, :, None, None] == group_ids[:, None])
        & (own_row[:, :, None, None] == row_ids)
    )
    need_own = jnp.any(own_entries.reshape(roi_here * slot_count, groups, rows_here), axis=0)
    need_count = need_own.astype(jnp.int32)
    own_order = jnp.cumsum(need_count, axis=1) - need_count
    entry_slot = jnp.sum(own_entries.astype(jnp.int32) * own_order, axis=(2, 3))
    chooser = (
        jnp.any(own_entries, axis=3)[:, :, :, None] & (entry_slot[:, :, None, None] == slot_ids)
    ).astype(jnp.bfloat16)
    dense_weights = jnp.einsum(
        "kmsc,kmp->scpk", chooser, footprint_w, preferred_element_type=jnp.float32
    ).astype(jnp.bfloat16)
    traces = jnp.einsum(
        "sctp,scpk->kt", incoming, dense_weights, preferred_element_type=jnp.float32
    )
    return (delta_field, traces)


def solution(mesh):
    placed = (
        P("tm", None, "roi"),
        P(None, "tm", "roi"),
        P(("tm", "roi"), None, None),
        P("tm", None),
        P("tm"),
    )
    return jax.shard_map(
        local,
        mesh=mesh,
        in_specs=placed,
        out_specs=(P(None, "tm", "roi"), P(("tm", "roi"), None)),
        check_vma=False,
    )
```

profile of v0, /device:TPU:0, one launch (start us, length us, event | category | flops | bytes accessed | tf_op | source)
XLA Modules:
  0.0 95.1 jit_solution(1538920751329038542)
XLA Ops:
  0.6 4.1 %copy.37 = bf16[16,128,512]{2,0,1:T(8,128)(2,1)} copy(bf16[16,128,512]{2,1,0:T(8,128)(2,1)} %param.5) | data formatting | bytes 4194304 | tf_op args[0]
  4.7 7.4 %all-to-all-start = ((bf16[16,128,512]{2,0,1:T(8,128)(2,1)}), bf16[16,128,512]{2,0,1:T(8,128)(2,1)S(1)}, u32[]{:S(2)}, u32[]{:S(2)}) async-start(bf16[16,128,512]{2,0,1:T(8,128)(2,1)} %copy.37), calls=%async_computation | async-start | bytes 4194304 | tf_op jit(solution)/shard_map/all_to_all | solution.py:23
  12.2 0.1 copy.46
  12.3 0.1 eq.128
  12.4 0.1 copy.45
  12.5 0.1 and.107
  12.6 0.2 fusion.18
  12.8 0.2 reduce_window_sum.18
  13.0 0.1 copy.42
  13.1 0.1 eq.119
  13.3 0.1 eq.115
  13.5 0.1 copy.40
  13.6 0.1 and.98
  13.8 46.6 %all-to-all-done = bf16[16,128,512]{2,0,1:T(8,128)(2,1)S(1)} async-done(((bf16[16,128,512]{2,0,1:T(8,128)(2,1)}), bf16[16,128,512]{2,0,1:T(8,128)(2,1)S(1)}, u32[]{:S(2)}, u32[]{:S(2)}) %all-to-all-start) | async-done | bytes 2097184 | tf_op jit(solution)/shard_map/all_to_all | solution.py:23
  60.4 1.2 %copy.38 = bf16[8,16,16,512]{3,2,1,0:T(8,128)(2,1)S(1)} copy(bf16[8,16,16,512]{3,1,2,0:T(8,128)(2,1)S(1)} %bitcast.42) | data formatting | bytes 4194304 | tf_op jit(solution)/shard_map/all_to_all | solution.py:23
  61.6 2.8 %add_convert_fusion = bf16[128,16,512]{2,1,0:T(8,128)(2,1)S(1)} fusion(bf16[128,16,512]{2,1,0:T(8,128)(2,1)S(1)} %bitcast.45, f32[16,512]{1,0:T(8,128)S(1)} %get-tuple-element.7, f32[16,512]{1,0:T(8,128)S(1)} %get-tuple-element.8, f32[16,512]{1,0:T(8,128)S(1)} %get-tuple-element.5, f32[16,512]{1,0:T(8,128)S(1)} %get-tuple-element.6, ...), kind=kLoop, calls=%fused_computation.3 | loop fusion | flops 15728640 | bytes 4358144 | tf_op jit(solution)/shard_map/convert_element_type | solution.py:19
  64.4 1.4 %copy.55 = bf16[16,8,16,512]{3,1,2,0:T(8,128)(2,1)S(1)} copy(bf16[16,8,16,512]{3,2,1,0:T(8,128)(2,1)S(1)} %bitcast.46) | data formatting | bytes 4194304
  65.8 0.8 fusion.1
  66.6 0.9 copy.56
  67.5 0.8 convolution_convert_fusion
  68.3 0.5 copy-done.1
  68.8 1.5 %copy.47 = bf16[4,3,128,512]{3,2,1,0:T(8,128)(2,1)} copy(bf16[4,3,128,512]{3,1,2,0:T(4,128)(2,1)S(1)} %convolution_convert_fusion) | data formatting | bytes 3145728 | tf_op jit(solution)/shard_map/convert_element_type | solution.py:61
  70.3 3.6 %all-to-all-start.1 = ((bf16[4,3,128,512]{3,2,1,0:T(8,128)(2,1)}), bf16[4,3,128,512]{3,2,1,0:T(8,128)(2,1)S(1)}, u32[]{:S(2)}, u32[]{:S(2)}) async-start(bf16[4,3,128,512]{3,2,1,0:T(8,128)(2,1)} %copy.47), calls=%async_computation.1 | async-start | bytes 3145728 | tf_op jit(solution)/shard_map/all_to_all | solution.py:62
  73.9 0.2 and_reduce_fusion.1
  74.1 0.2 reduce_window_sum.17
  74.3 0.2 fusion.9
  74.6 0.1 copy.43
  74.7 0.4 and_reduce_fusion
  75.0 0.1 copy.39
  75.2 0.2 fusion.4
  75.4 18.5 %all-to-all-done.1 = bf16[4,3,128,512]{3,2,1,0:T(8,128)(2,1)S(1)} async-done(((bf16[4,3,128,512]{3,2,1,0:T(8,128)(2,1)}), bf16[4,3,128,512]{3,2,1,0:T(8,128)(2,1)S(1)}, u32[]{:S(2)}, u32[]{:S(2)}) %all-to-all-start.1) | async-done | bytes 1572896 | tf_op jit(solution)/shard_map/all_to_all | solution.py:62
  93.9 1.1 %fusion.5 = f32[16,128]{1,0:T(8,128)} fusion(bf16[4,3,128,512]{3,2,1,0:T(8,128)(2,1)S(1)} %all-to-all-done.1, bf16[4,3,512,16]{2,0,1,3:T(4,128)(2,1)S(1)} %fusion.4), kind=kOutput, calls=%fused_computation.11 | convolution fusion | flops 25165824 | bytes 1777664 | tf_op jit(solution)/shard_map/sctp,scpk->kt/dot_general | solution.py:78
  (25 shorter events, 0.4 us)
Async XLA Ops:
  0.6 74.6 %copy-start = (bf16[16,3,512]{2,0,1:T(8,128)(2,1)S(1)}, bf16[16,3,512]{2,0,1:T(8,128)(2,1)}, u32[]{:S(2)}) copy-start(bf16[16,3,512]{2,0,1:T(8,128)(2,1)} %param.7) | copy-start | bytes 147460
  4.7 7.4 %copy-start.3 = (s32[64,3]{0,1:T(4,128)S(1)}, s32[64,3]{0,1:T(4,128)}, u32[]{:S(2)}) copy-start(s32[64,3]{0,1:T(4,128)} %param.8) | copy-start | bytes 2308
  4.7 7.6 %copy-start.4 = (s32[64]{0:T(128)S(1)}, s32[64]{0:T(128)}, u32[]{:S(2)}) copy-start(s32[64]{0:T(128)} %param.9) | copy-start | bytes 772
  4.7 9.0 %copy-start.2 = (bf16[5,16,512]{2,1,0:T(8,128)(2,1)S(1)}, bf16[5,16,512]{2,1,0:T(8,128)(2,1)}, u32[]{:S(2)}) copy-start(bf16[5,16,512]{2,1,0:T(8,128)(2,1)} %param.6) | copy-start | bytes 245764
  4.7 55.7 %all-to-all-start = ((bf16[16,128,512]{2,0,1:T(8,128)(2,1)}), bf16[16,128,512]{2,0,1:T(8,128)(2,1)S(1)}, u32[]{:S(2)}, u32[]{:S(2)}) async-start(bf16[16,128,512]{2,0,1:T(8,128)(2,1)} %copy.37), calls=%async_computation | async-start | bytes 4194304 | tf_op jit(solution)/shard_map/all_to_all | solution.py:23
  67.5 1.3 %copy-start.1 = (bf16[16,8,16,512]{3,2,1,0:T(8,128)(2,1)}, bf16[16,8,16,512]{3,2,1,0:T(8,128)(2,1)S(1)}, u32[]{:S(2)}) copy-start(bf16[16,8,16,512]{3,2,1,0:T(8,128)(2,1)S(1)} %copy.56) | copy-start | bytes 6291460
  70.3 23.6 %all-to-all-start.1 = ((bf16[4,3,128,512]{3,2,1,0:T(8,128)(2,1)}), bf16[4,3,128,512]{3,2,1,0:T(8,128)(2,1)S(1)}, u32[]{:S(2)}, u32[]{:S(2)}) async-start(bf16[4,3,128,512]{3,2,1,0:T(8,128)(2,1)} %copy.47), calls=%async_computation.1 | async-start | bytes 3145728 | tf_op jit(solution)/shard_map/all_to_all | solution.py:62
where the time goes:
time: 95.4 us; the launch traced here: 95.1 us
  waiting for transfers between devices  65.1 us (68%)
  local copies, waits for them, and re-layouts  11 us (12%)
  starting transfers between devices  11 us (12%)
  other arithmetic  4.24 us (4%)
  matrix products  2.94 us (3%)
    all_to_all x1, waiting for transfers between devices, local(): lax.all_to_all(movie, 'tm', split_axis=1, concat_axis=0, tiled=True)  46.6 us
    all_to_all x1, waiting for transfers between devices, local(): lax.all_to_all(outgoing, 'roi', split_axis=0, concat_axis=0, tiled=True)  18.5 us
    all_to_all x1, starting transfers between devices, local(): lax.all_to_all(movie, 'tm', split_axis=1, concat_axis=0, tiled=True)  7.41 us
    unnamed x13, local copies, waits for them, and re-layouts  6.87 us
    all_to_all x1, starting transfers between devices, local(): lax.all_to_all(outgoing, 'roi', split_axis=0, concat_axis=0, tiled=True)  3.56 us
    convert_element_type x1, other arithmetic, temporal_filter(): return filtered.astype(jnp.bfloat16)  2.76 us
  transfers between devices with their start and end apart: 2, of which 2 were waited for; matrix products, arithmetic and copies ran while one was open for 3% of the time, Pallas kernels for 0%

commit v1 on v0

v1 whole, which is shorter than its diff:
```python
import functools

import jax
import jax.numpy as jnp
from jax import lax
from jax.experimental import pallas as pl
from jax.experimental.pallas import tpu as pltpu
from jax.sharding import PartitionSpec as P

BASE_WIN = 128
LANES = 128


def chunk_kernel(
    ids_ref, inv_ref, coeff_ref, dense_ref, prev_ref, *rest, devices, owners
):
    blocks = rest[:devices]
    delta_ref = rest[devices]
    part_refs = rest[devices + 1 : devices + 1 + owners]
    pixels, filtered, delta32, partial = rest[devices + 1 + owners :]
    here = ids_ref[0]
    position = ids_ref[1]
    step, rows, width = blocks[0].shape
    taps = coeff_ref.shape[0]
    frames = devices * step
    for k in range(devices):
        start = pl.multiple_of((here ^ k) * step, step)
        pixels[pl.ds(start, step)] = blocks[k][...]

    for lane in range(0, width, LANES):
        span = slice(lane, lane + LANES)
        weights = [coeff_ref[k, :, span].astype(jnp.float32) for k in range(taps)]
        zero = jnp.zeros((rows, LANES), jnp.float32)

        def block_step(index, carry):
            running, history = carry[0], list(carry[1:])
            base = index * step
            for offset in range(step):
                frame = base + offset
                now = pixels[frame, :, span].astype(jnp.float32)
                total = weights[0] * now
                for k in range(1, taps):
                    total = total + weights[k] * history[k - 1]
                history = [now] + history[:-1]
                rounded = total.astype(jnp.bfloat16)
                value = rounded.astype(jnp.float32)
                running = running + value
                if frames > BASE_WIN:
                    filtered[frame, :, span] = rounded
                    gone = filtered[jnp.maximum(frame - BASE_WIN, 0), :, span]
                    running = running - jnp.where(
                        frame >= BASE_WIN, gone.astype(jnp.float32), 0.0
                    )
                delta = (value - running * inv_ref[frame]).astype(jnp.bfloat16)
                delta_ref[frame, :, span] = delta
                delta32[lane // LANES, pl.ds(frame * rows, rows), :] = delta.astype(
                    jnp.float32
                )
            return (running, *history)

        lax.fori_loop(0, devices, block_step, (zero,) * taps)

    total = prev_ref[...]
    for row in range(rows):
        picked = jnp.concatenate(
            [
                delta32[tile, pl.ds(row, frames, stride=rows), :].astype(jnp.bfloat16)
                for tile in range(width // LANES)
            ],
            axis=1,
        )
        total = total + lax.dot_general(
            dense_ref[row],
            picked,
            (((1,), (1,)), ((), ())),
            preferred_element_type=jnp.float32,
        )
    roi_here = total.shape[0] // owners
    partial[...] = total.reshape(owners, roi_here, frames)
    for k in range(owners):
        part_refs[k][...] = partial[position ^ k]


def run_chunk(ids, inverse, coeffs, dense, prev, blocks, owners):
    devices = len(blocks)
    step, rows, width = blocks[0].shape
    frames = devices * step
    rois = dense.shape[1]
    vmem = pl.BlockSpec(memory_space=pltpu.VMEM)
    smem = pl.BlockSpec(memory_space=pltpu.SMEM)
    held = frames if frames > BASE_WIN else 1
    return pl.pallas_call(
        functools.partial(chunk_kernel, devices=devices, owners=owners),
        out_shape=[jax.ShapeDtypeStruct((frames, rows, width), jnp.bfloat16)]
        + [jax.ShapeDtypeStruct((rois // owners, frames), jnp.float32)] * owners,
        in_specs=[smem, smem] + [vmem] * (3 + devices),
        out_specs=[vmem] * (1 + owners),
        scratch_shapes=[
            pltpu.VMEM((frames, rows, width), jnp.bfloat16),
            pltpu.VMEM((held, rows, width), jnp.bfloat16),
            pltpu.VMEM((width // LANES, frames * rows, LANES), jnp.float32),
            pltpu.VMEM((owners, rois // owners, frames), jnp.float32),
        ],
        compiler_params=pltpu.CompilerParams(vmem_limit_bytes=48 * 1024 * 1024),
        cost_estimate=pl.CostEstimate(
            flops=2 * frames * rows * width * rois,
            bytes_accessed=4 * frames * rows * width,
            transcendentals=0,
        ),
    )(ids, inverse, coeffs, dense, prev, *blocks)


def swaps(count, k):
    return [(i, i ^ k) for i in range(count)]


def local(movie, coeffs, footprint_w, roi_blocks, roi_len):
    devices = lax.axis_size("tm")
    owners = lax.axis_size("roi")
    here = lax.axis_index("tm")
    position = lax.axis_index("roi")
    step, _, slab_width = movie.shape
    rows = coeffs.shape[1]
    frames = devices * step
    slot_count = roi_blocks.shape[1]

    cuts = [0, slab_width - LANES, slab_width]
    order = list(range(devices - 1, 0, -1))
    chunks = []
    for low, high in zip(cuts[:-1], cuts[1:]):
        received = [None] * devices
        for k in order + [0]:
            block = lax.dynamic_slice(
                movie, (0, (here ^ k) * rows, low), (step, rows, high - low)
            )
            received[k] = lax.ppermute(block, "tm", swaps(devices, k)) if k else block
        chunks.append(received)

    gathered = lax.all_gather(footprint_w, "roi", axis=0, tiled=True)
    live = jnp.arange(slot_count, dtype=jnp.int32)[None, :] < roi_len[:, None]
    live = live & (roi_blocks // rows == position)
    hit = live[:, :, None] & (
        (roi_blocks % rows)[:, :, None] == jnp.arange(rows, dtype=jnp.int32)
    )
    dense = sum(
        jnp.where(hit[:, m, :].T[:, :, None], gathered[None, :, m, :], 0)
        for m in range(slot_count)
    ).astype(jnp.bfloat16)

    ids = jnp.stack([here, position]).astype(jnp.int32)
    counts = jnp.minimum(jnp.arange(frames, dtype=jnp.int32) + 1, BASE_WIN)
    inverse = 1.0 / counts.astype(jnp.float32)
    prev = jnp.zeros((dense.shape[1], frames), jnp.float32)
    deltas = []
    for low, high, received in zip(cuts[:-1], cuts[1:], chunks):
        delta, *parts = run_chunk(
            ids, inverse, coeffs[:, :, low:high], dense[:, :, low:high], prev, received, owners
        )
        deltas.append(delta)
        if high < slab_width:
            roi_here = parts[0].shape[0]
            stacked = jnp.stack(parts)
            back = jnp.arange(owners, dtype=jnp.int32) ^ position
            prev = stacked[back].reshape(owners * roi_here, frames)
    traces = parts[0]
    for k in range(1, owners):
        traces = traces + lax.ppermute(parts[k], "roi", swaps(owners, k))
    return jnp.concatenate(deltas, axis=2), traces


def solution(mesh):
    placed = (
        P("tm", None, "roi"),
        P(None, "tm", "roi"),
        P(("tm", "roi"), None, None),
        P("tm", None),
        P("tm"),
    )
    return jax.shard_map(
        local,
        mesh=mesh,
        in_specs=placed,
        out_specs=(P(None, "tm", "roi"), P(("tm", "roi"), None)),
        check_vma=False,
    )
```

time: 95.4 us -> 67.5 us (0.71)
  waiting for transfers between devices: 65.1 us -> 14.2 us
  starting transfers between devices: 11 us -> 33.6 us
  local copies, waits for them, and re-layouts: 11 us -> 4.22 us
  Pallas kernels: 0 us -> 5.87 us
  blocking collectives: 0 us -> 5.61 us
  matrix products: 2.94 us -> 0 us
  other arithmetic: 4.24 us -> 2.96 us
    all_to_all x2 -> x0, waiting for transfers between devices: 65.1 us -> none  [the longest x1 46.6 us: local(): lax.all_to_all(movie, 'tm', split_axis=1, concat_axis=0, tiled=True)]
    ppermute x0 -> x17, starting transfers between devices: none -> 33.6 us  [the longest x14 31.6 us: local(): received[k] = lax.ppermute(block, 'tm', swaps(devices, k)) if k else block]
    ppermute x0 -> x17, waiting for transfers between devices: none -> 14.2 us  [the longest x14 14 us: local(): received[k] = lax.ppermute(block, 'tm', swaps(devices, k)) if k else block]
    all_to_all x2 -> x0, starting transfers between devices: 11 us -> none  [the longest x1 7.41 us: local(): lax.all_to_all(movie, 'tm', split_axis=1, concat_axis=0, tiled=True)]
    unnamed x13 -> x8, local copies, waits for them, and re-layouts: 6.87 us -> 0.02 us
    pallas_call x0 -> x2, Pallas kernels: none -> 5.87 us  [run_chunk(): pl.pallas_call(functools.partial(chunk_kernel, devices=devices, owners=ow...]
    all_gather x0 -> x1, blocking collectives: none -> 5.61 us  [local(): gathered = lax.all_gather(footprint_w, 'roi', axis=0, tiled=True)]
    dynamic_slice x5 -> x2, local copies, waits for them, and re-layouts: 0.42 us -> 3.48 us  [local(): lax.dynamic_slice(movie, (0, (here ^ k) * rows, low), (step, rows, high -...]
  transfers between devices with their start and end apart: 2 -> 17, of which waited for: 2 -> 4; matrix products, arithmetic and copies ran while one was open for 3% -> 7% of each run, Pallas kernels for 0% -> 6%
where the time goes in v1:
time: 67.5 us; the launch traced here: 67.3 us
  starting transfers between devices  33.6 us (50%)
  waiting for transfers between devices  14.2 us (21%)
  Pallas kernels  5.87 us (9%)
  blocking collectives  5.61 us (8%)
  local copies, waits for them, and re-layouts  4.22 us (6%)
  other arithmetic  2.96 us (4%)
  between operations  0.89 us (1%)
    ppermute x14, starting transfers between devices, local(): received[k] = lax.ppermute(block, 'tm', swaps(devices, k)) if k else block  31.6 us
    ppermute x14, waiting for transfers between devices, local(): received[k] = lax.ppermute(block, 'tm', swaps(devices, k)) if k else block  14 us
    pallas_call x2, Pallas kernels, run_chunk(): pl.pallas_call(functools.partial(chunk_kernel, devices=devices, owners=ow...  5.87 us
    all_gather x1, blocking collectives, local(): gathered = lax.all_gather(footprint_w, 'roi', axis=0, tiled=True)  5.61 us
    dynamic_slice x2, local copies, waits for them, and re-layouts, local(): lax.dynamic_slice(movie, (0, (here ^ k) * rows, low), (step, rows, high -...  3.48 us
    ppermute x3, starting transfers between devices, local(): traces = traces + lax.ppermute(parts[k], 'roi', swaps(owners, k))  1.92 us
    concatenate x1, other arithmetic, local(): return (jnp.concatenate(deltas, axis=2), traces)  1.63 us
  transfers between devices with their start and end apart: 17, of which 4 were waited for; matrix products, arithmetic and copies ran while one was open for 7% of the time, Pallas kernels for 6%

profile of v1, /device:TPU:0, one launch (start us, length us, event | category | flops | bytes accessed | tf_op | source)
XLA Modules:
  0.0 67.3 jit_solution(9279703901396047533)
XLA Ops:
  0.7 1.7 %constant_dynamic-slice_fusion.8 = (bf16[16,16,384]{2,1,0:T(8,128)(2,1)S(1)}, bf16[16,16,384]{2,1,0:T(8,128)(2,1)S(1)}, bf16[16,16,384]{2,1,0:T(8,128)(2,1)S(1)}...) fusion(bf16[16,128,512]{2,1,0:T(8,128)(2,1)} %param.5, ...), kind=kLoop, calls=%fused_computation.22 | loop fusion | bytes 3145760 | tf_op jit(solution)/shard_map/dynamic_slice | solution.py:133
  2.4 0.0 copy-start
  2.4 3.0 %collective-permute-start = (bf16[16,16,384]{2,1,0:T(8,128)(2,1)S(1)}, bf16[16,16,384]{2,1,0:T(8,128)(2,1)S(1)}, u32[]{:S(2)}, u32[]{:S(2)}) collective-permute-start(bf16[16,16,384]{2,1,0:T(8,128)(2,1)S(1)} %get-tuple-element.36), channel_id=1, source_target_pairs={{0,4},{4,0},{8,12},{12,8},{16,20},{20,16},{24,28},{28,24},{1,5},{5... | collective-permute-start | bytes 589832 | tf_op jit(solution)/shard_map/ppermute | solution.py:136
  5.4 1.6 %collective-permute-start.1 = (bf16[16,16,384]{2,1,0:T(8,128)(2,1)S(1)}, bf16[16,16,384]{2,1,0:T(8,128)(2,1)S(1)}, u32[]{:S(2)}, u32[]{:S(2)}) collective-permute-start(bf16[16,16,384]{2,1,0:T(8,128)(2,1)S(1)} %get-tuple-element.35), channel_id=1, source_target_pairs={{0,8},{4,12},{8,0},{12,4},{16,24},{20,28},{24,16},{28,20},{1,9},{5... | collective-permute-start | bytes 589832 | tf_op jit(solution)/shard_map/ppermute | solution.py:136
  7.0 0.0 collective-permute-start.2
  7.0 3.0 %collective-permute-start.3 = (bf16[16,16,384]{2,1,0:T(8,128)(2,1)S(1)}, bf16[16,16,384]{2,1,0:T(8,128)(2,1)S(1)}, u32[]{:S(2)}, u32[]{:S(2)}) collective-permute-start(bf16[16,16,384]{2,1,0:T(8,128)(2,1)S(1)} %get-tuple-element.33), channel_id=1, source_target_pairs={{0,16},{4,20},{8,24},{12,28},{16,0},{20,4},{24,8},{28,12},{1,17},{... | collective-permute-start | bytes 589832 | tf_op jit(solution)/shard_map/ppermute | solution.py:136
  10.0 1.3 %collective-permute-start.4 = (bf16[16,16,384]{2,1,0:T(8,128)(2,1)S(1)}, bf16[16,16,384]{2,1,0:T(8,128)(2,1)S(1)}, u32[]{:S(2)}, u32[]{:S(2)}) collective-permute-start(bf16[16,16,384]{2,1,0:T(8,128)(2,1)S(1)} %get-tuple-element.32), channel_id=1, source_target_pairs={{0,20},{4,16},{8,28},{12,24},{16,4},{20,0},{24,12},{28,8},{1,21},{... | collective-permute-start | bytes 589832 | tf_op jit(solution)/shard_map/ppermute | solution.py:136
  11.3 1.8 %constant_dynamic-slice_fusion = (bf16[16,16,128]{2,1,0:T(8,128)(2,1)S(1)}, bf16[16,16,128]{2,1,0:T(8,128)(2,1)}, bf16[16,16,128]{2,1,0:T(8,128)(2,1)}, bf16[16,...) fusion(bf16[16,128,512]{2,1,0:T(8,128)(2,1)} %param.5, ...), kind=kLoop, calls=%fused_computation.14 | loop fusion | bytes 1048608 | tf_op jit(solution)/shard_map/dynamic_slice | solution.py:133
  13.2 5.6 %all_gather.3 = bf16[64,3,512]{2,0,1:T(8,128)(2,1)S(1)} all-gather(bf16[16,3,512]{2,0,1:T(8,128)(2,1)S(1)} %copy-done.1), channel_id=1, replica_groups=mesh['tm'=8,'roi'=4] {'roi'}, dimensions={0}, use_global_device_ids=true | all-gather | bytes 245760 | tf_op jit(solution)/shard_map/all_gather | solution.py:139
  18.8 0.6 select_add_fusion
  19.4 3.7 %collective-permute-start.5 = (bf16[16,16,384]{2,1,0:T(8,128)(2,1)S(1)}, bf16[16,16,384]{2,1,0:T(8,128)(2,1)S(1)}, u32[]{:S(2)}, u32[]{:S(2)}) collective-permute-start(bf16[16,16,384]{2,1,0:T(8,128)(2,1)S(1)} %get-tuple-element.31), channel_id=1, source_target_pairs={{0,24},{4,28},{8,16},{12,20},{16,8},{20,12},{24,0},{28,4},{1,25},{... | collective-permute-start | bytes 589832 | tf_op jit(solution)/shard_map/ppermute | solution.py:136
  23.1 0.0 collective-permute-start.6
  23.1 2.6 %collective-permute-start.7 = (bf16[16,16,128]{2,1,0:T(8,128)(2,1)}, bf16[16,16,128]{2,1,0:T(8,128)(2,1)S(1)}, u32[]{:S(2)}, u32[]{:S(2)}) collective-permute-start(bf16[16,16,128]{2,1,0:T(8,128)(2,1)} %get-tuple-element.27), channel_id=1, source_target_pairs={{0,4},{4,0},{8,12},{12,8},{16,20},{20,16},{24,28},{28,24},{1,5},{5... | collective-permute-start | bytes 196616 | tf_op jit(solution)/shard_map/ppermute | solution.py:136
  25.7 0.1 pad_add_fusion.ids_ref
  25.9 0.1 slice.48.dense_ref
  26.0 11.4 %collective-permute-done.4.rest_5_ = bf16[16,16,384]{2,1,0:T(8,128)(2,1)S(1)} collective-permute-done((bf16[16,16,384]{2,1,0:T(8,128)(2,1)S(1)}, bf16[16,16,384]{2,1,0:T(8,128)(2,1)S(1)}, u32[]{:S(2)}, u32[]{:S(2)}) %collective-permute-start.4) | collective-permute-done | bytes 196640 | tf_op jit(solution)/shard_map/ppermute | solution.py:136
  37.4 1.6 %collective-permute-start.9 = (bf16[16,16,128]{2,1,0:T(8,128)(2,1)}, bf16[16,16,128]{2,1,0:T(8,128)(2,1)S(1)}, u32[]{:S(2)}, u32[]{:S(2)}) collective-permute-start(bf16[16,16,128]{2,1,0:T(8,128)(2,1)} %get-tuple-element.25), channel_id=1, source_target_pairs={{0,12},{4,8},{8,4},{12,0},{16,28},{20,24},{24,20},{28,16},{1,13},{... | collective-permute-start | bytes 196616 | tf_op jit(solution)/shard_map/ppermute | solution.py:136
  39.0 5.3 %collective-permute-start.10 = (bf16[16,16,128]{2,1,0:T(8,128)(2,1)}, bf16[16,16,128]{2,1,0:T(8,128)(2,1)S(1)}, u32[]{:S(2)}, u32[]{:S(2)}) collective-permute-start(bf16[16,16,128]{2,1,0:T(8,128)(2,1)} %get-tuple-element.24), channel_id=1, source_target_pairs={{0,16},{4,20},{8,24},{12,28},{16,0},{20,4},{24,8},{28,12},{1,17},{... | collective-permute-start | bytes 196616 | tf_op jit(solution)/shard_map/ppermute | solution.py:136
  44.3 4.7 %collective-permute-start.11 = (bf16[16,16,128]{2,1,0:T(8,128)(2,1)}, bf16[16,16,128]{2,1,0:T(8,128)(2,1)S(1)}, u32[]{:S(2)}, u32[]{:S(2)}) collective-permute-start(bf16[16,16,128]{2,1,0:T(8,128)(2,1)} %get-tuple-element.23), channel_id=1, source_target_pairs={{0,20},{4,16},{8,28},{12,24},{16,4},{20,0},{24,12},{28,8},{1,21},{... | collective-permute-start | bytes 196616 | tf_op jit(solution)/shard_map/ppermute | solution.py:136
  49.0 4.4 %shard_map.68 = (bf16[128,16,384]{2,1,0:T(8,128)(2,1)S(1)}, f32[16,128]{1,0:T(8,128)S(1)}, f32[16,128]{1,0:T(8,128)S(1)}, f32[16,128]{1,0:T(8,128)S(1)}, f32[16,128]{1,0:T(8,128)S(1)}) custom-call(s32[2]{0:T(128)S(1)} %pad_add_fusion.ids_ref, f32[128]{0:T(128)S(1)} %convert_divide_fusion.inv_ref, bf16[5,16,384]{2,1,0:T(8,128)(2,1)S(1)} %slice.30.coeff_ref, ...), custom_call_target="tpu_custom_call" | custom-call | flops 100663296 | bytes 3145728 | tf_op jit(solution)/shard_map/pallas_call | solution.py:92
  53.4 0.6 collective-permute-start.12
  54.0 4.3 %collective-permute-start.13 = (bf16[16,16,128]{2,1,0:T(8,128)(2,1)S(1)}, bf16[16,16,128]{2,1,0:T(8,128)(2,1)S(1)}, u32[]{:S(2)}, u32[]{:S(2)}) collective-permute-start(bf16[16,16,128]{2,1,0:T(8,128)(2,1)S(1)} %get-tuple-element.22), channel_id=1, source_target_pairs={{0,28},{4,24},{8,20},{12,16},{16,12},{20,8},{24,4},{28,0},{1,29},{... | collective-permute-start | bytes 196616 | tf_op jit(solution)/shard_map/ppermute | solution.py:136
  58.3 0.5 gather_fusion
  58.8 0.9 %collective-permute-done.12.rest_6_ = bf16[16,16,128]{2,1,0:T(8,128)(2,1)S(1)} collective-permute-done((bf16[16,16,128]{2,1,0:T(8,128)(2,1)}, bf16[16,16,128]{2,1,0:T(8,128)(2,1)S(1)}, u32[]{:S(2)}, u32[]{:S(2)}) %collective-permute-start.12) | collective-permute-done | bytes 65568 | tf_op jit(solution)/shard_map/ppermute | solution.py:136
  59.7 1.7 %collective-permute-done.13.rest_7_ = bf16[16,16,128]{2,1,0:T(8,128)(2,1)S(1)} collective-permute-done((bf16[16,16,128]{2,1,0:T(8,128)(2,1)S(1)}, bf16[16,16,128]{2,1,0:T(8,128)(2,1)S(1)}, u32[]{:S(2)}, u32[]{:S(2)}) %collective-permute-start.13) | collective-permute-done | bytes 65568 | tf_op jit(solution)/shard_map/ppermute | solution.py:136
  61.4 1.5 %shard_map.69 = (bf16[128,16,128]{2,1,0:T(8,128)(2,1)S(1)}, f32[16,128]{1,0:T(8,128)S(1)}, f32[16,128]{1,0:T(8,128)S(1)}, f32[16,128]{1,0:T(8,128)S(1)}, f32[16,128]{1,0:T(8,128)S(1)}) custom-call(s32[2]{0:T(128)S(1)} %pad_add_fusion.ids_ref, f32[128]{0:T(128)S(1)} %convert_divide_fusion.inv_ref, bf16[5,16,128]{2,1,0:T(8,128)(2,1)S(1)} %slice.38.coeff_ref, ...), custom_call_target="tpu_custom_call" | custom-call | flops 33554432 | bytes 1048576 | tf_op jit(solution)/shard_map/pallas_call | solution.py:92
  62.9 0.1 collective-permute-start.16
  63.0 1.6 %collective-permute-start.15 = (f32[16,128]{1,0:T(8,128)S(1)}, f32[16,128]{1,0:T(8,128)S(1)}, u32[]{:S(2)}, u32[]{:S(2)}) collective-permute-start(f32[16,128]{1,0:T(8,128)S(1)} %get-tuple-element.20), channel_id=1, source_target_pairs={{0,2},{1,3},{2,0},{3,1},{4,6},{5,7},{6,4},{7,5},{8,10},{9,11},{10,... | collective-permute-start | bytes 24584 | tf_op jit(solution)/shard_map/ppermute | solution.py:167
  64.6 0.3 collective-permute-start.14
  64.9 1.6 %pad_maximum_fusion = bf16[128,16,512]{2,1,0:T(8,128)(2,1)} fusion(bf16[128,16,128]{2,1,0:T(8,128)(2,1)S(1)} %get-tuple-element.17, bf16[128,16,384]{2,1,0:T(8,128)(2,1)S(1)} %get-tuple-element.12), kind=kLoop, calls=%fused_computation.1 | loop fusion | flops 4194304 | bytes 4194304 | tf_op jit(solution)/shard_map/concatenate | solution.py:168
  66.5 0.2 collective-permute-done.15
  66.7 0.6 add_add_fusion
  (34 shorter events, 0.2 us)
Async XLA Ops:
  0.7 12.4 %copy-start.2 = (s32[64,3]{0,1:T(4,128)S(1)}, s32[64,3]{0,1:T(4,128)}, u32[]{:S(2)}) copy-start(s32[64,3]{0,1:T(4,128)} %param.8) | copy-start | bytes 2308
  0.7 12.4 %copy-start.3 = (s32[64]{0:T(128)S(1)}, s32[64]{0:T(128)}, u32[]{:S(2)}) copy-start(s32[64]{0:T(128)} %param.9) | copy-start | bytes 772
  0.7 12.5 %copy-start.1 = (bf16[16,3,512]{2,0,1:T(8,128)(2,1)S(1)}, bf16[16,3,512]{2,0,1:T(8,128)(2,1)}, u32[]{:S(2)}) copy-start(bf16[16,3,512]{2,0,1:T(8,128)(2,1)} %param.7) | copy-start | bytes 147460
  2.4 23.4 %copy-start = (bf16[5,16,512]{2,1,0:T(8,128)(2,1)S(1)}, bf16[5,16,512]{2,1,0:T(8,128)(2,1)}, u32[]{:S(2)}) copy-start(bf16[5,16,512]{2,1,0:T(8,128)(2,1)} %param.6) | copy-start | bytes 245764
  2.4 17.0 %collective-permute-start = (bf16[16,16,384]{2,1,0:T(8,128)(2,1)S(1)}, bf16[16,16,384]{2,1,0:T(8,128)(2,1)S(1)}, u32[]{:S(2)}, u32[]{:S(2)}) collective-permute-start(bf16[16,16,384]{2,1,0:T(8,128)(2,1)S(1)} %get-tuple-element.36), channel_id=1, source_target_pairs={{0,4},{4,0},{8,12},{12,8},{16,20},{20,16},{24,28},{28,24},{1,5},{5... | collective-permute-start | bytes 589832 | tf_op jit(solution)/shard_map/ppermute | solution.py:136
  5.4 17.7 %collective-permute-start.1 = (bf16[16,16,384]{2,1,0:T(8,128)(2,1)S(1)}, bf16[16,16,384]{2,1,0:T(8,128)(2,1)S(1)}, u32[]{:S(2)}, u32[]{:S(2)}) collective-permute-start(bf16[16,16,384]{2,1,0:T(8,128)(2,1)S(1)} %get-tuple-element.35), channel_id=1, source_target_pairs={{0,8},{4,12},{8,0},{12,4},{16,24},{20,28},{24,16},{28,20},{1,9},{5... | collective-permute-start | bytes 589832 | tf_op jit(solution)/shard_map/ppermute | solution.py:136
  7.0 16.1 %collective-permute-start.2 = (bf16[16,16,384]{2,1,0:T(8,128)(2,1)S(1)}, bf16[16,16,384]{2,1,0:T(8,128)(2,1)S(1)}, u32[]{:S(2)}, u32[]{:S(2)}) collective-permute-start(bf16[16,16,384]{2,1,0:T(8,128)(2,1)S(1)} %get-tuple-element.34), channel_id=1, source_target_pairs={{0,12},{4,8},{8,4},{12,0},{16,28},{20,24},{24,20},{28,16},{1,13},{... | collective-permute-start | bytes 589832 | tf_op jit(solution)/shard_map/ppermute | solution.py:136
  7.0 18.7 %collective-permute-start.3 = (bf16[16,16,384]{2,1,0:T(8,128)(2,1)S(1)}, bf16[16,16,384]{2,1,0:T(8,128)(2,1)S(1)}, u32[]{:S(2)}, u32[]{:S(2)}) collective-permute-start(bf16[16,16,384]{2,1,0:T(8,128)(2,1)S(1)} %get-tuple-element.33), channel_id=1, source_target_pairs={{0,16},{4,20},{8,24},{12,28},{16,0},{20,4},{24,8},{28,12},{1,17},{... | collective-permute-start | bytes 589832 | tf_op jit(solution)/shard_map/ppermute | solution.py:136
  10.0 27.4 %collective-permute-start.4 = (bf16[16,16,384]{2,1,0:T(8,128)(2,1)S(1)}, bf16[16,16,384]{2,1,0:T(8,128)(2,1)S(1)}, u32[]{:S(2)}, u32[]{:S(2)}) collective-permute-start(bf16[16,16,384]{2,1,0:T(8,128)(2,1)S(1)} %get-tuple-element.32), channel_id=1, source_target_pairs={{0,20},{4,16},{8,28},{12,24},{16,4},{20,0},{24,12},{28,8},{1,21},{... | collective-permute-start | bytes 589832 | tf_op jit(solution)/shard_map/ppermute | solution.py:136
  19.4 19.5 %collective-permute-start.5 = (bf16[16,16,384]{2,1,0:T(8,128)(2,1)S(1)}, bf16[16,16,384]{2,1,0:T(8,128)(2,1)S(1)}, u32[]{:S(2)}, u32[]{:S(2)}) collective-permute-start(bf16[16,16,384]{2,1,0:T(8,128)(2,1)S(1)} %get-tuple-element.31), channel_id=1, source_target_pairs={{0,24},{4,28},{8,16},{12,20},{16,8},{20,12},{24,0},{28,4},{1,25},{... | collective-permute-start | bytes 589832 | tf_op jit(solution)/shard_map/ppermute | solution.py:136
  23.1 21.2 %collective-permute-start.6 = (bf16[16,16,384]{2,1,0:T(8,128)(2,1)S(1)}, bf16[16,16,384]{2,1,0:T(8,128)(2,1)S(1)}, u32[]{:S(2)}, u32[]{:S(2)}) collective-permute-start(bf16[16,16,384]{2,1,0:T(8,128)(2,1)S(1)} %get-tuple-element.30), channel_id=1, source_target_pairs={{0,28},{4,24},{8,20},{12,16},{16,12},{20,8},{24,4},{28,0},{1,29},{... | collective-permute-start | bytes 589832 | tf_op jit(solution)/shard_map/ppermute | solution.py:136
  23.1 30.3 %collective-permute-start.7 = (bf16[16,16,128]{2,1,0:T(8,128)(2,1)}, bf16[16,16,128]{2,1,0:T(8,128)(2,1)S(1)}, u32[]{:S(2)}, u32[]{:S(2)}) collective-permute-start(bf16[16,16,128]{2,1,0:T(8,128)(2,1)} %get-tuple-element.27), channel_id=1, source_target_pairs={{0,4},{4,0},{8,12},{12,8},{16,20},{20,16},{24,28},{28,24},{1,5},{5... | collective-permute-start | bytes 196616 | tf_op jit(solution)/shard_map/ppermute | solution.py:136
  25.7 28.3 %collective-permute-start.8 = (bf16[16,16,128]{2,1,0:T(8,128)(2,1)}, bf16[16,16,128]{2,1,0:T(8,128)(2,1)S(1)}, u32[]{:S(2)}, u32[]{:S(2)}) collective-permute-start(bf16[16,16,128]{2,1,0:T(8,128)(2,1)} %get-tuple-element.26), channel_id=1, source_target_pairs={{0,8},{4,12},{8,0},{12,4},{16,24},{20,28},{24,16},{28,20},{1,9},{5... | collective-permute-start | bytes 196616 | tf_op jit(solution)/shard_map/ppermute | solution.py:136
  37.4 21.4 %collective-permute-start.9 = (bf16[16,16,128]{2,1,0:T(8,128)(2,1)}, bf16[16,16,128]{2,1,0:T(8,128)(2,1)S(1)}, u32[]{:S(2)}, u32[]{:S(2)}) collective-permute-start(bf16[16,16,128]{2,1,0:T(8,128)(2,1)} %get-tuple-element.25), channel_id=1, source_target_pairs={{0,12},{4,8},{8,4},{12,0},{16,28},{20,24},{24,20},{28,16},{1,13},{... | collective-permute-start | bytes 196616 | tf_op jit(solution)/shard_map/ppermute | solution.py:136
  39.0 19.8 %collective-permute-start.10 = (bf16[16,16,128]{2,1,0:T(8,128)(2,1)}, bf16[16,16,128]{2,1,0:T(8,128)(2,1)S(1)}, u32[]{:S(2)}, u32[]{:S(2)}) collective-permute-start(bf16[16,16,128]{2,1,0:T(8,128)(2,1)} %get-tuple-element.24), channel_id=1, source_target_pairs={{0,16},{4,20},{8,24},{12,28},{16,0},{20,4},{24,8},{28,12},{1,17},{... | collective-permute-start | bytes 196616 | tf_op jit(solution)/shard_map/ppermute | solution.py:136
  44.3 14.5 %collective-permute-start.11 = (bf16[16,16,128]{2,1,0:T(8,128)(2,1)}, bf16[16,16,128]{2,1,0:T(8,128)(2,1)S(1)}, u32[]{:S(2)}, u32[]{:S(2)}) collective-permute-start(bf16[16,16,128]{2,1,0:T(8,128)(2,1)} %get-tuple-element.23), channel_id=1, source_target_pairs={{0,20},{4,16},{8,28},{12,24},{16,4},{20,0},{24,12},{28,8},{1,21},{... | collective-permute-start | bytes 196616 | tf_op jit(solution)/shard_map/ppermute | solution.py:136
  53.4 6.3 %collective-permute-start.12 = (bf16[16,16,128]{2,1,0:T(8,128)(2,1)}, bf16[16,16,128]{2,1,0:T(8,128)(2,1)S(1)}, u32[]{:S(2)}, u32[]{:S(2)}) collective-permute-start(bf16[16,16,128]{2,1,0:T(8,128)(2,1)} %get-tuple-element.29), channel_id=1, source_target_pairs={{0,24},{4,28},{8,16},{12,20},{16,8},{20,12},{24,0},{28,4},{1,25},{... | collective-permute-start | bytes 196616 | tf_op jit(solution)/shard_map/ppermute | solution.py:136
  54.0 7.4 %collective-permute-start.13 = (bf16[16,16,128]{2,1,0:T(8,128)(2,1)S(1)}, bf16[16,16,128]{2,1,0:T(8,128)(2,1)S(1)}, u32[]{:S(2)}, u32[]{:S(2)}) collective-permute-start(bf16[16,16,128]{2,1,0:T(8,128)(2,1)S(1)} %get-tuple-element.22), channel_id=1, source_target_pairs={{0,28},{4,24},{8,20},{12,16},{16,12},{20,8},{24,4},{28,0},{1,29},{... | collective-permute-start | bytes 196616 | tf_op jit(solution)/shard_map/ppermute | solution.py:136
  62.9 3.6 %collective-permute-start.16 = (f32[16,128]{1,0:T(8,128)S(1)}, f32[16,128]{1,0:T(8,128)S(1)}, u32[]{:S(2)}, u32[]{:S(2)}) collective-permute-start(f32[16,128]{1,0:T(8,128)S(1)} %get-tuple-element.21), channel_id=1, source_target_pairs={{0,3},{1,2},{2,1},{3,0},{4,7},{5,6},{6,5},{7,4},{8,11},{9,10},{10,... | collective-permute-start | bytes 24584 | tf_op jit(solution)/shard_map/ppermute | solution.py:167
  63.0 3.7 %collective-permute-start.15 = (f32[16,128]{1,0:T(8,128)S(1)}, f32[16,128]{1,0:T(8,128)S(1)}, u32[]{:S(2)}, u32[]{:S(2)}) collective-permute-start(f32[16,128]{1,0:T(8,128)S(1)} %get-tuple-element.20), channel_id=1, source_target_pairs={{0,2},{1,3},{2,0},{3,1},{4,6},{5,7},{6,4},{7,5},{8,10},{9,11},{10,... | collective-permute-start | bytes 24584 | tf_op jit(solution)/shard_map/ppermute | solution.py:167
  64.6 2.2 %collective-permute-start.14 = (f32[16,128]{1,0:T(8,128)S(1)}, f32[16,128]{1,0:T(8,128)S(1)}, u32[]{:S(2)}, u32[]{:S(2)}) collective-permute-start(f32[16,128]{1,0:T(8,128)S(1)} %get-tuple-element.19), channel_id=1, source_target_pairs={{0,1},{1,0},{2,3},{3,2},{4,5},{5,4},{6,7},{7,6},{8,9},{9,8},{10,11... | collective-permute-start | bytes 24584 | tf_op jit(solution)/shard_map/ppermute | solution.py:167

commit v2 on v1

--- a/solution.py
+++ b/solution.py
@@ -12,20 +12,22 @@
 
 
 def chunk_kernel(
-    ids_ref, inv_ref, coeff_ref, dense_ref, prev_ref, *rest, devices, owners
+    ids_ref, inv_ref, coeff_ref, dense_ref, prev_ref, *rest, places, owners
 ):
+    devices = len(places)
     blocks = rest[:devices]
     delta_ref = rest[devices]
     part_refs = rest[devices + 1 : devices + 1 + owners]
     pixels, filtered, delta32, partial = rest[devices + 1 + owners :]
     here = ids_ref[0]
     position = ids_ref[1]
-    step, rows, width = blocks[0].shape
+    _, rows, width = pixels.shape
+    step = blocks[0].shape[0]
     taps = coeff_ref.shape[0]
     frames = devices * step
-    for k in range(devices):
+    for block, (k, offset) in zip(blocks, places):
         start = pl.multiple_of((here ^ k) * step, step)
-        pixels[pl.ds(start, step)] = blocks[k][...]
+        pixels[pl.ds(start, step)] = block[:, :, offset : offset + width]
 
     for lane in range(0, width, LANES):
         span = slice(lane, lane + LANES)
@@ -81,16 +83,17 @@
         part_refs[k][...] = partial[position ^ k]
 
 
-def run_chunk(ids, inverse, coeffs, dense, prev, blocks, owners):
+def run_chunk(ids, inverse, coeffs, dense, prev, blocks, places, owners):
     devices = len(blocks)
-    step, rows, width = blocks[0].shape
+    step = blocks[0].shape[0]
+    _, rows, width = coeffs.shape
     frames = devices * step
     rois = dense.shape[1]
     vmem = pl.BlockSpec(memory_space=pltpu.VMEM)
     smem = pl.BlockSpec(memory_space=pltpu.SMEM)
     held = frames if frames > BASE_WIN else 1
     return pl.pallas_call(
-        functools.partial(chunk_kernel, devices=devices, owners=owners),
+        functools.partial(chunk_kernel, places=tuple(places), owners=owners),
         out_shape=[jax.ShapeDtypeStruct((frames, rows, width), jnp.bfloat16)]
         + [jax.ShapeDtypeStruct((rois // owners, frames), jnp.float32)] * owners,
         in_specs=[smem, smem] + [vmem] * (3 + devices),
@@ -101,7 +104,7 @@
             pltpu.VMEM((width // LANES, frames * rows, LANES), jnp.float32),
             pltpu.VMEM((owners, rois // owners, frames), jnp.float32),
         ],
-        compiler_params=pltpu.CompilerParams(vmem_limit_bytes=48 * 1024 * 1024),
+        compiler_params=pltpu.CompilerParams(vmem_limit_bytes=24 * 1024 * 1024),
         cost_estimate=pl.CostEstimate(
             flops=2 * frames * rows * width * rois,
             bytes_accessed=4 * frames * rows * width,
@@ -124,17 +127,41 @@
     frames = devices * step
     slot_count = roi_blocks.shape[1]
 
-    cuts = [0, slab_width - LANES, slab_width]
-    order = list(range(devices - 1, 0, -1))
+    middle = slab_width // LANES // 2 * LANES
+    cuts = [0, middle, slab_width]
+    near = list(range(devices // 2 - 1, 0, -1))
+    far = list(range(devices - 1, devices // 2 - 1, -1))
+    first = [(k, 0, middle) for k in far]
+    whole = [(k, 0, slab_width) for k in near]
+    second = [(k, middle, slab_width) for k in far]
+    window = len(far) + 1
+    sends, finish = first + whole[:1], []
+    waiting, done = [], first[:-1] + whole[:1] + first[-1:] + whole[1:]
+    for index, item in enumerate(second):
+        waiting += [item] + whole[1 + index : 2 + index]
+    sends += waiting
+    finish = done[: len(waiting)]
+    arrived = {}
+    for turn, (k, low, high) in enumerate(sends):
+        block = lax.dynamic_slice(
+            movie, (0, (here ^ k) * rows, low), (step, rows, high - low)
+        )
+        if turn >= window and turn - window < len(finish):
+            before = finish[turn - window]
+            block, arrived[before] = lax.optimization_barrier((block, arrived[before]))
+        arrived[k, low, high] = lax.ppermute(block, "tm", swaps(devices, k))
+    arrived[0, 0, slab_width] = lax.dynamic_slice(
+        movie, (0, here * rows, 0), (step, rows, slab_width)
+    )
     chunks = []
     for low, high in zip(cuts[:-1], cuts[1:]):
-        received = [None] * devices
-        for k in order + [0]:
-            block = lax.dynamic_slice(
-                movie, (0, (here ^ k) * rows, low), (step, rows, high - low)
-            )
-            received[k] = lax.ppermute(block, "tm", swaps(devices, k)) if k else block
-        chunks.append(received)
+        chunks.append(
+            [
+                (block, (k, low - start))
+                for (k, start, end), block in arrived.items()
+                if start <= low and high <= end
+            ]
+        )
 
     gathered = lax.all_gather(footprint_w, "roi", axis=0, tiled=True)
     live = jnp.arange(slot_count, dtype=jnp.int32)[None, :] < roi_len[:, None]
@@ -154,7 +181,14 @@
     deltas = []
     for low, high, received in zip(cuts[:-1], cuts[1:], chunks):
         delta, *parts = run_chunk(
-            ids, inverse, coeffs[:, :, low:high], dense[:, :, low:high], prev, received, owners
+            ids,
+            inverse,
+            coeffs[:, :, low:high],
+            dense[:, :, low:high],
+            prev,
+            [block for block, _ in received],
+            [place for _, place in received],
+            owners,
         )
         deltas.append(delta)
         if high < slab_width:

time: 67.5 us -> 62.7 us (0.929)
  starting transfers between devices: 33.6 us -> 23.6 us
  waiting for transfers between devices: 14.2 us -> 19.6 us
    ppermute x14 -> x11, starting transfers between devices: 31.6 us -> 21.7 us  [local(): arrived[k, low, high] = lax.ppermute(block, 'tm', swaps(devices, k))]
    ppermute x14 -> x11, waiting for transfers between devices: 14 us -> 19.4 us  [local(): arrived[k, low, high] = lax.ppermute(block, 'tm', swaps(devices, k))]
    dynamic_slice x2 -> x1, local copies, waits for them, and re-layouts: 3.48 us -> 2.36 us  [local(): lax.dynamic_slice(movie, (0, (here ^ k) * rows, low), (step, rows, high -...]
    dynamic_slice x0 -> x1, local copies, waits for them, and re-layouts: none -> 0.87 us  [local(): lax.dynamic_slice(movie, (0, here * rows, 0), (step, rows, slab_width))]
  transfers between devices with their start and end apart: 17 -> 14, of which waited for: 4 -> 6; matrix products, arithmetic and copies ran while one was open for 7% -> 6% of each run, Pallas kernels for 6% -> 4%
where the time goes in v2:
time: 62.7 us; the launch traced here: 62.5 us
  starting transfers between devices  23.6 us (38%)
  waiting for transfers between devices  19.6 us (31%)
  blocking collectives  5.82 us (9%)
  Pallas kernels  5.72 us (9%)
  local copies, waits for them, and re-layouts  3.95 us (6%)
  other arithmetic  2.94 us (5%)
  between operations  0.82 us (1%)
    ppermute x11, starting transfers between devices, local(): arrived[k, low, high] = lax.ppermute(block, 'tm', swaps(devices, k))  21.7 us
    ppermute x11, waiting for transfers between devices, local(): arrived[k, low, high] = lax.ppermute(block, 'tm', swaps(devices, k))  19.4 us
    all_gather x1, blocking collectives, local(): gathered = lax.all_gather(footprint_w, 'roi', axis=0, tiled=True)  5.82 us
    pallas_call x2, Pallas kernels, run_chunk(): pl.pallas_call(functools.partial(chunk_kernel, places=tuple(places), owne...  5.72 us
    dynamic_slice x1, local copies, waits for them, and re-layouts, local(): lax.dynamic_slice(movie, (0, (here ^ k) * rows, low), (step, rows, high -...  2.36 us
    ppermute x3, starting transfers between devices, local(): traces = traces + lax.ppermute(parts[k], 'roi', swaps(owners, k))  1.92 us
    concatenate x1, other arithmetic, local(): return (jnp.concatenate(deltas, axis=2), traces)  1.61 us
  transfers between devices with their start and end apart: 14, of which 6 were waited for; matrix products, arithmetic and copies ran while one was open for 6% of the time, Pallas kernels for 4%

profile of v2, /device:TPU:0, one launch (start us, length us, event | category | flops | bytes accessed | tf_op | source)
XLA Modules:
  0.0 62.5 jit_solution(17281531186704078691)
XLA Ops:
  0.7 2.4 %constant_dynamic-slice_fusion.1 = (bf16[16,16,256]{2,1,0:T(8,128)(2,1)}, bf16[16,16,256]{2,1,0:T(8,128)(2,1)S(1)}, bf16[16,16,256]{2,1,0:T(8,128)(2,1)}, bf16[1...) fusion(bf16[16,128,512]{2,1,0:T(8,128)(2,1)} %param.5, ...), kind=kLoop, calls=%fused_computation.20 | loop fusion | bytes 2097168 | tf_op jit(solution)/shard_map/dynamic_slice | solution.py:146
  3.0 6.0 %collective-permute-start = (bf16[16,16,256]{2,1,0:T(8,128)(2,1)}, bf16[16,16,256]{2,1,0:T(8,128)(2,1)S(1)}, u32[]{:S(2)}, u32[]{:S(2)}) collective-permute-start(bf16[16,16,256]{2,1,0:T(8,128)(2,1)} %get-tuple-element.56), channel_id=1, source_target_pairs={{0,28},{4,24},{8,20},{12,16},{16,12},{20,8},{24,4},{28,0},{1,29},{... | collective-permute-start | bytes 393224 | tf_op jit(solution)/shard_map/ppermute | solution.py:152
  9.1 0.2 collective-permute-start.1
  9.3 0.7 %collective-permute-start.2 = (bf16[16,16,256]{2,1,0:T(8,128)(2,1)S(1)}, bf16[16,16,256]{2,1,0:T(8,128)(2,1)S(1)}, u32[]{:S(2)}, u32[]{:S(2)}) collective-permute-start(bf16[16,16,256]{2,1,0:T(8,128)(2,1)S(1)} %get-tuple-element.53), channel_id=1, source_target_pairs={{0,20},{4,16},{8,28},{12,24},{16,4},{20,0},{24,12},{28,8},{1,21},{... | collective-permute-start | bytes 393224 | tf_op jit(solution)/shard_map/ppermute | solution.py:152
  10.0 2.0 %collective-permute-start.3 = (bf16[16,16,256]{2,1,0:T(8,128)(2,1)S(1)}, bf16[16,16,256]{2,1,0:T(8,128)(2,1)S(1)}, u32[]{:S(2)}, u32[]{:S(2)}) collective-permute-start(bf16[16,16,256]{2,1,0:T(8,128)(2,1)S(1)} %get-tuple-element.51), channel_id=1, source_target_pairs={{0,16},{4,20},{8,24},{12,28},{16,0},{20,4},{24,8},{28,12},{1,17},{... | collective-permute-start | bytes 393224 | tf_op jit(solution)/shard_map/ppermute | solution.py:152
  12.0 0.9 %constant_dynamic-slice_fusion = (bf16[16,16,512]{2,1,0:T(8,128)(2,1)S(1)}, bf16[16,16,512]{2,1,0:T(8,128)(2,1)S(1)}, bf16[16,16,512]{2,1,0:T(8,128)(2,1)}, bf16[16,16,512]{2,1,0:T(8,128)(2,1)}) fusion(bf16[16,128,512]{2,1,0:T(8,128)(2,1)S(1)} %copy-done, s32[]{:T(128)S(6)} %select_n.72, s32[]{:T(128)S(6)} %select_n.71, s32[]{:T(128)S(6)} %select_n.70, ...), kind=kLoop, calls=%fused_computation.19 | loop fusion | bytes 2097168 | tf_op jit(solution)/shard_map/dynamic_slice | solution.py:153
  12.9 2.3 %collective-permute-start.4 = (bf16[16,16,512]{2,1,0:T(8,128)(2,1)S(1)}, bf16[16,16,512]{2,1,0:T(8,128)(2,1)S(1)}, u32[]{:S(2)}, u32[]{:S(2)}) collective-permute-start(bf16[16,16,512]{2,1,0:T(8,128)(2,1)S(1)} %get-tuple-element.47), channel_id=1, source_target_pairs={{0,12},{4,8},{8,4},{12,0},{16,28},{20,24},{24,20},{28,16},{1,13},{... | collective-permute-start | bytes 786440 | tf_op jit(solution)/shard_map/ppermute | solution.py:152
  15.3 5.8 %all_gather.3 = bf16[64,3,512]{2,0,1:T(8,128)(2,1)S(1)} all-gather(bf16[16,3,512]{2,0,1:T(8,128)(2,1)} %param.7), channel_id=1, replica_groups=mesh['tm'=8,'roi'=4] {'roi'}, dimensions={0}, use_global_device_ids=true | all-gather | bytes 245760 | tf_op jit(solution)/shard_map/all_gather | solution.py:166
  21.1 0.6 select_add_fusion
  21.7 0.1 fusion.5
  21.9 5.5 %collective-permute-start.5 = (bf16[16,16,512]{2,1,0:T(8,128)(2,1)}, bf16[16,16,512]{2,1,0:T(8,128)(2,1)S(1)}, u32[]{:S(2)}, u32[]{:S(2)}) collective-permute-start(bf16[16,16,512]{2,1,0:T(8,128)(2,1)} %get-tuple-element.29), channel_id=1, source_target_pairs={{0,8},{4,12},{8,0},{12,4},{16,24},{20,28},{24,16},{28,20},{1,9},{5... | collective-permute-start | bytes 786440 | tf_op jit(solution)/shard_map/ppermute | solution.py:152
  27.4 0.7 %collective-permute-start.6 = (bf16[16,16,512]{2,1,0:T(8,128)(2,1)}, bf16[16,16,512]{2,1,0:T(8,128)(2,1)S(1)}, u32[]{:S(2)}, u32[]{:S(2)}) collective-permute-start(bf16[16,16,512]{2,1,0:T(8,128)(2,1)} %get-tuple-element.31), channel_id=1, source_target_pairs={{0,4},{4,0},{8,12},{12,8},{16,20},{20,16},{24,28},{28,24},{1,5},{5... | collective-permute-start | bytes 786440 | tf_op jit(solution)/shard_map/ppermute | solution.py:152
  28.1 0.0 collective-permute-done.rest_0_
  28.1 1.7 %collective-permute-done.2.rest_2_ = bf16[16,16,256]{2,1,0:T(8,128)(2,1)S(1)} collective-permute-done((bf16[16,16,256]{2,1,0:T(8,128)(2,1)S(1)}, bf16[16,16,256]{2,1,0:T(8,128)(2,1)S(1)}, u32[]{:S(2)}, u32[]{:S(2)}) %collective-permute-start.2) | collective-permute-done | bytes 131104 | tf_op jit(solution)/shard_map/ppermute | solution.py:152
  29.8 1.9 %collective-permute-done.3.rest_3_ = bf16[16,16,256]{2,1,0:T(8,128)(2,1)S(1)} collective-permute-done((bf16[16,16,256]{2,1,0:T(8,128)(2,1)S(1)}, bf16[16,16,256]{2,1,0:T(8,128)(2,1)S(1)}, u32[]{:S(2)}, u32[]{:S(2)}) %collective-permute-start.3) | collective-permute-done | bytes 131104 | tf_op jit(solution)/shard_map/ppermute | solution.py:152
  31.7 2.4 %collective-permute-start.7 = (bf16[16,16,256]{2,1,0:T(8,128)(2,1)}, bf16[16,16,256]{2,1,0:T(8,128)(2,1)S(1)}, u32[]{:S(2)}, u32[]{:S(2)}) collective-permute-start(bf16[16,16,256]{2,1,0:T(8,128)(2,1)} %get-tuple-element.37), channel_id=1, source_target_pairs={{0,28},{4,24},{8,20},{12,16},{16,12},{20,8},{24,4},{28,0},{1,29},{... | collective-permute-start | bytes 393224 | tf_op jit(solution)/shard_map/ppermute | solution.py:152
  34.1 1.3 %collective-permute-start.8 = (bf16[16,16,256]{2,1,0:T(8,128)(2,1)}, bf16[16,16,256]{2,1,0:T(8,128)(2,1)S(1)}, u32[]{:S(2)}, u32[]{:S(2)}) collective-permute-start(bf16[16,16,256]{2,1,0:T(8,128)(2,1)} %get-tuple-element.38), channel_id=1, source_target_pairs={{0,24},{4,28},{8,16},{12,20},{16,8},{20,12},{24,0},{28,4},{1,25},{... | collective-permute-start | bytes 393224 | tf_op jit(solution)/shard_map/ppermute | solution.py:152
  35.4 0.0 collective-permute-start.9
  35.4 7.3 %collective-permute-done.5.rest_5_.rest_2_ = bf16[16,16,512]{2,1,0:T(8,128)(2,1)S(1)} collective-permute-done((bf16[16,16,512]{2,1,0:T(8,128)(2,1)}, bf16[16,16,512]{2,1,0:T(8,128)(2,1)S(1)}, u32[]{:S(2)}, u32[]{:S(2)}) %collective-permute-start.5) | collective-permute-done | bytes 262176 | tf_op jit(solution)/shard_map/ppermute | solution.py:152
  42.8 0.4 collective-permute-start.10
  43.2 0.1 pad_add_fusion.ids_ref
  43.3 2.6 %shard_map.68 = (bf16[128,16,256]{2,1,0:T(8,128)(2,1)S(1)}, f32[16,128]{1,0:T(8,128)S(1)}, f32[16,128]{1,0:T(8,128)S(1)}, f32[16,128]{1,0:T(8,128)S(1)}, f32[16,128]{1,0:T(8,128)S(1)}) custom-call(s32[2]{0:T(128)S(1)} %pad_add_fusion.ids_ref, f32[128]{0:T(128)S(1)} %convert_divide_fusion.inv_ref, bf16[5,16,256]{2,1,0:T(8,128)(2,1)S(1)} %get-tuple-element.63.coeff_ref, ...), custom_call_target="tpu_custom_call" | custom-call | flops 67108864 | bytes 2097152 | tf_op jit(solution)/shard_map/pallas_call | solution.py:95
  46.0 0.6 gather_fusion
  46.5 8.1 %collective-permute-done.9.rest_5_ = bf16[16,16,256]{2,1,0:T(8,128)(2,1)} collective-permute-done((bf16[16,16,256]{2,1,0:T(8,128)(2,1)}, bf16[16,16,256]{2,1,0:T(8,128)(2,1)}, u32[]{:S(2)}, u32[]{:S(2)}) %collective-permute-start.9) | collective-permute-done | bytes 131104 | tf_op jit(solution)/shard_map/ppermute | solution.py:152
  54.6 0.5 collective-permute-done.10.rest_6_
  55.0 3.1 %shard_map.69 = (bf16[128,16,256]{2,1,0:T(8,128)(2,1)S(1)}, f32[16,128]{1,0:T(8,128)S(1)}, f32[16,128]{1,0:T(8,128)S(1)}, f32[16,128]{1,0:T(8,128)S(1)}, f32[16,128]{1,0:T(8,128)S(1)}) custom-call(s32[2]{0:T(128)S(1)} %pad_add_fusion.ids_ref, f32[128]{0:T(128)S(1)} %convert_divide_fusion.inv_ref, bf16[5,16,256]{2,1,0:T(8,128)(2,1)S(1)} %get-tuple-element.64.coeff_ref, ...), custom_call_target="tpu_custom_call" | custom-call | flops 67108864 | bytes 2097152 | tf_op jit(solution)/shard_map/pallas_call | solution.py:95
  58.1 0.1 collective-permute-start.13
  58.2 1.6 %collective-permute-start.12 = (f32[16,128]{1,0:T(8,128)S(1)}, f32[16,128]{1,0:T(8,128)S(1)}, u32[]{:S(2)}, u32[]{:S(2)}) collective-permute-start(f32[16,128]{1,0:T(8,128)S(1)} %get-tuple-element.44), channel_id=1, source_target_pairs={{0,2},{1,3},{2,0},{3,1},{4,6},{5,7},{6,4},{7,5},{8,10},{9,11},{10,... | collective-permute-start | bytes 24584 | tf_op jit(solution)/shard_map/ppermute | solution.py:201
  59.8 0.3 collective-permute-start.11
  60.1 1.6 %pad_maximum_fusion = bf16[128,16,512]{2,1,0:T(8,128)(2,1)} fusion(bf16[128,16,256]{2,1,0:T(8,128)(2,1)S(1)} %get-tuple-element.41, bf16[128,16,256]{2,1,0:T(8,128)(2,1)S(1)} %get-tuple-element.32), kind=kLoop, calls=%fused_computation.1 | loop fusion | flops 4194304 | bytes 4194304 | tf_op jit(solution)/shard_map/concatenate | solution.py:202
  61.7 0.3 collective-permute-done.12
  61.9 0.6 add_add_fusion
  (26 shorter events, 0.1 us)
Async XLA Ops:
  0.6 11.4 %copy-start = (bf16[16,128,512]{2,1,0:T(8,128)(2,1)S(1)}, bf16[16,128,512]{2,1,0:T(8,128)(2,1)}, u32[]{:S(2)}) copy-start(bf16[16,128,512]{2,1,0:T(8,128)(2,1)} %param.5) | copy-start | bytes 6291460
  0.7 14.6 %copy-start.2 = (s32[64,3]{0,1:T(4,128)S(1)}, s32[64,3]{0,1:T(4,128)}, u32[]{:S(2)}) copy-start(s32[64,3]{0,1:T(4,128)} %param.8) | copy-start | bytes 2308
  0.7 14.6 %copy-start.3 = (s32[64]{0:T(128)S(1)}, s32[64]{0:T(128)}, u32[]{:S(2)}) copy-start(s32[64]{0:T(128)} %param.9) | copy-start | bytes 772
  3.0 25.1 %collective-permute-start = (bf16[16,16,256]{2,1,0:T(8,128)(2,1)}, bf16[16,16,256]{2,1,0:T(8,128)(2,1)S(1)}, u32[]{:S(2)}, u32[]{:S(2)}) collective-permute-start(bf16[16,16,256]{2,1,0:T(8,128)(2,1)} %get-tuple-element.56), channel_id=1, source_target_pairs={{0,28},{4,24},{8,20},{12,16},{16,12},{20,8},{24,4},{28,0},{1,29},{... | collective-permute-start | bytes 393224 | tf_op jit(solution)/shard_map/ppermute | solution.py:152
  9.1 12.8 %collective-permute-start.1 = (bf16[16,16,256]{2,1,0:T(8,128)(2,1)}, bf16[16,16,256]{2,1,0:T(8,128)(2,1)S(1)}, u32[]{:S(2)}, u32[]{:S(2)}) collective-permute-start(bf16[16,16,256]{2,1,0:T(8,128)(2,1)} %get-tuple-element.55), channel_id=1, source_target_pairs={{0,24},{4,28},{8,16},{12,20},{16,8},{20,12},{24,0},{28,4},{1,25},{... | collective-permute-start | bytes 393224 | tf_op jit(solution)/shard_map/ppermute | solution.py:152
  9.3 20.5 %collective-permute-start.2 = (bf16[16,16,256]{2,1,0:T(8,128)(2,1)S(1)}, bf16[16,16,256]{2,1,0:T(8,128)(2,1)S(1)}, u32[]{:S(2)}, u32[]{:S(2)}) collective-permute-start(bf16[16,16,256]{2,1,0:T(8,128)(2,1)S(1)} %get-tuple-element.53), channel_id=1, source_target_pairs={{0,20},{4,16},{8,28},{12,24},{16,4},{20,0},{24,12},{28,8},{1,21},{... | collective-permute-start | bytes 393224 | tf_op jit(solution)/shard_map/ppermute | solution.py:152
  10.0 21.7 %collective-permute-start.3 = (bf16[16,16,256]{2,1,0:T(8,128)(2,1)S(1)}, bf16[16,16,256]{2,1,0:T(8,128)(2,1)S(1)}, u32[]{:S(2)}, u32[]{:S(2)}) collective-permute-start(bf16[16,16,256]{2,1,0:T(8,128)(2,1)S(1)} %get-tuple-element.51), channel_id=1, source_target_pairs={{0,16},{4,20},{8,24},{12,28},{16,0},{20,4},{24,8},{28,12},{1,17},{... | collective-permute-start | bytes 393224 | tf_op jit(solution)/shard_map/ppermute | solution.py:152
  12.9 9.0 %copy-start.1 = (bf16[5,16,512]{2,1,0:T(8,128)(2,1)S(1)}, bf16[5,16,512]{2,1,0:T(8,128)(2,1)}, u32[]{:S(2)}) copy-start(bf16[5,16,512]{2,1,0:T(8,128)(2,1)} %param.6) | copy-start | bytes 245764
  12.9 14.5 %collective-permute-start.4 = (bf16[16,16,512]{2,1,0:T(8,128)(2,1)S(1)}, bf16[16,16,512]{2,1,0:T(8,128)(2,1)S(1)}, u32[]{:S(2)}, u32[]{:S(2)}) collective-permute-start(bf16[16,16,512]{2,1,0:T(8,128)(2,1)S(1)} %get-tuple-element.47), channel_id=1, source_target_pairs={{0,12},{4,8},{8,4},{12,0},{16,28},{20,24},{24,20},{28,16},{1,13},{... | collective-permute-start | bytes 786440 | tf_op jit(solution)/shard_map/ppermute | solution.py:152
  21.9 20.9 %collective-permute-start.5 = (bf16[16,16,512]{2,1,0:T(8,128)(2,1)}, bf16[16,16,512]{2,1,0:T(8,128)(2,1)S(1)}, u32[]{:S(2)}, u32[]{:S(2)}) collective-permute-start(bf16[16,16,512]{2,1,0:T(8,128)(2,1)} %get-tuple-element.29), channel_id=1, source_target_pairs={{0,8},{4,12},{8,0},{12,4},{16,24},{20,28},{24,16},{28,20},{1,9},{5... | collective-permute-start | bytes 786440 | tf_op jit(solution)/shard_map/ppermute | solution.py:152
  27.4 15.9 %collective-permute-start.6 = (bf16[16,16,512]{2,1,0:T(8,128)(2,1)}, bf16[16,16,512]{2,1,0:T(8,128)(2,1)S(1)}, u32[]{:S(2)}, u32[]{:S(2)}) collective-permute-start(bf16[16,16,512]{2,1,0:T(8,128)(2,1)} %get-tuple-element.31), channel_id=1, source_target_pairs={{0,4},{4,0},{8,12},{12,8},{16,20},{20,16},{24,28},{28,24},{1,5},{5... | collective-permute-start | bytes 786440 | tf_op jit(solution)/shard_map/ppermute | solution.py:152
  31.7 14.8 %collective-permute-start.7 = (bf16[16,16,256]{2,1,0:T(8,128)(2,1)}, bf16[16,16,256]{2,1,0:T(8,128)(2,1)S(1)}, u32[]{:S(2)}, u32[]{:S(2)}) collective-permute-start(bf16[16,16,256]{2,1,0:T(8,128)(2,1)} %get-tuple-element.37), channel_id=1, source_target_pairs={{0,28},{4,24},{8,20},{12,16},{16,12},{20,8},{24,4},{28,0},{1,29},{... | collective-permute-start | bytes 393224 | tf_op jit(solution)/shard_map/ppermute | solution.py:152
  34.1 12.4 %collective-permute-start.8 = (bf16[16,16,256]{2,1,0:T(8,128)(2,1)}, bf16[16,16,256]{2,1,0:T(8,128)(2,1)S(1)}, u32[]{:S(2)}, u32[]{:S(2)}) collective-permute-start(bf16[16,16,256]{2,1,0:T(8,128)(2,1)} %get-tuple-element.38), channel_id=1, source_target_pairs={{0,24},{4,28},{8,16},{12,20},{16,8},{20,12},{24,0},{28,4},{1,25},{... | collective-permute-start | bytes 393224 | tf_op jit(solution)/shard_map/ppermute | solution.py:152
  35.4 19.2 %collective-permute-start.9 = (bf16[16,16,256]{2,1,0:T(8,128)(2,1)}, bf16[16,16,256]{2,1,0:T(8,128)(2,1)}, u32[]{:S(2)}, u32[]{:S(2)}) collective-permute-start(bf16[16,16,256]{2,1,0:T(8,128)(2,1)} %get-tuple-element.39), channel_id=1, source_target_pairs={{0,20},{4,16},{8,28},{12,24},{16,4},{20,0},{24,12},{28,8},{1,21},{... | collective-permute-start | bytes 393224 | tf_op jit(solution)/shard_map/ppermute | solution.py:152
  42.8 12.3 %collective-permute-start.10 = (bf16[16,16,256]{2,1,0:T(8,128)(2,1)}, bf16[16,16,256]{2,1,0:T(8,128)(2,1)}, u32[]{:S(2)}, u32[]{:S(2)}) collective-permute-start(bf16[16,16,256]{2,1,0:T(8,128)(2,1)} %get-tuple-element.40), channel_id=1, source_target_pairs={{0,16},{4,20},{8,24},{12,28},{16,0},{20,4},{24,8},{28,12},{1,17},{... | collective-permute-start | bytes 393224 | tf_op jit(solution)/shard_map/ppermute | solution.py:152
  58.1 3.5 %collective-permute-start.13 = (f32[16,128]{1,0:T(8,128)S(1)}, f32[16,128]{1,0:T(8,128)S(1)}, u32[]{:S(2)}, u32[]{:S(2)}) collective-permute-start(f32[16,128]{1,0:T(8,128)S(1)} %get-tuple-element.45), channel_id=1, source_target_pairs={{0,3},{1,2},{2,1},{3,0},{4,7},{5,6},{6,5},{7,4},{8,11},{9,10},{10,... | collective-permute-start | bytes 24584 | tf_op jit(solution)/shard_map/ppermute | solution.py:201
  58.2 3.7 %collective-permute-start.12 = (f32[16,128]{1,0:T(8,128)S(1)}, f32[16,128]{1,0:T(8,128)S(1)}, u32[]{:S(2)}, u32[]{:S(2)}) collective-permute-start(f32[16,128]{1,0:T(8,128)S(1)} %get-tuple-element.44), channel_id=1, source_target_pairs={{0,2},{1,3},{2,0},{3,1},{4,6},{5,7},{6,4},{7,5},{8,10},{9,11},{10,... | collective-permute-start | bytes 24584 | tf_op jit(solution)/shard_map/ppermute | solution.py:201
  59.8 2.2 %collective-permute-start.11 = (f32[16,128]{1,0:T(8,128)S(1)}, f32[16,128]{1,0:T(8,128)S(1)}, u32[]{:S(2)}, u32[]{:S(2)}) collective-permute-start(f32[16,128]{1,0:T(8,128)S(1)} %get-tuple-element.43), channel_id=1, source_target_pairs={{0,1},{1,0},{2,3},{3,2},{4,5},{5,4},{6,7},{7,6},{8,9},{9,8},{10,11... | collective-permute-start | bytes 24584 | tf_op jit(solution)/shard_map/ppermute | solution.py:201

commit v3 on v2

--- a/solution.py
+++ b/solution.py
@@ -12,13 +12,14 @@
 
 
 def chunk_kernel(
-    ids_ref, inv_ref, coeff_ref, dense_ref, prev_ref, *rest, places, owners
+    ids_ref, inv_ref, coeff_ref, dense_ref, prev_ref, *rest, places, owners, last
 ):
     devices = len(places)
+    parts = owners if last else 1
     blocks = rest[:devices]
     delta_ref = rest[devices]
-    part_refs = rest[devices + 1 : devices + 1 + owners]
-    pixels, filtered, delta32, partial = rest[devices + 1 + owners :]
+    part_refs = rest[devices + 1 : devices + 1 + parts]
+    pixels, filtered, delta32, partial = rest[devices + 1 + parts :]
     here = ids_ref[0]
     position = ids_ref[1]
     _, rows, width = pixels.shape
@@ -78,12 +79,15 @@
             preferred_element_type=jnp.float32,
         )
     roi_here = total.shape[0] // owners
-    partial[...] = total.reshape(owners, roi_here, frames)
-    for k in range(owners):
-        part_refs[k][...] = partial[position ^ k]
-
-
-def run_chunk(ids, inverse, coeffs, dense, prev, blocks, places, owners):
+    if last:
+        partial[...] = total.reshape(owners, roi_here, frames)
+        for k in range(owners):
+            part_refs[k][...] = partial[position ^ k]
+    else:
+        part_refs[0][...] = total
+
+
+def run_chunk(ids, inverse, coeffs, dense, prev, blocks, places, owners, last):
     devices = len(blocks)
     step = blocks[0].shape[0]
     _, rows, width = coeffs.shape
@@ -92,12 +96,13 @@
     vmem = pl.BlockSpec(memory_space=pltpu.VMEM)
     smem = pl.BlockSpec(memory_space=pltpu.SMEM)
     held = frames if frames > BASE_WIN else 1
+    parts = owners if last else 1
     return pl.pallas_call(
-        functools.partial(chunk_kernel, places=tuple(places), owners=owners),
+        functools.partial(chunk_kernel, places=tuple(places), owners=owners, last=last),
         out_shape=[jax.ShapeDtypeStruct((frames, rows, width), jnp.bfloat16)]
-        + [jax.ShapeDtypeStruct((rois // owners, frames), jnp.float32)] * owners,
+        + [jax.ShapeDtypeStruct((rois // parts, frames), jnp.float32)] * parts,
         in_specs=[smem, smem] + [vmem] * (3 + devices),
-        out_specs=[vmem] * (1 + owners),
+        out_specs=[vmem] * (1 + parts),
         scratch_shapes=[
             pltpu.VMEM((frames, rows, width), jnp.bfloat16),
             pltpu.VMEM((held, rows, width), jnp.bfloat16),
@@ -131,28 +136,25 @@
     cuts = [0, middle, slab_width]
     near = list(range(devices // 2 - 1, 0, -1))
     far = list(range(devices - 1, devices // 2 - 1, -1))
-    first = [(k, 0, middle) for k in far]
-    whole = [(k, 0, slab_width) for k in near]
-    second = [(k, middle, slab_width) for k in far]
-    window = len(far) + 1
-    sends, finish = first + whole[:1], []
-    waiting, done = [], first[:-1] + whole[:1] + first[-1:] + whole[1:]
-    for index, item in enumerate(second):
-        waiting += [item] + whole[1 + index : 2 + index]
-    sends += waiting
-    finish = done[: len(waiting)]
+    split = far[len(far) // 2 :]
+    opening = [(k, 0, slab_width) for k in far[: len(far) // 2]]
+    beside = [(k, 0, slab_width) for k in near]
+    first = [(k, 0, middle) for k in split]
+    second = [(k, middle, slab_width) for k in split]
+    ties = dict(zip(first + second, beside[::-1][: len(first) - 1] + opening + first))
+
+    def rows_of(source, k, low, high):
+        return lax.dynamic_slice(source, (0, (here ^ k) * rows, low), (step, rows, high - low))
+
+    blocks = [rows_of(movie, *item) for item in opening]
+    rest, *blocks = lax.optimization_barrier((movie, *blocks))
     arrived = {}
-    for turn, (k, low, high) in enumerate(sends):
-        block = lax.dynamic_slice(
-            movie, (0, (here ^ k) * rows, low), (step, rows, high - low)
-        )
-        if turn >= window and turn - window < len(finish):
-            before = finish[turn - window]
-            block, arrived[before] = lax.optimization_barrier((block, arrived[before]))
-        arrived[k, low, high] = lax.ppermute(block, "tm", swaps(devices, k))
-    arrived[0, 0, slab_width] = lax.dynamic_slice(
-        movie, (0, here * rows, 0), (step, rows, slab_width)
-    )
+    for item in opening + beside + first + second:
+        block = blocks.pop(0) if blocks else rows_of(rest, *item)
+        if item in ties:
+            block, arrived[ties[item]] = lax.optimization_barrier((block, arrived[ties[item]]))
+        arrived[item] = lax.ppermute(block, "tm", swaps(devices, item[0]))
+    arrived[0, 0, slab_width] = rows_of(rest, 0, 0, slab_width)
     chunks = []
     for low, high in zip(cuts[:-1], cuts[1:]):
         chunks.append(
@@ -189,13 +191,10 @@
             [block for block, _ in received],
             [place for _, place in received],
             owners,
+            high == slab_width,
         )
         deltas.append(delta)
-        if high < slab_width:
-            roi_here = parts[0].shape[0]
-            stacked = jnp.stack(parts)
-            back = jnp.arange(owners, dtype=jnp.int32) ^ position
-            prev = stacked[back].reshape(owners * roi_here, frames)
+        prev = parts[0]
     traces = parts[0]
     for k in range(1, owners):
         traces = traces + lax.ppermute(parts[k], "roi", swaps(owners, k))

time: 62.7 us -> 60.8 us (0.970)
  waiting for transfers between devices: 19.6 us -> 18 us
  starting transfers between devices: 23.6 us -> 24.3 us
    ppermute x11 -> x9, waiting for transfers between devices: 19.4 us -> 16.8 us  [local(): arrived[item] = lax.ppermute(block, 'tm', swaps(devices, item[0]))]
    ppermute x3, waiting for transfers between devices: 0.26 us -> 1.16 us  [local(): traces = traces + lax.ppermute(parts[k], 'roi', swaps(owners, k))]
    ppermute x11 -> x9, starting transfers between devices: 21.7 us -> 22.4 us  [local(): arrived[item] = lax.ppermute(block, 'tm', swaps(devices, item[0]))]
    dynamic_slice x2 -> x3, local copies, waits for them, and re-layouts: 3.23 us -> 3.49 us  [rows_of(): lax.dynamic_slice(source, (0, (here ^ k) * rows, low), (step, rows, high...]
  transfers between devices with their start and end apart: 14 -> 12, of which waited for: 6 -> 6; matrix products, arithmetic and copies ran while one was open for 6% -> 8% of each run, Pallas kernels for 4% -> 4%
where the time goes in v3:
time: 60.8 us; the launch traced here: 60.6 us
  starting transfers between devices  24.3 us (40%)
  waiting for transfers between devices  18 us (30%)
  blocking collectives  5.61 us (9%)
  Pallas kernels  5.28 us (9%)
  local copies, waits for them, and re-layouts  3.66 us (6%)
  other arithmetic  2.93 us (5%)
  between operations  0.81 us (1%)
    ppermute x9, starting transfers between devices, local(): arrived[item] = lax.ppermute(block, 'tm', swaps(devices, item[0]))  22.4 us
    ppermute x9, waiting for transfers between devices, local(): arrived[item] = lax.ppermute(block, 'tm', swaps(devices, item[0]))  16.8 us
    all_gather x1, blocking collectives, local(): gathered = lax.all_gather(footprint_w, 'roi', axis=0, tiled=True)  5.61 us
    pallas_call x2, Pallas kernels, run_chunk(): pl.pallas_call(functools.partial(chunk_kernel, places=tuple(places), owne...  5.28 us
    dynamic_slice x3, local copies, waits for them, and re-layouts, rows_of(): lax.dynamic_slice(source, (0, (here ^ k) * rows, low), (step, rows, high...  3.49 us
    ppermute x3, starting transfers between devices, local(): traces = traces + lax.ppermute(parts[k], 'roi', swaps(owners, k))  1.93 us
    concatenate x1, other arithmetic, local(): return (jnp.concatenate(deltas, axis=2), traces)  1.61 us
  transfers between devices with their start and end apart: 12, of which 6 were waited for; matrix products, arithmetic and copies ran while one was open for 8% of the time, Pallas kernels for 4%

profile of v3, /device:TPU:0, one launch (start us, length us, event | category | flops | bytes accessed | tf_op | source)
XLA Modules:
  0.0 60.6 jit_solution(4012993461247595143)
XLA Ops:
  0.7 1.1 %constant_dynamic-slice_fusion.8 = (bf16[16,16,512]{2,1,0:T(8,128)(2,1)S(1)}, bf16[16,16,512]{2,1,0:T(8,128)(2,1)S(1)}) fusion(bf16[16,128,512]{2,1,0:T(8,128)(2,1)} %param.5, s32[]{:T(128)S(6)} %select_n.54, s32[]{:T(128)S(6)} %select_n.53), kind=kLoop, calls=%fused_computation.24 | loop fusion | bytes 1048584 | tf_op jit(solution)/shard_map/dynamic_slice | solution.py:147
  1.8 6.1 %collective-permute-start = (bf16[16,16,512]{2,1,0:T(8,128)(2,1)S(1)}, bf16[16,16,512]{2,1,0:T(8,128)(2,1)S(1)}, u32[]{:S(2)}, u32[]{:S(2)}) collective-permute-start(bf16[16,16,512]{2,1,0:T(8,128)(2,1)S(1)} %get-tuple-element.21), channel_id=1, source_target_pairs={{0,28},{4,24},{8,20},{12,16},{16,12},{20,8},{24,4},{28,0},{1,29},{... | collective-permute-start | bytes 786440 | tf_op jit(solution)/shard_map/ppermute | solution.py:156
  7.8 0.2 collective-permute-start.1
  8.0 1.3 %constant_dynamic-slice_fusion = (bf16[16,16,512]{2,1,0:T(8,128)(2,1)S(1)}, bf16[16,16,512]{2,1,0:T(8,128)(2,1)S(1)}, bf16[16,16,512]{2,1,0:T(8,128)(2,1)S(1)}, bf16[16,16,512]{2,1,0:T(8,128)(2,1)S(1)}) fusion(bf16[16,128,512]{2,1,0:T(8,128)(2,1)} %param.5, s32[]{:T(128)S(6)} %select_n.60, s32[]{:T(128)S(6)} %select_n.59, s32[]{:T(128)S(6)} %select_n.58, ...), kind=kLoop, calls=%fused_computation.16 | loop fusion | bytes 2097168 | tf_op jit(solution)/shard_map/dynamic_slice | solution.py:147
  9.3 0.5 collective-permute-start.4
  9.8 0.0 collective-permute-start.3
  9.8 3.1 %collective-permute-start.2 = (bf16[16,16,512]{2,1,0:T(8,128)(2,1)S(1)}, bf16[16,16,512]{2,1,0:T(8,128)(2,1)S(1)}, u32[]{:S(2)}, u32[]{:S(2)}) collective-permute-start(bf16[16,16,512]{2,1,0:T(8,128)(2,1)S(1)} %get-tuple-element.41), channel_id=1, source_target_pairs={{0,12},{4,8},{8,4},{12,0},{16,28},{20,24},{24,20},{28,16},{1,13},{... | collective-permute-start | bytes 786440 | tf_op jit(solution)/shard_map/ppermute | solution.py:156
  13.0 5.6 %all_gather.3 = bf16[64,3,512]{2,0,1:T(8,128)(2,1)S(1)} all-gather(bf16[16,3,512]{2,0,1:T(8,128)(2,1)S(1)} %copy-done.1), channel_id=1, replica_groups=mesh['tm'=8,'roi'=4] {'roi'}, dimensions={0}, use_global_device_ids=true | all-gather | bytes 245760 | tf_op jit(solution)/shard_map/all_gather | solution.py:168
  18.6 0.0 copy-start
  18.6 0.6 select_add_fusion
  19.2 0.1 fusion.4
  19.3 1.2 %constant_dynamic-slice_fusion.1 = (bf16[16,16,256]{2,1,0:T(8,128)(2,1)S(1)}, bf16[16,16,256]{2,1,0:T(8,128)(2,1)S(1)}, bf16[16,16,256]{2,1,0:T(8,128)(2,1)S(1)}, bf16[16,16,256]{2,1,0:T(8,128)(2,1)S(1)}) fusion(bf16[16,128,512]{2,1,0:T(8,128)(2,1)} %param.5, s32[]{:T(128)S(6)} %select_n.55, s32[]{:T(128)S(6)} %select_n.56), kind=kLoop, calls=%fused_computation.17 | loop fusion | bytes 1048584 | tf_op jit(solution)/shard_map/dynamic_slice | solution.py:147
  20.5 2.2 %collective-permute-start.5 = (bf16[16,16,256]{2,1,0:T(8,128)(2,1)S(1)}, bf16[16,16,256]{2,1,0:T(8,128)(2,1)S(1)}, u32[]{:S(2)}, u32[]{:S(2)}) collective-permute-start(bf16[16,16,256]{2,1,0:T(8,128)(2,1)S(1)} %get-tuple-element.26), channel_id=1, source_target_pairs={{0,20},{4,16},{8,28},{12,24},{16,4},{20,0},{24,12},{28,8},{1,21},{... | collective-permute-start | bytes 393224 | tf_op jit(solution)/shard_map/ppermute | solution.py:156
  22.7 0.0 collective-permute-done.1.rest_1_
  22.7 10.3 %collective-permute-start.6 = (bf16[16,16,256]{2,1,0:T(8,128)(2,1)S(1)}, bf16[16,16,256]{2,1,0:T(8,128)(2,1)S(1)}, u32[]{:S(2)}, u32[]{:S(2)}) collective-permute-start(bf16[16,16,256]{2,1,0:T(8,128)(2,1)S(1)} %get-tuple-element.28), channel_id=1, source_target_pairs={{0,16},{4,20},{8,24},{12,28},{16,0},{20,4},{24,8},{28,12},{1,17},{... | collective-permute-start | bytes 393224 | tf_op jit(solution)/shard_map/ppermute | solution.py:156
  33.1 10.7 %collective-permute-done.5.rest_5_ = bf16[16,16,256]{2,1,0:T(8,128)(2,1)S(1)} collective-permute-done((bf16[16,16,256]{2,1,0:T(8,128)(2,1)S(1)}, bf16[16,16,256]{2,1,0:T(8,128)(2,1)S(1)}, u32[]{:S(2)}, u32[]{:S(2)}) %collective-permute-start.5) | collective-permute-done | bytes 131104 | tf_op jit(solution)/shard_map/ppermute | solution.py:156
  43.7 0.0 collective-permute-start.8
  43.8 0.1 pad_add_fusion.ids_ref
  43.8 0.0 collective-permute-done.3.rest_3_
  43.8 0.0 collective-permute-done.2.rest_2_
  43.8 2.7 %collective-permute-done.6.rest_6_ = bf16[16,16,256]{2,1,0:T(8,128)(2,1)S(1)} collective-permute-done((bf16[16,16,256]{2,1,0:T(8,128)(2,1)S(1)}, bf16[16,16,256]{2,1,0:T(8,128)(2,1)S(1)}, u32[]{:S(2)}, u32[]{:S(2)}) %collective-permute-start.6) | collective-permute-done | bytes 131104 | tf_op jit(solution)/shard_map/ppermute | solution.py:156
  46.5 2.6 %shard_map.68 = (bf16[128,16,256]{2,1,0:T(8,128)(2,1)S(1)}, f32[64,128]{1,0:T(8,128)S(1)}) custom-call(s32[2]{0:T(128)S(1)} %pad_add_fusion.ids_ref, f32[128]{0:T(128)S(1)} %convert_divide_fusion.inv_ref, bf16[5,16,256]{2,1,0:T(8,128)(2,1)S(1)} %get-tuple-element.53.coeff_ref, bf16[16,64,256]{2,1,0:T(8,128)(2,1)S(1)} %get-tuple-element.48.dense_ref, ...), custom_call_target="tpu_custom_call" | custom-call | flops 67108864 | bytes 2097152 | tf_op jit(solution)/shard_map/pallas_call | solution.py:100
  49.1 1.6 %collective-permute-done.7.rest_5_ = bf16[16,16,256]{2,1,0:T(8,128)(2,1)S(1)} collective-permute-done((bf16[16,16,256]{2,1,0:T(8,128)(2,1)S(1)}, bf16[16,16,256]{2,1,0:T(8,128)(2,1)S(1)}, u32[]{:S(2)}, u32[]{:S(2)}) %collective-permute-start.7) | collective-permute-done | bytes 131104 | tf_op jit(solution)/shard_map/ppermute | solution.py:156
  50.8 1.8 %collective-permute-done.8.rest_6_ = bf16[16,16,256]{2,1,0:T(8,128)(2,1)S(1)} collective-permute-done((bf16[16,16,256]{2,1,0:T(8,128)(2,1)S(1)}, bf16[16,16,256]{2,1,0:T(8,128)(2,1)S(1)}, u32[]{:S(2)}, u32[]{:S(2)}) %collective-permute-start.8) | collective-permute-done | bytes 131104 | tf_op jit(solution)/shard_map/ppermute | solution.py:156
  52.6 2.6 %shard_map.69 = (bf16[128,16,256]{2,1,0:T(8,128)(2,1)S(1)}, f32[16,128]{1,0:T(8,128)S(1)}, f32[16,128]{1,0:T(8,128)S(1)}, f32[16,128]{1,0:T(8,128)S(1)}, f32[16,128]{1,0:T(8,128)S(1)}) custom-call(s32[2]{0:T(128)S(1)} %pad_add_fusion.ids_ref, f32[128]{0:T(128)S(1)} %convert_divide_fusion.inv_ref, bf16[5,16,256]{2,1,0:T(8,128)(2,1)S(1)} %get-tuple-element.54.coeff_ref, ...), custom_call_target="tpu_custom_call" | custom-call | flops 67108864 | bytes 2097152 | tf_op jit(solution)/shard_map/pallas_call | solution.py:100
  55.3 0.1 collective-permute-start.9
  55.3 1.6 %collective-permute-start.10 = (f32[16,128]{1,0:T(8,128)S(1)}, f32[16,128]{1,0:T(8,128)S(1)}, u32[]{:S(2)}, u32[]{:S(2)}) collective-permute-start(f32[16,128]{1,0:T(8,128)S(1)} %get-tuple-element.36), channel_id=1, source_target_pairs={{0,2},{1,3},{2,0},{3,1},{4,6},{5,7},{6,4},{7,5},{8,10},{9,11},{10,... | collective-permute-start | bytes 24584 | tf_op jit(solution)/shard_map/ppermute | solution.py:200
  56.9 0.3 collective-permute-start.11
  57.2 1.6 %pad_maximum_fusion = bf16[128,16,512]{2,1,0:T(8,128)(2,1)} fusion(bf16[128,16,256]{2,1,0:T(8,128)(2,1)S(1)} %get-tuple-element.33, bf16[128,16,256]{2,1,0:T(8,128)(2,1)S(1)} %get-tuple-element.29), kind=kLoop, calls=%fused_computation | loop fusion | flops 4194304 | bytes 4194304 | tf_op jit(solution)/shard_map/concatenate | solution.py:201
  58.8 0.2 collective-permute-done.10
  59.0 0.9 %collective-permute-done.11 = f32[16,128]{1,0:T(8,128)S(1)} collective-permute-done((f32[16,128]{1,0:T(8,128)S(1)}, f32[16,128]{1,0:T(8,128)S(1)}, u32[]{:S(2)}, u32[]{:S(2)}) %collective-permute-start.11) | collective-permute-done | bytes 8224 | tf_op jit(solution)/shard_map/ppermute | solution.py:200
  60.0 0.6 add_add_fusion
  (19 shorter events, 0.1 us)
Async XLA Ops:
  0.6 12.2 %copy-start.2 = (s32[64,3]{0,1:T(4,128)S(1)}, s32[64,3]{0,1:T(4,128)}, u32[]{:S(2)}) copy-start(s32[64,3]{0,1:T(4,128)} %param.8) | copy-start | bytes 2308
  0.6 12.2 %copy-start.3 = (s32[64]{0:T(128)S(1)}, s32[64]{0:T(128)}, u32[]{:S(2)}) copy-start(s32[64]{0:T(128)} %param.9) | copy-start | bytes 772
  0.7 12.3 %copy-start.1 = (bf16[16,3,512]{2,0,1:T(8,128)(2,1)S(1)}, bf16[16,3,512]{2,0,1:T(8,128)(2,1)}, u32[]{:S(2)}) copy-start(bf16[16,3,512]{2,0,1:T(8,128)(2,1)} %param.7) | copy-start | bytes 147460
  1.8 21.0 %collective-permute-start = (bf16[16,16,512]{2,1,0:T(8,128)(2,1)S(1)}, bf16[16,16,512]{2,1,0:T(8,128)(2,1)S(1)}, u32[]{:S(2)}, u32[]{:S(2)}) collective-permute-start(bf16[16,16,512]{2,1,0:T(8,128)(2,1)S(1)} %get-tuple-element.21), channel_id=1, source_target_pairs={{0,28},{4,24},{8,20},{12,16},{16,12},{20,8},{24,4},{28,0},{1,29},{... | collective-permute-start | bytes 786440 | tf_op jit(solution)/shard_map/ppermute | solution.py:156
  7.8 14.9 %collective-permute-start.1 = (bf16[16,16,512]{2,1,0:T(8,128)(2,1)S(1)}, bf16[16,16,512]{2,1,0:T(8,128)(2,1)S(1)}, u32[]{:S(2)}, u32[]{:S(2)}) collective-permute-start(bf16[16,16,512]{2,1,0:T(8,128)(2,1)S(1)} %get-tuple-element.23), channel_id=1, source_target_pairs={{0,24},{4,28},{8,16},{12,20},{16,8},{20,12},{24,0},{28,4},{1,25},{... | collective-permute-start | bytes 786440 | tf_op jit(solution)/shard_map/ppermute | solution.py:156
  9.3 11.2 %collective-permute-start.4 = (bf16[16,16,512]{2,1,0:T(8,128)(2,1)S(1)}, bf16[16,16,512]{2,1,0:T(8,128)(2,1)S(1)}, u32[]{:S(2)}, u32[]{:S(2)}) collective-permute-start(bf16[16,16,512]{2,1,0:T(8,128)(2,1)S(1)} %get-tuple-element.39), channel_id=1, source_target_pairs={{0,4},{4,0},{8,12},{12,8},{16,20},{20,16},{24,28},{28,24},{1,5},{5... | collective-permute-start | bytes 786440 | tf_op jit(solution)/shard_map/ppermute | solution.py:156
  9.8 34.0 %collective-permute-start.3 = (bf16[16,16,512]{2,1,0:T(8,128)(2,1)S(1)}, bf16[16,16,512]{2,1,0:T(8,128)(2,1)S(1)}, u32[]{:S(2)}, u32[]{:S(2)}) collective-permute-start(bf16[16,16,512]{2,1,0:T(8,128)(2,1)S(1)} %get-tuple-element.40), channel_id=1, source_target_pairs={{0,8},{4,12},{8,0},{12,4},{16,24},{20,28},{24,16},{28,20},{1,9},{5... | collective-permute-start | bytes 786440 | tf_op jit(solution)/shard_map/ppermute | solution.py:156
  9.8 34.0 %collective-permute-start.2 = (bf16[16,16,512]{2,1,0:T(8,128)(2,1)S(1)}, bf16[16,16,512]{2,1,0:T(8,128)(2,1)S(1)}, u32[]{:S(2)}, u32[]{:S(2)}) collective-permute-start(bf16[16,16,512]{2,1,0:T(8,128)(2,1)S(1)} %get-tuple-element.41), channel_id=1, source_target_pairs={{0,12},{4,8},{8,4},{12,0},{16,28},{20,24},{24,20},{28,16},{1,13},{... | collective-permute-start | bytes 786440 | tf_op jit(solution)/shard_map/ppermute | solution.py:156
  18.6 4.1 %copy-start = (bf16[5,16,512]{2,1,0:T(8,128)(2,1)S(1)}, bf16[5,16,512]{2,1,0:T(8,128)(2,1)}, u32[]{:S(2)}) copy-start(bf16[5,16,512]{2,1,0:T(8,128)(2,1)} %param.6) | copy-start | bytes 245764
  20.5 23.2 %collective-permute-start.5 = (bf16[16,16,256]{2,1,0:T(8,128)(2,1)S(1)}, bf16[16,16,256]{2,1,0:T(8,128)(2,1)S(1)}, u32[]{:S(2)}, u32[]{:S(2)}) collective-permute-start(bf16[16,16,256]{2,1,0:T(8,128)(2,1)S(1)} %get-tuple-element.26), channel_id=1, source_target_pairs={{0,20},{4,16},{8,28},{12,24},{16,4},{20,0},{24,12},{28,8},{1,21},{... | collective-permute-start | bytes 393224 | tf_op jit(solution)/shard_map/ppermute | solution.py:156
  22.7 23.8 %collective-permute-start.6 = (bf16[16,16,256]{2,1,0:T(8,128)(2,1)S(1)}, bf16[16,16,256]{2,1,0:T(8,128)(2,1)S(1)}, u32[]{:S(2)}, u32[]{:S(2)}) collective-permute-start(bf16[16,16,256]{2,1,0:T(8,128)(2,1)S(1)} %get-tuple-element.28), channel_id=1, source_target_pairs={{0,16},{4,20},{8,24},{12,28},{16,0},{20,4},{24,8},{28,12},{1,17},{... | collective-permute-start | bytes 393224 | tf_op jit(solution)/shard_map/ppermute | solution.py:156
  33.1 17.7 %collective-permute-start.7 = (bf16[16,16,256]{2,1,0:T(8,128)(2,1)S(1)}, bf16[16,16,256]{2,1,0:T(8,128)(2,1)S(1)}, u32[]{:S(2)}, u32[]{:S(2)}) collective-permute-start(bf16[16,16,256]{2,1,0:T(8,128)(2,1)S(1)} %get-tuple-element.31), channel_id=1, source_target_pairs={{0,20},{4,16},{8,28},{12,24},{16,4},{20,0},{24,12},{28,8},{1,21},{... | collective-permute-start | bytes 393224 | tf_op jit(solution)/shard_map/ppermute | solution.py:156
  43.7 8.9 %collective-permute-start.8 = (bf16[16,16,256]{2,1,0:T(8,128)(2,1)S(1)}, bf16[16,16,256]{2,1,0:T(8,128)(2,1)S(1)}, u32[]{:S(2)}, u32[]{:S(2)}) collective-permute-start(bf16[16,16,256]{2,1,0:T(8,128)(2,1)S(1)} %get-tuple-element.32), channel_id=1, source_target_pairs={{0,16},{4,20},{8,24},{12,28},{16,0},{20,4},{24,8},{28,12},{1,17},{... | collective-permute-start | bytes 393224 | tf_op jit(solution)/shard_map/ppermute | solution.py:156
  55.3 3.6 %collective-permute-start.9 = (f32[16,128]{1,0:T(8,128)S(1)}, f32[16,128]{1,0:T(8,128)S(1)}, u32[]{:S(2)}, u32[]{:S(2)}) collective-permute-start(f32[16,128]{1,0:T(8,128)S(1)} %get-tuple-element.35), channel_id=1, source_target_pairs={{0,1},{1,0},{2,3},{3,2},{4,5},{5,4},{6,7},{7,6},{8,9},{9,8},{10,11... | collective-permute-start | bytes 24584 | tf_op jit(solution)/shard_map/ppermute | solution.py:200
  55.3 3.7 %collective-permute-start.10 = (f32[16,128]{1,0:T(8,128)S(1)}, f32[16,128]{1,0:T(8,128)S(1)}, u32[]{:S(2)}, u32[]{:S(2)}) collective-permute-start(f32[16,128]{1,0:T(8,128)S(1)} %get-tuple-element.36), channel_id=1, source_target_pairs={{0,2},{1,3},{2,0},{3,1},{4,6},{5,7},{6,4},{7,5},{8,10},{9,11},{10,... | collective-permute-start | bytes 24584 | tf_op jit(solution)/shard_map/ppermute | solution.py:200
  56.9 3.1 %collective-permute-start.11 = (f32[16,128]{1,0:T(8,128)S(1)}, f32[16,128]{1,0:T(8,128)S(1)}, u32[]{:S(2)}, u32[]{:S(2)}) collective-permute-start(f32[16,128]{1,0:T(8,128)S(1)} %get-tuple-element.37), channel_id=1, source_target_pairs={{0,3},{1,2},{2,1},{3,0},{4,7},{5,6},{6,5},{7,4},{8,11},{9,10},{10,... | collective-permute-start | bytes 24584 | tf_op jit(solution)/shard_map/ppermute | solution.py:200

commit v4 on v3

--- a/solution.py
+++ b/solution.py
@@ -118,20 +118,281 @@
     )(ids, inverse, coeffs, dense, prev, *blocks)
 
 
+REACH = 8
+
+
+def filtered_at(now, history, weights):
+    total = weights[0] * now
+    for tap in range(1, len(weights)):
+        total = total + weights[tap] * history[tap - 1]
+    return total.astype(jnp.bfloat16).astype(jnp.float32)
+
+
+def tap_weights(coeff_ref, tile):
+    span = slice(tile * LANES, (tile + 1) * LANES)
+    return [coeff_ref[tap, :, span].astype(jnp.float32) for tap in range(coeff_ref.shape[0])]
+
+
+def frame_rows(frame, rows):
+    return pl.ds(pl.multiple_of(frame * rows, rows), rows)
+
+
+def filter_rows(pixels, filtered, coeff_ref, frames, step):
+    taps, rows, _ = coeff_ref.shape
+    for tile in range(pixels.shape[0]):
+        weights = tap_weights(coeff_ref, tile)
+
+        def block_step(index, history):
+            history = list(history)
+            for offset in range(step):
+                at = frame_rows(index * step + offset, rows)
+                now = pixels[tile, at, :]
+                filtered[tile, at, :] = filtered_at(now, history, weights)
+                history = [now] + history[:-1]
+            return tuple(history)
+
+        zero = jnp.zeros((rows, LANES), jnp.float32)
+        lax.fori_loop(0, frames // step, block_step, (zero,) * (taps - 1))
+
+
+def subtract_mean(filtered, packed, inv_ref, step):
+    tiles, frames, rows, _ = packed.shape
+
+    def block_step(index, running):
+        running = list(running)
+        for offset in range(step):
+            frame = index * step + offset
+            for tile in range(tiles):
+                value = filtered[tile, frame_rows(frame, rows), :]
+                running[tile] = running[tile] + value
+                packed[tile, frame] = (value - running[tile] * inv_ref[frame]).astype(
+                    jnp.bfloat16
+                )
+        return tuple(running)
+
+    zero = jnp.zeros((rows, LANES), jnp.float32)
+    lax.fori_loop(0, frames // step, block_step, (zero,) * tiles)
+
+
+def project(filtered, dense_ref, first, frames):
+    rows = dense_ref.shape[0]
+    total = 0.0
+    for row in range(rows):
+        picked = jnp.concatenate(
+            [
+                filtered[tile, pl.ds(first * rows + row, frames, stride=rows), :].astype(
+                    jnp.bfloat16
+                )
+                for tile in range(filtered.shape[0])
+            ],
+            axis=1,
+        )
+        total = total + lax.dot_general(
+            dense_ref[row],
+            picked,
+            (((1,), (1,)), ((), ())),
+            preferred_element_type=jnp.float32,
+        )
+    return total
+
+
+def send_out(packed, out_ref, first, sems):
+    copies = [
+        pltpu.make_async_copy(
+            packed.at[tile], out_ref.at[:, :, pl.ds(first + tile * LANES, LANES)], sems.at[tile]
+        )
+        for tile in range(packed.shape[0])
+    ]
+    for copy in copies:
+        copy.start()
+    return copies
+
+
+def fill(pixels, blocks, places, here, step, rows):
+    for block, (k, lane) in zip(blocks, places):
+        start = pl.multiple_of((here ^ k) * (step * rows), step * rows)
+        for tile in range(pixels.shape[0]):
+            first = lane + tile * LANES
+            pixels[tile, pl.ds(start, step * rows), :] = block[
+                :, first : first + LANES
+            ].astype(jnp.float32)
+
+
+def front_kernel(ids_ref, inv_ref, coeff_ref, dense_ref, *rest, places, step):
+    blocks = rest[: len(places)]
+    out_ref, total_ref, pixels, filtered, packed, sems = rest[len(places) :]
+    frames, rows = inv_ref.shape[0], coeff_ref.shape[1]
+    fill(pixels, blocks, places, ids_ref[0], step, rows)
+    filter_rows(pixels, filtered, coeff_ref, frames, step)
+    subtract_mean(filtered, packed, inv_ref, step)
+    copies = send_out(packed, out_ref, 0, sems)
+    total_ref[...] = project(filtered, dense_ref, 0, frames)
+    for copy in copies:
+        copy.wait()
+
+
+def ready_kernel(ids_ref, coeff_ref, dense_ref, *rest, places, step, frames, late):
+    blocks = rest[: len(places)]
+    pixels, filtered, total_ref = rest[len(places) :]
+    tiles, rows = pixels.shape[0], coeff_ref.shape[1]
+    here = ids_ref[0]
+    first = (here ^ late[-1]) // len(late) * (len(late) * step)
+    span = (len(late) * step + REACH) * rows
+    at = pl.ds(pl.multiple_of(first * rows, step * rows), span)
+    for tile in range(tiles):
+        pixels[tile, at, :] = jnp.zeros((span, LANES), jnp.float32)
+    fill(pixels, blocks, places, here, step, rows)
+    filter_rows(pixels, filtered, coeff_ref, frames, step)
+    for tile in range(tiles):
+        filtered[tile, at, :] = jnp.zeros((span, LANES), jnp.float32)
+    total_ref[...] = project(filtered, dense_ref, 0, frames)
+
+
+def trace_kernel(
+    ids_ref, coeff_ref, dense_ref, front_ref, ready_ref, _px, _ft, *rest, late, owners
+):
+    blocks = rest[: len(late)]
+    pixels, filtered, *part_refs = rest[len(late) : -2]
+    strip, partial = rest[-2:]
+    here, position = ids_ref[0], ids_ref[1]
+    taps, rows, _ = coeff_ref.shape
+    step = blocks[0].shape[0] // rows
+    frames = front_ref.shape[1]
+    first = (here ^ late[-1]) // len(late) * (len(late) * step)
+    length = len(late) * step + REACH
+    fill(pixels, blocks, [(k, 0) for k in late], here, step, rows)
+    for tile in range(pixels.shape[0]):
+        weights = tap_weights(coeff_ref, tile)
+        history = []
+        for tap in range(1, taps):
+            earlier = pixels[tile, frame_rows(jnp.maximum(first - tap, 0), rows), :]
+            history.append(jnp.where(first > 0, earlier, 0.0))
+
+        def block_step(index, history):
+            history = list(history)
+            for offset in range(REACH):
+                at = frame_rows(first + index * REACH + offset, rows)
+                now = pixels[tile, at, :]
+                filtered[tile, at, :] = filtered_at(now, history, weights)
+                history = [now] + history[:-1]
+            return tuple(history)
+
+        lax.fori_loop(0, length // REACH, block_step, tuple(history))
+    strip[...] = jnp.zeros(strip.shape, jnp.float32)
+    strip[:, :length] = project(filtered, dense_ref, first, length)
+    frame_ids = lax.broadcasted_iota(jnp.int32, strip.shape, 1)
+    found = jnp.where(frame_ids < frames - first, strip[...], 0.0)
+    total = front_ref[...] + ready_ref[...] + pltpu.roll(found, first, 1)
+    running, reach = total, 1
+    while reach < frames:
+        shifted = pltpu.roll(running, reach, 1)
+        running = running + jnp.where(frame_ids >= reach, shifted, 0.0)
+        reach *= 2
+    counts = jnp.minimum(frame_ids + 1, BASE_WIN).astype(jnp.float32)
+    partial[...] = (total - running / counts).reshape(partial.shape)
+    for k in range(owners):
+        part_refs[k][...] = partial[position ^ k]
+
+
+def delta_kernel(inv_ref, filtered, _, out_ref, packed, sems, *, first, step):
+    subtract_mean(filtered, packed, inv_ref, step)
+    for copy in send_out(packed, out_ref, first, sems):
+        copy.wait()
+
+
+VMEM = pl.BlockSpec(memory_space=pltpu.VMEM)
+SMEM = pl.BlockSpec(memory_space=pltpu.SMEM)
+ANYWHERE = pl.BlockSpec(memory_space=pl.ANY)
+
+
+def options(mib, work):
+    return dict(
+        compiler_params=pltpu.CompilerParams(vmem_limit_bytes=mib * 1024 * 1024),
+        cost_estimate=pl.CostEstimate(flops=16 * work, bytes_accessed=4 * work, transcendentals=0),
+    )
+
+
+def run_front(ids, inverse, coeffs, dense, blocks, places, slab_width):
+    _, rows, width = coeffs.shape
+    frames, tiles = inverse.shape[0], width // LANES
+    step = blocks[0].shape[0] // rows
+    held = pltpu.VMEM((tiles, frames * rows, LANES), jnp.float32)
+    return pl.pallas_call(
+        functools.partial(front_kernel, places=tuple(places), step=step),
+        out_shape=[
+            jax.ShapeDtypeStruct((frames, rows, slab_width), jnp.bfloat16),
+            jax.ShapeDtypeStruct((dense.shape[1], frames), jnp.float32),
+        ],
+        in_specs=[SMEM, SMEM] + [VMEM] * (2 + len(blocks)),
+        out_specs=[ANYWHERE, VMEM],
+        scratch_shapes=[
+            held,
+            held,
+            pltpu.VMEM((tiles, frames, rows, LANES), jnp.bfloat16),
+            pltpu.SemaphoreType.DMA((tiles,)),
+        ],
+        **options(12, frames * rows * width),
+    )(ids, inverse, coeffs, dense, *blocks)
+
+
+def run_ready(ids, coeffs, dense, blocks, places, frames, late):
+    _, rows, width = coeffs.shape
+    step = blocks[0].shape[0] // rows
+    held = jax.ShapeDtypeStruct((width // LANES, (frames + REACH) * rows, LANES), jnp.float32)
+    return pl.pallas_call(
+        functools.partial(
+            ready_kernel, places=tuple(places), step=step, frames=frames, late=tuple(late)
+        ),
+        out_shape=[held, held, jax.ShapeDtypeStruct((dense.shape[1], frames), jnp.float32)],
+        in_specs=[SMEM] + [VMEM] * (2 + len(blocks)),
+        out_specs=[VMEM] * 3,
+        **options(4, frames * rows * width),
+    )(ids, coeffs, dense, *blocks)
+
+
+def run_traces(ids, coeffs, dense, front, ready, pixels, filtered, late, owners):
+    _, rows, width = coeffs.shape
+    rois, frames = front.shape
+    held = jax.ShapeDtypeStruct(pixels.shape, jnp.float32)
+    part = jax.ShapeDtypeStruct((rois // owners, frames), jnp.float32)
+    return pl.pallas_call(
+        functools.partial(trace_kernel, late=tuple(late), owners=owners),
+        out_shape=[held, held] + [part] * owners,
+        in_specs=[SMEM] + [VMEM] * (6 + len(late)),
+        out_specs=[VMEM] * (2 + owners),
+        input_output_aliases={5: 0, 6: 1},
+        scratch_shapes=[
+            pltpu.VMEM((rois, frames), jnp.float32),
+            pltpu.VMEM((owners, rois // owners, frames), jnp.float32),
+        ],
+        **options(4, frames * rows * width),
+    )(ids, coeffs, dense, front, ready, pixels, filtered, *late.values())
+
+
+def run_delta(inverse, filtered, out, first, rows, step):
+    tiles, frames = filtered.shape[0], inverse.shape[0]
+    return pl.pallas_call(
+        functools.partial(delta_kernel, first=first, step=step),
+        out_shape=jax.ShapeDtypeStruct(out.shape, jnp.bfloat16),
+        in_specs=[SMEM, VMEM, ANYWHERE],
+        out_specs=ANYWHERE,
+        input_output_aliases={2: 0},
+        scratch_shapes=[
+            pltpu.VMEM((tiles, frames, rows, LANES), jnp.bfloat16),
+            pltpu.SemaphoreType.DMA((tiles,)),
+        ],
+        **options(4, frames * rows * tiles * LANES),
+    )(inverse, filtered, out)
+
+
 def swaps(count, k):
     return [(i, i ^ k) for i in range(count)]
 
 
-def local(movie, coeffs, footprint_w, roi_blocks, roi_len):
-    devices = lax.axis_size("tm")
-    owners = lax.axis_size("roi")
-    here = lax.axis_index("tm")
-    position = lax.axis_index("roi")
+def plain_plan(movie, coeffs, dense_of, ids, inverse, here, position, devices, owners):
     step, _, slab_width = movie.shape
     rows = coeffs.shape[1]
     frames = devices * step
-    slot_count = roi_blocks.shape[1]
-
     middle = slab_width // LANES // 2 * LANES
     cuts = [0, middle, slab_width]
     near = list(range(devices // 2 - 1, 0, -1))
@@ -165,20 +426,7 @@
             ]
         )
 
-    gathered = lax.all_gather(footprint_w, "roi", axis=0, tiled=True)
-    live = jnp.arange(slot_count, dtype=jnp.int32)[None, :] < roi_len[:, None]
-    live = live & (roi_blocks // rows == position)
-    hit = live[:, :, None] & (
-        (roi_blocks % rows)[:, :, None] == jnp.arange(rows, dtype=jnp.int32)
-    )
-    dense = sum(
-        jnp.where(hit[:, m, :].T[:, :, None], gathered[None, :, m, :], 0)
-        for m in range(slot_count)
-    ).astype(jnp.bfloat16)
-
-    ids = jnp.stack([here, position]).astype(jnp.int32)
-    counts = jnp.minimum(jnp.arange(frames, dtype=jnp.int32) + 1, BASE_WIN)
-    inverse = 1.0 / counts.astype(jnp.float32)
+    dense = dense_of()
     prev = jnp.zeros((dense.shape[1], frames), jnp.float32)
     deltas = []
     for low, high, received in zip(cuts[:-1], cuts[1:], chunks):
@@ -201,6 +449,87 @@
     return jnp.concatenate(deltas, axis=2), traces
 
 
+def local(movie, coeffs, footprint_w, roi_blocks, roi_len):
+    devices = lax.axis_size("tm")
+    owners = lax.axis_size("roi")
+    here = lax.axis_index("tm")
+    position = lax.axis_index("roi")
+    step, _, slab_width = movie.shape
+    rows = coeffs.shape[1]
+    frames = devices * step
+    slot_count = roi_blocks.shape[1]
+
+    live = jnp.arange(slot_count, dtype=jnp.int32)[None, :] < roi_len[:, None]
+    live = live & (roi_blocks // rows == position)
+    hit = live[:, :, None] & (
+        (roi_blocks % rows)[:, :, None] == jnp.arange(rows, dtype=jnp.int32)
+    )
+
+    def dense_of():
+        gathered = lax.all_gather(footprint_w, "roi", axis=0, tiled=True)
+        return sum(
+            jnp.where(hit[:, m, :].T[:, :, None], gathered[None, :, m, :], 0)
+            for m in range(slot_count)
+        ).astype(jnp.bfloat16)
+
+    counts = jnp.minimum(jnp.arange(frames, dtype=jnp.int32) + 1, BASE_WIN)
+    inverse = 1.0 / counts.astype(jnp.float32)
+    middle = slab_width // LANES // 2 * LANES
+    ids = jnp.stack([here, position]).astype(jnp.int32)
+    if frames > BASE_WIN or devices % 4 or middle == 0:
+        return plain_plan(
+            movie, coeffs, dense_of, ids, inverse, here, position, devices, owners
+        )
+
+    far = list(range(devices - 1, devices // 2 - 1, -1))
+    near = list(range(devices // 2 - 1, 0, -1))
+    early, late = far[: len(far) // 2], far[len(far) // 2 :]
+
+    def rows_of(source, k, low=0, high=slab_width):
+        block = lax.dynamic_slice(
+            source, (0, (here ^ k) * rows, low), (step, rows, high - low)
+        )
+        return block.reshape(step * rows, high - low)
+
+    def send(block, k, *after):
+        if after:
+            block, *_ = lax.optimization_barrier((block, *after))
+        return lax.ppermute(block, "tm", swaps(devices, k))
+
+    opening = [rows_of(movie, k) for k in early]
+    rest, *opening = lax.optimization_barrier((movie, *opening))
+    whole = {k: send(block, k) for block, k in zip(opening, early)}
+    whole |= {k: send(rows_of(rest, k), k) for k in near}
+    ties = [whole[near[-1]]] + [whole[k] for k in early]
+    low = {k: send(rows_of(rest, k, 0, middle), k, tie) for k, tie in zip(late, ties)}
+    ties = ties[len(late) :] + list(low.values())
+    high = {k: send(rows_of(rest, k, middle), k, tie) for k, tie in zip(late, ties)}
+    whole[0] = rows_of(rest, 0)
+    dense = dense_of()
+
+    blocks, places = list(whole.values()), list(whole)
+    delta, front = run_front(
+        ids,
+        inverse,
+        coeffs[:, :, :middle],
+        dense[:, :, :middle],
+        blocks + list(low.values()),
+        [(k, 0) for k in places + late],
+        slab_width,
+    )
+    second, heavy = coeffs[:, :, middle:], dense[:, :, middle:]
+    pixels, filtered, ready = run_ready(
+        ids, second, heavy, blocks, [(k, middle) for k in places], frames, late
+    )
+    _, filtered, *parts = run_traces(
+        ids, second, heavy, front, ready, pixels, filtered, high, owners
+    )
+    traces = parts[0]
+    for k in range(1, owners):
+        traces = traces + lax.ppermute(parts[k], "roi", swaps(owners, k))
+    return run_delta(inverse, filtered, delta, middle, rows, step), traces
+
+
 def solution(mesh):
     placed = (
         P("tm", None, "roi"),

time: 60.8 us -> 59.9 us (0.985)
  Pallas kernels: 5.28 us -> 9.33 us
  waiting for transfers between devices: 18 us -> 14.6 us
  other arithmetic: 2.93 us -> 1.32 us
    pallas_call x2 -> x4, Pallas kernels: 5.28 us -> 9.33 us  [the longest x1 3.39 us: run_front(): pl.pallas_call(functools.partial(front_kernel, places=tuple(places), step...]
    ppermute x9, waiting for transfers between devices: 16.8 us -> 13.8 us  [send(): return lax.ppermute(block, 'tm', swaps(devices, k))]
    concatenate x1 -> x0, other arithmetic: 1.61 us -> none  [local(): return (jnp.concatenate(deltas, axis=2), traces)]
  transfers between devices with their start and end apart: 12 -> 12, of which waited for: 6 -> 5; matrix products, arithmetic and copies ran while one was open for 8% -> 5% of each run, Pallas kernels for 4% -> 13%
where the time goes in v4:
time: 59.9 us; the launch traced here: 59.7 us
  starting transfers between devices  24.3 us (41%)
  waiting for transfers between devices  14.6 us (24%)
  Pallas kernels  9.33 us (16%)
  blocking collectives  5.61 us (9%)
  local copies, waits for them, and re-layouts  3.65 us (6%)
  other arithmetic  1.32 us (2%)
  between operations  0.85 us (1%)
    ppermute x9, starting transfers between devices, send(): return lax.ppermute(block, 'tm', swaps(devices, k))  22.4 us
    ppermute x9, waiting for transfers between devices, send(): return lax.ppermute(block, 'tm', swaps(devices, k))  13.8 us
    all_gather x1, blocking collectives, dense_of(): gathered = lax.all_gather(footprint_w, 'roi', axis=0, tiled=True)  5.61 us
    dynamic_slice x3, local copies, waits for them, and re-layouts, rows_of(): lax.dynamic_slice(source, (0, (here ^ k) * rows, low), (step, rows, high...  3.49 us
    pallas_call x1, Pallas kernels, run_front(): pl.pallas_call(functools.partial(front_kernel, places=tuple(places), step...  3.39 us
    pallas_call x1, Pallas kernels, run_ready(): pl.pallas_call(functools.partial(ready_kernel, places=tuple(places), step...  2.28 us
    ppermute x3, starting transfers between devices, local(): traces = traces + lax.ppermute(parts[k], 'roi', swaps(owners, k))  1.93 us
    pallas_call x1, Pallas kernels, run_delta(): pl.pallas_call(functools.partial(delta_kernel, first=first, step=step), o...  1.84 us
  transfers between devices with their start and end apart: 12, of which 5 were waited for; matrix products, arithmetic and copies ran while one was open for 5% of the time, Pallas kernels for 13%

profile of v4, /device:TPU:0, one launch (start us, length us, event | category | flops | bytes accessed | tf_op | source)
XLA Modules:
  0.0 59.7 jit_solution(9135360719365420247)
XLA Ops:
  0.7 1.1 %constant_dynamic-slice_fusion.8 = (bf16[16,16,512]{2,1,0:T(8,128)(2,1)S(1)}, bf16[16,16,512]{2,1,0:T(8,128)(2,1)S(1)}) fusion(bf16[16,128,512]{2,1,0:T(8,128)(2,1)} %param.5, s32[]{:T(128)S(6)} %select_n.54, s32[]{:T(128)S(6)} %select_n.53), kind=kLoop, calls=%fused_computation.23 | loop fusion | bytes 1048584 | tf_op jit(solution)/shard_map/dynamic_slice | solution.py:489
  1.8 6.1 %collective-permute-start = (bf16[256,512]{1,0:T(8,128)(2,1)S(1)}, bf16[256,512]{1,0:T(8,128)(2,1)S(1)}, u32[]{:S(2)}, u32[]{:S(2)}) collective-permute-start(bf16[256,512]{1,0:T(8,128)(2,1)S(1)} %bitcast.32), channel_id=1, source_target_pairs={{0,28},{4,24},{8,20},{12,16},{16,12},{20,8},{24,4},{28,0},{1,29},{... | collective-permute-start | bytes 786440 | tf_op jit(solution)/shard_map/ppermute | solution.py:497
  7.8 0.2 collective-permute-start.1
  8.0 1.3 %constant_dynamic-slice_fusion.4 = (bf16[16,16,512]{2,1,0:T(8,128)(2,1)S(1)}, bf16[16,16,512]{2,1,0:T(8,128)(2,1)S(1)}, bf16[16,16,512]{2,1,0:T(8,128)(2,1)S(1)}, bf16[16,16,512]{2,1,0:T(8,128)(2,1)S(1)}) fusion(bf16[16,128,512]{2,1,0:T(8,128)(2,1)} %param.5, s32[]{:T(128)S(6)} %select_n.58, s32[]{:T(128)S(6)} %select_n.57, s32[]{:T(128)S(6)} %select_n.56, ...), kind=kLoop, calls=%fused_computation.19 | loop fusion | bytes 2097168 | tf_op jit(solution)/shard_map/dynamic_slice | solution.py:489
  9.3 0.5 collective-permute-start.4
  9.8 0.0 collective-permute-start.3
  9.8 3.1 %collective-permute-start.2 = (bf16[256,512]{1,0:T(8,128)(2,1)S(1)}, bf16[256,512]{1,0:T(8,128)(2,1)S(1)}, u32[]{:S(2)}, u32[]{:S(2)}) collective-permute-start(bf16[256,512]{1,0:T(8,128)(2,1)S(1)} %bitcast.34), channel_id=1, source_target_pairs={{0,12},{4,8},{8,4},{12,0},{16,28},{20,24},{24,20},{28,16},{1,13},{... | collective-permute-start | bytes 786440 | tf_op jit(solution)/shard_map/ppermute | solution.py:497
  13.0 5.6 %all_gather.3 = bf16[64,3,512]{2,0,1:T(8,128)(2,1)S(1)} all-gather(bf16[16,3,512]{2,0,1:T(8,128)(2,1)S(1)} %copy-done.1), channel_id=1, replica_groups=mesh['tm'=8,'roi'=4] {'roi'}, dimensions={0}, use_global_device_ids=true | all-gather | bytes 245760 | tf_op jit(solution)/shard_map/all_gather | solution.py:469
  18.6 0.0 copy-start
  18.6 0.6 select_add_fusion
  19.2 0.1 fusion.4
  19.3 1.2 %constant_dynamic-slice_fusion = (bf16[16,16,256]{2,1,0:T(8,128)(2,1)S(1)}, bf16[16,16,256]{2,1,0:T(8,128)(2,1)S(1)}, bf16[16,16,256]{2,1,0:T(8,128)(2,1)S(1)}, bf16[16,16,256]{2,1,0:T(8,128)(2,1)S(1)}) fusion(bf16[16,128,512]{2,1,0:T(8,128)(2,1)} %param.5, s32[]{:T(128)S(6)} %select_n.60, s32[]{:T(128)S(6)} %select_n.59), kind=kLoop, calls=%fused_computation.15 | loop fusion | bytes 1048584 | tf_op jit(solution)/shard_map/dynamic_slice | solution.py:489
  20.5 0.0 collective-permute-done.4.rest_4_
  20.5 2.2 %collective-permute-start.5 = (bf16[256,256]{1,0:T(8,128)(2,1)S(1)}, bf16[256,256]{1,0:T(8,128)(2,1)S(1)}, u32[]{:S(2)}, u32[]{:S(2)}) collective-permute-start(bf16[256,256]{1,0:T(8,128)(2,1)S(1)} %bitcast.40), channel_id=1, source_target_pairs={{0,20},{4,16},{8,28},{12,24},{16,4},{20,0},{24,12},{28,8},{1,21},{... | collective-permute-start | bytes 393224 | tf_op jit(solution)/shard_map/ppermute | solution.py:497
  22.7 0.0 collective-permute-done.1.rest_1_
  22.7 0.0 collective-permute-done.rest_0_
  22.7 10.3 %collective-permute-start.6 = (bf16[256,256]{1,0:T(8,128)(2,1)S(1)}, bf16[256,256]{1,0:T(8,128)(2,1)S(1)}, u32[]{:S(2)}, u32[]{:S(2)}) collective-permute-start(bf16[256,256]{1,0:T(8,128)(2,1)S(1)} %bitcast.39), channel_id=1, source_target_pairs={{0,16},{4,20},{8,24},{12,28},{16,0},{20,4},{24,8},{28,12},{1,17},{... | collective-permute-start | bytes 393224 | tf_op jit(solution)/shard_map/ppermute | solution.py:497
  33.1 0.0 collective-permute-start.7
  33.1 10.7 %collective-permute-done.5.rest_6_ = bf16[256,256]{1,0:T(8,128)(2,1)S(1)} collective-permute-done((bf16[256,256]{1,0:T(8,128)(2,1)S(1)}, bf16[256,256]{1,0:T(8,128)(2,1)S(1)}, u32[]{:S(2)}, u32[]{:S(2)}) %collective-permute-start.5) | collective-permute-done | bytes 131104 | tf_op jit(solution)/shard_map/ppermute | solution.py:497
  43.8 0.1 pad_add_fusion.ids_ref
  43.8 2.3 %shard_map.69 = (f32[2,2176,128]{2,1,0:T(8,128)S(1)}, f32[2,2176,128]{2,1,0:T(8,128)S(1)}, f32[64,128]{1,0:T(8,128)S(1)}) custom-call(s32[2]{0:T(128)S(1)} %pad_add_fusion.ids_ref, bf16[5,16,256]{2,1,0:T(8,128)(2,1)S(1)} %get-tuple-element.52.coeff_ref, bf16[16,64,256]{2,1,0:T(8,128)(2,1)S(1)} %get-tuple-element.47.dense_ref, ...), custom_call_target="tpu_custom_call" | custom-call | flops 8388608 | bytes 2097152 | tf_op jit(solution)/shard_map/pallas_call | solution.py:342
  46.1 0.4 collective-permute-done.6.rest_7_
  46.5 3.4 %shard_map.68 = (bf16[128,16,512]{2,1,0:T(8,128)(2,1)}, f32[64,128]{1,0:T(8,128)S(1)}) custom-call(s32[2]{0:T(128)S(1)} %pad_add_fusion.ids_ref, f32[128]{0:T(128)S(1)} %convert_divide_fusion.inv_ref, bf16[5,16,256]{2,1,0:T(8,128)(2,1)S(1)} %get-tuple-element.51.coeff_ref, bf16[16,64,256]{2,1,0:T(8,128)(2,1)S(1)} %get-tuple-element.46.dense_ref, ...), custom_call_target="tpu_custom_call" | custom-call | flops 8388608 | bytes 2097152 | tf_op jit(solution)/shard_map/pallas_call | solution.py:320
  49.9 0.9 %collective-permute-done.7.rest_0_ = bf16[256,256]{1,0:T(8,128)(2,1)S(1)} collective-permute-done((bf16[256,256]{1,0:T(8,128)(2,1)S(1)}, bf16[256,256]{1,0:T(8,128)(2,1)S(1)}, u32[]{:S(2)}, u32[]{:S(2)}) %collective-permute-start.7) | collective-permute-done | bytes 131104 | tf_op jit(solution)/shard_map/ppermute | solution.py:497
  50.8 1.8 %collective-permute-done.8.rest_1_ = bf16[256,256]{1,0:T(8,128)(2,1)S(1)} collective-permute-done((bf16[256,256]{1,0:T(8,128)(2,1)S(1)}, bf16[256,256]{1,0:T(8,128)(2,1)S(1)}, u32[]{:S(2)}, u32[]{:S(2)}) %collective-permute-start.8) | collective-permute-done | bytes 131104 | tf_op jit(solution)/shard_map/ppermute | solution.py:497
  52.6 1.8 %shard_map.70 = (f32[2,2176,128]{2,1,0:T(8,128)S(1)}, f32[2,2176,128]{2,1,0:T(8,128)S(1)}, f32[16,128]{1,0:T(8,128)S(1)}, f32[16,128]{1,0:T(8,128)S(1)}, f32[16,128]{1,0:T(8,128)S(1)}, /*index=5*/f32[16,128]{1,0:T(8,128)S(1)}) custom-call(s32[2]{0:T(128)S(1)} %pad_add_fusion.ids_ref, ...), custom_call_target="tpu_custom_call", output_to_operand_aliasing={{0}: (5, {}), {1}: (6, {})} | custom-call | flops 8388608 | bytes 2097152 | tf_op jit(solution)/shard_map/pallas_call | solution.py:358
  54.4 0.1 collective-permute-start.9
  54.5 1.5 %collective-permute-start.10 = (f32[16,128]{1,0:T(8,128)S(1)}, f32[16,128]{1,0:T(8,128)S(1)}, u32[]{:S(2)}, u32[]{:S(2)}) collective-permute-start(f32[16,128]{1,0:T(8,128)S(1)} %get-tuple-element.34), channel_id=1, source_target_pairs={{0,2},{1,3},{2,0},{3,1},{4,6},{5,7},{6,4},{7,5},{8,10},{9,11},{10,... | collective-permute-start | bytes 24584 | tf_op jit(solution)/shard_map/ppermute | solution.py:529
  56.0 0.3 collective-permute-start.11
  56.4 1.8 %shard_map.71 = bf16[128,16,512]{2,1,0:T(8,128)(2,1)} custom-call(f32[128]{0:T(128)S(1)} %convert_divide_fusion.inv_ref, f32[2,2176,128]{2,1,0:T(8,128)S(1)} %get-tuple-element.30.filtered, bf16[128,16,512]{2,1,0:T(8,128)(2,1)} %get-tuple-element.31._), custom_call_target="tpu_custom_call", output_to_operand_aliasing={{}: (2, {})} | custom-call | flops 8388608 | bytes 2097152 | tf_op jit(solution)/shard_map/pallas_call | solution.py:374
  58.2 0.9 %collective-permute-done.11 = f32[16,128]{1,0:T(8,128)S(1)} collective-permute-done((f32[16,128]{1,0:T(8,128)S(1)}, f32[16,128]{1,0:T(8,128)S(1)}, u32[]{:S(2)}, u32[]{:S(2)}) %collective-permute-start.11) | collective-permute-done | bytes 8224 | tf_op jit(solution)/shard_map/ppermute | solution.py:529
  59.1 0.6 %add_add_fusion = f32[16,128]{1,0:T(8,128)} fusion(f32[16,128]{1,0:T(8,128)S(1)} %collective-permute-done.11, f32[16,128]{1,0:T(8,128)S(1)} %collective-permute-done.10, f32[16,128]{1,0:T(8,128)S(1)} %get-tuple-element.32, f32[16,128]{1,0:T(8,128)S(1)} %collective-permute-done.9), kind=kLoop, calls=%fused_computation.6 | loop fusion | flops 6144 | bytes 40960 | tf_op jit(solution)/shard_map/add | solution.py:529
  (19 shorter events, 0.1 us)
Async XLA Ops:
  0.6 12.2 %copy-start.2 = (s32[64,3]{0,1:T(4,128)S(1)}, s32[64,3]{0,1:T(4,128)}, u32[]{:S(2)}) copy-start(s32[64,3]{0,1:T(4,128)} %param.8) | copy-start | bytes 2308
  0.6 12.2 %copy-start.3 = (s32[64]{0:T(128)S(1)}, s32[64]{0:T(128)}, u32[]{:S(2)}) copy-start(s32[64]{0:T(128)} %param.9) | copy-start | bytes 772
  0.7 12.3 %copy-start.1 = (bf16[16,3,512]{2,0,1:T(8,128)(2,1)S(1)}, bf16[16,3,512]{2,0,1:T(8,128)(2,1)}, u32[]{:S(2)}) copy-start(bf16[16,3,512]{2,0,1:T(8,128)(2,1)} %param.7) | copy-start | bytes 147460
  1.8 21.0 %collective-permute-start = (bf16[256,512]{1,0:T(8,128)(2,1)S(1)}, bf16[256,512]{1,0:T(8,128)(2,1)S(1)}, u32[]{:S(2)}, u32[]{:S(2)}) collective-permute-start(bf16[256,512]{1,0:T(8,128)(2,1)S(1)} %bitcast.32), channel_id=1, source_target_pairs={{0,28},{4,24},{8,20},{12,16},{16,12},{20,8},{24,4},{28,0},{1,29},{... | collective-permute-start | bytes 786440 | tf_op jit(solution)/shard_map/ppermute | solution.py:497
  7.8 14.9 %collective-permute-start.1 = (bf16[256,512]{1,0:T(8,128)(2,1)S(1)}, bf16[256,512]{1,0:T(8,128)(2,1)S(1)}, u32[]{:S(2)}, u32[]{:S(2)}) collective-permute-start(bf16[256,512]{1,0:T(8,128)(2,1)S(1)} %bitcast.33), channel_id=1, source_target_pairs={{0,24},{4,28},{8,16},{12,20},{16,8},{20,12},{24,0},{28,4},{1,25},{... | collective-permute-start | bytes 786440 | tf_op jit(solution)/shard_map/ppermute | solution.py:497
  9.3 11.2 %collective-permute-start.4 = (bf16[256,512]{1,0:T(8,128)(2,1)S(1)}, bf16[256,512]{1,0:T(8,128)(2,1)S(1)}, u32[]{:S(2)}, u32[]{:S(2)}) collective-permute-start(bf16[256,512]{1,0:T(8,128)(2,1)S(1)} %bitcast.36), channel_id=1, source_target_pairs={{0,4},{4,0},{8,12},{12,8},{16,20},{20,16},{24,28},{28,24},{1,5},{5... | collective-permute-start | bytes 786440 | tf_op jit(solution)/shard_map/ppermute | solution.py:497
  9.8 34.0 %collective-permute-start.3 = (bf16[256,512]{1,0:T(8,128)(2,1)S(1)}, bf16[256,512]{1,0:T(8,128)(2,1)S(1)}, u32[]{:S(2)}, u32[]{:S(2)}) collective-permute-start(bf16[256,512]{1,0:T(8,128)(2,1)S(1)} %bitcast.35), channel_id=1, source_target_pairs={{0,8},{4,12},{8,0},{12,4},{16,24},{20,28},{24,16},{28,20},{1,9},{5... | collective-permute-start | bytes 786440 | tf_op jit(solution)/shard_map/ppermute | solution.py:497
  9.8 34.0 %collective-permute-start.2 = (bf16[256,512]{1,0:T(8,128)(2,1)S(1)}, bf16[256,512]{1,0:T(8,128)(2,1)S(1)}, u32[]{:S(2)}, u32[]{:S(2)}) collective-permute-start(bf16[256,512]{1,0:T(8,128)(2,1)S(1)} %bitcast.34), channel_id=1, source_target_pairs={{0,12},{4,8},{8,4},{12,0},{16,28},{20,24},{24,20},{28,16},{1,13},{... | collective-permute-start | bytes 786440 | tf_op jit(solution)/shard_map/ppermute | solution.py:497
  18.6 4.1 %copy-start = (bf16[5,16,512]{2,1,0:T(8,128)(2,1)S(1)}, bf16[5,16,512]{2,1,0:T(8,128)(2,1)}, u32[]{:S(2)}) copy-start(bf16[5,16,512]{2,1,0:T(8,128)(2,1)} %param.6) | copy-start | bytes 245764
  20.5 23.2 %collective-permute-start.5 = (bf16[256,256]{1,0:T(8,128)(2,1)S(1)}, bf16[256,256]{1,0:T(8,128)(2,1)S(1)}, u32[]{:S(2)}, u32[]{:S(2)}) collective-permute-start(bf16[256,256]{1,0:T(8,128)(2,1)S(1)} %bitcast.40), channel_id=1, source_target_pairs={{0,20},{4,16},{8,28},{12,24},{16,4},{20,0},{24,12},{28,8},{1,21},{... | collective-permute-start | bytes 393224 | tf_op jit(solution)/shard_map/ppermute | solution.py:497
  22.7 23.8 %collective-permute-start.6 = (bf16[256,256]{1,0:T(8,128)(2,1)S(1)}, bf16[256,256]{1,0:T(8,128)(2,1)S(1)}, u32[]{:S(2)}, u32[]{:S(2)}) collective-permute-start(bf16[256,256]{1,0:T(8,128)(2,1)S(1)} %bitcast.39), channel_id=1, source_target_pairs={{0,16},{4,20},{8,24},{12,28},{16,0},{20,4},{24,8},{28,12},{1,17},{... | collective-permute-start | bytes 393224 | tf_op jit(solution)/shard_map/ppermute | solution.py:497
  33.1 17.7 %collective-permute-start.7 = (bf16[256,256]{1,0:T(8,128)(2,1)S(1)}, bf16[256,256]{1,0:T(8,128)(2,1)S(1)}, u32[]{:S(2)}, u32[]{:S(2)}) collective-permute-start(bf16[256,256]{1,0:T(8,128)(2,1)S(1)} %bitcast.38), channel_id=1, source_target_pairs={{0,20},{4,16},{8,28},{12,24},{16,4},{20,0},{24,12},{28,8},{1,21},{... | collective-permute-start | bytes 393224 | tf_op jit(solution)/shard_map/ppermute | solution.py:497
  43.7 8.9 %collective-permute-start.8 = (bf16[256,256]{1,0:T(8,128)(2,1)S(1)}, bf16[256,256]{1,0:T(8,128)(2,1)S(1)}, u32[]{:S(2)}, u32[]{:S(2)}) collective-permute-start(bf16[256,256]{1,0:T(8,128)(2,1)S(1)} %bitcast.37), channel_id=1, source_target_pairs={{0,16},{4,20},{8,24},{12,28},{16,0},{20,4},{24,8},{28,12},{1,17},{... | collective-permute-start | bytes 393224 | tf_op jit(solution)/shard_map/ppermute | solution.py:497
  54.4 3.8 %collective-permute-start.9 = (f32[16,128]{1,0:T(8,128)S(1)}, f32[16,128]{1,0:T(8,128)S(1)}, u32[]{:S(2)}, u32[]{:S(2)}) collective-permute-start(f32[16,128]{1,0:T(8,128)S(1)} %get-tuple-element.33), channel_id=1, source_target_pairs={{0,1},{1,0},{2,3},{3,2},{4,5},{5,4},{6,7},{7,6},{8,9},{9,8},{10,11... | collective-permute-start | bytes 24584 | tf_op jit(solution)/shard_map/ppermute | solution.py:529
  54.5 3.7 %collective-permute-start.10 = (f32[16,128]{1,0:T(8,128)S(1)}, f32[16,128]{1,0:T(8,128)S(1)}, u32[]{:S(2)}, u32[]{:S(2)}) collective-permute-start(f32[16,128]{1,0:T(8,128)S(1)} %get-tuple-element.34), channel_id=1, source_target_pairs={{0,2},{1,3},{2,0},{3,1},{4,6},{5,7},{6,4},{7,5},{8,10},{9,11},{10,... | collective-permute-start | bytes 24584 | tf_op jit(solution)/shard_map/ppermute | solution.py:529
  56.0 3.1 %collective-permute-start.11 = (f32[16,128]{1,0:T(8,128)S(1)}, f32[16,128]{1,0:T(8,128)S(1)}, u32[]{:S(2)}, u32[]{:S(2)}) collective-permute-start(f32[16,128]{1,0:T(8,128)S(1)} %get-tuple-element.35), channel_id=1, source_target_pairs={{0,3},{1,2},{2,1},{3,0},{4,7},{5,6},{6,5},{7,4},{8,11},{9,10},{10,... | collective-permute-start | bytes 24584 | tf_op jit(solution)/shard_map/ppermute | solution.py:529

commit v5 on v4

--- a/solution.py
+++ b/solution.py
@@ -196,18 +196,6 @@
     return total
 
 
-def send_out(packed, out_ref, first, sems):
-    copies = [
-        pltpu.make_async_copy(
-            packed.at[tile], out_ref.at[:, :, pl.ds(first + tile * LANES, LANES)], sems.at[tile]
-        )
-        for tile in range(packed.shape[0])
-    ]
-    for copy in copies:
-        copy.start()
-    return copies
-
-
 def fill(pixels, blocks, places, here, step, rows):
     for block, (k, lane) in zip(blocks, places):
         start = pl.multiple_of((here ^ k) * (step * rows), step * rows)
@@ -218,50 +206,56 @@
             ].astype(jnp.float32)
 
 
-def front_kernel(ids_ref, inv_ref, coeff_ref, dense_ref, *rest, places, step):
-    blocks = rest[: len(places)]
-    out_ref, total_ref, pixels, filtered, packed, sems = rest[len(places) :]
-    frames, rows = inv_ref.shape[0], coeff_ref.shape[1]
-    fill(pixels, blocks, places, ids_ref[0], step, rows)
-    filter_rows(pixels, filtered, coeff_ref, frames, step)
-    subtract_mean(filtered, packed, inv_ref, step)
-    copies = send_out(packed, out_ref, 0, sems)
-    total_ref[...] = project(filtered, dense_ref, 0, frames)
-    for copy in copies:
-        copy.wait()
-
-
-def ready_kernel(ids_ref, coeff_ref, dense_ref, *rest, places, step, frames, late):
+def late_frames(here, late, step):
+    return (here ^ late[-1]) // len(late) * (len(late) * step), len(late) * step + REACH
+
+
+def minus_mean(total):
+    frames = total.shape[1]
+    earlier = lax.broadcasted_iota(jnp.int32, (frames, frames), 0)
+    later = lax.broadcasted_iota(jnp.int32, (frames, frames), 1)
+    upto = jnp.where(earlier <= later, 1.0, 0.0).astype(jnp.bfloat16)
+    high = total.astype(jnp.bfloat16)
+    rest = total - high.astype(jnp.float32)
+    middle = rest.astype(jnp.bfloat16)
+    low = (rest - middle.astype(jnp.float32)).astype(jnp.bfloat16)
+    running = sum(
+        jnp.dot(term, upto, preferred_element_type=jnp.float32) for term in (low, middle, high)
+    )
+    frame_ids = lax.broadcasted_iota(jnp.int32, total.shape, 1)
+    return total - running / jnp.minimum(frame_ids + 1, BASE_WIN).astype(jnp.float32)
+
+
+def early_kernel(ids_ref, coeff_ref, dense_ref, *rest, places, step, frames, late):
     blocks = rest[: len(places)]
     pixels, filtered, total_ref = rest[len(places) :]
-    tiles, rows = pixels.shape[0], coeff_ref.shape[1]
+    rows = coeff_ref.shape[1]
     here = ids_ref[0]
-    first = (here ^ late[-1]) // len(late) * (len(late) * step)
-    span = (len(late) * step + REACH) * rows
-    at = pl.ds(pl.multiple_of(first * rows, step * rows), span)
+    first, length = late_frames(here, late, step)
+    at = pl.ds(pl.multiple_of(first * rows, step * rows), length * rows)
+    zeros = jnp.zeros((length * rows, LANES), jnp.float32)
+    for tile in range(pixels.shape[0]):
+        pixels[tile, at, :] = zeros
+    fill(pixels, blocks, [(k, 0) for k in places], here, step, rows)
+    filter_rows(pixels, filtered, coeff_ref, frames, step)
+    for tile in range(pixels.shape[0]):
+        filtered[tile, at, :] = zeros
+    total_ref[...] = project(filtered, dense_ref, 0, frames)
+
+
+def late_kernel(ids_ref, coeff_ref, dense_ref, total_ref, _px, _ft, *rest, late, tile, last):
+    blocks = rest[: len(late)]
+    all_pixels, all_filtered, *outs, strip, partial = rest[len(late) :]
+    here, position = ids_ref[0], ids_ref[1]
+    taps, rows, width = coeff_ref.shape
+    step = blocks[0].shape[0] // rows
+    tiles = width // LANES
+    frames = total_ref.shape[1]
+    pixels = all_pixels.at[tile : tile + tiles]
+    filtered = all_filtered.at[tile : tile + tiles]
+    first, length = late_frames(here, late, step)
+    fill(pixels, blocks, [(k, 0) for k in late], here, step, rows)
     for tile in range(tiles):
-        pixels[tile, at, :] = jnp.zeros((span, LANES), jnp.float32)
-    fill(pixels, blocks, places, here, step, rows)
-    filter_rows(pixels, filtered, coeff_ref, frames, step)
-    for tile in range(tiles):
-        filtered[tile, at, :] = jnp.zeros((span, LANES), jnp.float32)
-    total_ref[...] = project(filtered, dense_ref, 0, frames)
-
-
-def trace_kernel(
-    ids_ref, coeff_ref, dense_ref, front_ref, ready_ref, _px, _ft, *rest, late, owners
-):
-    blocks = rest[: len(late)]
-    pixels, filtered, *part_refs = rest[len(late) : -2]
-    strip, partial = rest[-2:]
-    here, position = ids_ref[0], ids_ref[1]
-    taps, rows, _ = coeff_ref.shape
-    step = blocks[0].shape[0] // rows
-    frames = front_ref.shape[1]
-    first = (here ^ late[-1]) // len(late) * (len(late) * step)
-    length = len(late) * step + REACH
-    fill(pixels, blocks, [(k, 0) for k in late], here, step, rows)
-    for tile in range(pixels.shape[0]):
         weights = tap_weights(coeff_ref, tile)
         history = []
         for tap in range(1, taps):
@@ -282,21 +276,24 @@
     strip[:, :length] = project(filtered, dense_ref, first, length)
     frame_ids = lax.broadcasted_iota(jnp.int32, strip.shape, 1)
     found = jnp.where(frame_ids < frames - first, strip[...], 0.0)
-    total = front_ref[...] + ready_ref[...] + pltpu.roll(found, first, 1)
-    running, reach = total, 1
-    while reach < frames:
-        shifted = pltpu.roll(running, reach, 1)
-        running = running + jnp.where(frame_ids >= reach, shifted, 0.0)
-        reach *= 2
-    counts = jnp.minimum(frame_ids + 1, BASE_WIN).astype(jnp.float32)
-    partial[...] = (total - running / counts).reshape(partial.shape)
-    for k in range(owners):
-        part_refs[k][...] = partial[position ^ k]
-
-
-def delta_kernel(inv_ref, filtered, _, out_ref, packed, sems, *, first, step):
-    subtract_mean(filtered, packed, inv_ref, step)
-    for copy in send_out(packed, out_ref, first, sems):
+    total = total_ref[...] + pltpu.roll(found, first, 1)
+    if last:
+        partial[...] = minus_mean(total).reshape(partial.shape)
+        for k, out in enumerate(outs):
+            out[...] = partial[position ^ k]
+    else:
+        outs[0][...] = total
+
+
+def delta_kernel(inv_ref, filtered, out_ref, packed, sems, *, step):
+    copies = []
+    for tile in range(packed.shape[0]):
+        at = pl.ds(tile, 1)
+        subtract_mean(filtered.at[at], packed.at[at], inv_ref, step)
+        place = out_ref.at[:, :, pl.ds(tile * LANES, LANES)]
+        copies.append(pltpu.make_async_copy(packed.at[tile], place, sems.at[tile]))
+        copies[-1].start()
+    for copy in copies:
         copy.wait()
 
 
@@ -312,36 +309,13 @@
     )
 
 
-def run_front(ids, inverse, coeffs, dense, blocks, places, slab_width):
-    _, rows, width = coeffs.shape
-    frames, tiles = inverse.shape[0], width // LANES
-    step = blocks[0].shape[0] // rows
-    held = pltpu.VMEM((tiles, frames * rows, LANES), jnp.float32)
-    return pl.pallas_call(
-        functools.partial(front_kernel, places=tuple(places), step=step),
-        out_shape=[
-            jax.ShapeDtypeStruct((frames, rows, slab_width), jnp.bfloat16),
-            jax.ShapeDtypeStruct((dense.shape[1], frames), jnp.float32),
-        ],
-        in_specs=[SMEM, SMEM] + [VMEM] * (2 + len(blocks)),
-        out_specs=[ANYWHERE, VMEM],
-        scratch_shapes=[
-            held,
-            held,
-            pltpu.VMEM((tiles, frames, rows, LANES), jnp.bfloat16),
-            pltpu.SemaphoreType.DMA((tiles,)),
-        ],
-        **options(12, frames * rows * width),
-    )(ids, inverse, coeffs, dense, *blocks)
-
-
-def run_ready(ids, coeffs, dense, blocks, places, frames, late):
+def run_early(ids, coeffs, dense, blocks, places, frames, late):
     _, rows, width = coeffs.shape
     step = blocks[0].shape[0] // rows
-    held = jax.ShapeDtypeStruct((width // LANES, (frames + REACH) * rows, LANES), jnp.float32)
+    held = jax.ShapeDtypeStruct((width // LANES, (frames + 2 * REACH) * rows, LANES), jnp.float32)
     return pl.pallas_call(
         functools.partial(
-            ready_kernel, places=tuple(places), step=step, frames=frames, late=tuple(late)
+            early_kernel, places=tuple(places), step=step, frames=frames, late=tuple(late)
         ),
         out_shape=[held, held, jax.ShapeDtypeStruct((dense.shape[1], frames), jnp.float32)],
         in_specs=[SMEM] + [VMEM] * (2 + len(blocks)),
@@ -350,39 +324,39 @@
     )(ids, coeffs, dense, *blocks)
 
 
-def run_traces(ids, coeffs, dense, front, ready, pixels, filtered, late, owners):
+def run_late(ids, coeffs, dense, total, pixels, filtered, late, owners, tile, last):
     _, rows, width = coeffs.shape
-    rois, frames = front.shape
+    rois, frames = total.shape
     held = jax.ShapeDtypeStruct(pixels.shape, jnp.float32)
-    part = jax.ShapeDtypeStruct((rois // owners, frames), jnp.float32)
+    parts = owners if last else 1
+    part = jax.ShapeDtypeStruct((rois // parts, frames), jnp.float32)
     return pl.pallas_call(
-        functools.partial(trace_kernel, late=tuple(late), owners=owners),
-        out_shape=[held, held] + [part] * owners,
-        in_specs=[SMEM] + [VMEM] * (6 + len(late)),
-        out_specs=[VMEM] * (2 + owners),
-        input_output_aliases={5: 0, 6: 1},
+        functools.partial(late_kernel, late=tuple(late), tile=tile, last=last),
+        out_shape=[held, held] + [part] * parts,
+        in_specs=[SMEM] + [VMEM] * (5 + len(late)),
+        out_specs=[VMEM] * (2 + parts),
+        input_output_aliases={4: 0, 5: 1},
         scratch_shapes=[
             pltpu.VMEM((rois, frames), jnp.float32),
             pltpu.VMEM((owners, rois // owners, frames), jnp.float32),
         ],
         **options(4, frames * rows * width),
-    )(ids, coeffs, dense, front, ready, pixels, filtered, *late.values())
-
-
-def run_delta(inverse, filtered, out, first, rows, step):
+    )(ids, coeffs, dense, total, pixels, filtered, *late.values())
+
+
+def run_delta(inverse, filtered, rows, step):
     tiles, frames = filtered.shape[0], inverse.shape[0]
     return pl.pallas_call(
-        functools.partial(delta_kernel, first=first, step=step),
-        out_shape=jax.ShapeDtypeStruct(out.shape, jnp.bfloat16),
-        in_specs=[SMEM, VMEM, ANYWHERE],
+        functools.partial(delta_kernel, step=step),
+        out_shape=jax.ShapeDtypeStruct((frames, rows, tiles * LANES), jnp.bfloat16),
+        in_specs=[SMEM, VMEM],
         out_specs=ANYWHERE,
-        input_output_aliases={2: 0},
         scratch_shapes=[
             pltpu.VMEM((tiles, frames, rows, LANES), jnp.bfloat16),
             pltpu.SemaphoreType.DMA((tiles,)),
         ],
         **options(4, frames * rows * tiles * LANES),
-    )(inverse, filtered, out)
+    )(inverse, filtered)
 
 
 def swaps(count, k):
@@ -474,7 +448,7 @@
 
     counts = jnp.minimum(jnp.arange(frames, dtype=jnp.int32) + 1, BASE_WIN)
     inverse = 1.0 / counts.astype(jnp.float32)
-    middle = slab_width // LANES // 2 * LANES
+    middle = slab_width - LANES
     ids = jnp.stack([here, position]).astype(jnp.int32)
     if frames > BASE_WIN or devices % 4 or middle == 0:
         return plain_plan(
@@ -507,27 +481,37 @@
     whole[0] = rows_of(rest, 0)
     dense = dense_of()
 
-    blocks, places = list(whole.values()), list(whole)
-    delta, front = run_front(
+    pixels, filtered, total = run_early(
+        ids, coeffs, dense, list(whole.values()), list(whole), frames, late
+    )
+    pixels, filtered, total = run_late(
         ids,
-        inverse,
         coeffs[:, :, :middle],
         dense[:, :, :middle],
-        blocks + list(low.values()),
-        [(k, 0) for k in places + late],
-        slab_width,
-    )
-    second, heavy = coeffs[:, :, middle:], dense[:, :, middle:]
-    pixels, filtered, ready = run_ready(
-        ids, second, heavy, blocks, [(k, middle) for k in places], frames, late
-    )
-    _, filtered, *parts = run_traces(
-        ids, second, heavy, front, ready, pixels, filtered, high, owners
+        total,
+        pixels,
+        filtered,
+        low,
+        owners,
+        0,
+        False,
+    )
+    _, filtered, *parts = run_late(
+        ids,
+        coeffs[:, :, middle:],
+        dense[:, :, middle:],
+        total,
+        pixels,
+        filtered,
+        high,
+        owners,
+        middle // LANES,
+        True,
     )
     traces = parts[0]
-    for k in range(1, owners):
+    for k in range(owners - 1, 0, -1):
         traces = traces + lax.ppermute(parts[k], "roi", swaps(owners, k))
-    return run_delta(inverse, filtered, delta, middle, rows, step), traces
+    return run_delta(inverse, filtered, rows, step), traces
 
 
 def solution(mesh):

time: 59.9 us -> 58.9 us (0.983)
  starting transfers between devices: 24.3 us -> 21.9 us
  other arithmetic: 1.32 us -> 2.66 us
  local copies, waits for them, and re-layouts: 3.65 us -> 4.51 us
  waiting for transfers between devices: 14.6 us -> 14 us
    ppermute x9, starting transfers between devices: 22.4 us -> 20 us  [send(): return lax.ppermute(block, 'tm', swaps(devices, k))]
    ppermute x3, waiting for transfers between devices: 0.88 us -> 0.01 us  [local(): traces = traces + lax.ppermute(parts[k], 'roi', swaps(owners, k))]
    dynamic_slice x3 -> x4, local copies, waits for them, and re-layouts: 3.49 us -> 4.33 us  [rows_of(): lax.dynamic_slice(source, (0, (here ^ k) * rows, low), (step, rows, high...]
    and x1, other arithmetic: 0.02 us -> 0.7 us  [local(): live = live & (roi_blocks // rows == position)]
    select_n x1, other arithmetic: 0.01 us -> 0.69 us  [local(): roi_blocks % rows]
  transfers between devices with their start and end apart: 12 -> 12, of which waited for: 5 -> 3; matrix products, arithmetic and copies ran while one was open for 5% -> 9% of each run, Pallas kernels for 13% -> 13%
where the time goes in v5:
time: 58.9 us; the launch traced here: 58.6 us
  starting transfers between devices  21.9 us (37%)
  waiting for transfers between devices  14 us (24%)
  Pallas kernels  8.86 us (15%)
  blocking collectives  5.8 us (10%)
  local copies, waits for them, and re-layouts  4.51 us (8%)
  other arithmetic  2.66 us (5%)
  between operations  0.84 us (1%)
    ppermute x9, starting transfers between devices, send(): return lax.ppermute(block, 'tm', swaps(devices, k))  20 us
    ppermute x9, waiting for transfers between devices, send(): return lax.ppermute(block, 'tm', swaps(devices, k))  14 us
    all_gather x1, blocking collectives, dense_of(): gathered = lax.all_gather(footprint_w, 'roi', axis=0, tiled=True)  5.8 us
    dynamic_slice x4, local copies, waits for them, and re-layouts, rows_of(): lax.dynamic_slice(source, (0, (here ^ k) * rows, low), (step, rows, high...  4.33 us
    pallas_call x1, Pallas kernels, run_early(): pl.pallas_call(functools.partial(early_kernel, places=tuple(places), step...  3.88 us
    pallas_call x2, Pallas kernels, run_late(): pl.pallas_call(functools.partial(late_kernel, late=tuple(late), tile=tile...  2.83 us
    pallas_call x1, Pallas kernels, run_delta(): pl.pallas_call(functools.partial(delta_kernel, step=step), out_shape=jax....  2.15 us
    ppermute x3, starting transfers between devices, local(): traces = traces + lax.ppermute(parts[k], 'roi', swaps(owners, k))  1.93 us
  transfers between devices with their start and end apart: 12, of which 3 were waited for; matrix products, arithmetic and copies ran while one was open for 9% of the time, Pallas kernels for 13%

profile of v5, /device:TPU:0, one launch (start us, length us, event | category | flops | bytes accessed | tf_op | source)
XLA Modules:
  0.0 58.6 jit_solution(7388419672557947232)
XLA Ops:
  0.7 1.1 %constant_dynamic-slice_fusion.8 = (bf16[16,16,512]{2,1,0:T(8,128)(2,1)S(1)}, bf16[16,16,512]{2,1,0:T(8,128)(2,1)S(1)}) fusion(bf16[16,128,512]{2,1,0:T(8,128)(2,1)} %param.5, s32[]{:T(128)S(6)} %select_n.54, s32[]{:T(128)S(6)} %select_n.53), kind=kLoop, calls=%fused_computation.23 | loop fusion | bytes 1048584 | tf_op jit(solution)/shard_map/dynamic_slice | solution.py:463
  1.8 6.1 %collective-permute-start = (bf16[256,512]{1,0:T(8,128)(2,1)S(1)}, bf16[256,512]{1,0:T(8,128)(2,1)S(1)}, u32[]{:S(2)}, u32[]{:S(2)}) collective-permute-start(bf16[256,512]{1,0:T(8,128)(2,1)S(1)} %bitcast.32), channel_id=1, source_target_pairs={{0,28},{4,24},{8,20},{12,16},{16,12},{20,8},{24,4},{28,0},{1,29},{... | collective-permute-start | bytes 786440 | tf_op jit(solution)/shard_map/ppermute | solution.py:471
  7.8 0.2 collective-permute-start.1
  8.1 1.3 %constant_dynamic-slice_fusion.4 = (bf16[16,16,512]{2,1,0:T(8,128)(2,1)S(1)}, bf16[16,16,512]{2,1,0:T(8,128)(2,1)S(1)}, bf16[16,16,512]{2,1,0:T(8,128)(2,1)S(1)}, bf16[16,16,512]{2,1,0:T(8,128)(2,1)S(1)}) fusion(bf16[16,128,512]{2,1,0:T(8,128)(2,1)} %param.5, s32[]{:T(128)S(6)} %select_n.58, s32[]{:T(128)S(6)} %select_n.57, s32[]{:T(128)S(6)} %select_n.56, ...), kind=kLoop, calls=%fused_computation.19 | loop fusion | bytes 2097168 | tf_op jit(solution)/shard_map/dynamic_slice | solution.py:463
  9.3 0.5 collective-permute-start.4
  9.8 0.0 collective-permute-start.3
  9.8 3.1 %collective-permute-start.2 = (bf16[256,512]{1,0:T(8,128)(2,1)S(1)}, bf16[256,512]{1,0:T(8,128)(2,1)S(1)}, u32[]{:S(2)}, u32[]{:S(2)}) collective-permute-start(bf16[256,512]{1,0:T(8,128)(2,1)S(1)} %bitcast.33), channel_id=1, source_target_pairs={{0,12},{4,8},{8,4},{12,0},{16,28},{20,24},{24,20},{28,16},{1,13},{... | collective-permute-start | bytes 786440 | tf_op jit(solution)/shard_map/ppermute | solution.py:471
  12.9 0.7 %add_select_fusion = s32[64,3]{0,1:T(4,128)S(1)} fusion(s32[64,3]{0,1:T(4,128)} %param.8), kind=kLoop, calls=%fused_computation.10 | loop fusion | flops 2112 | bytes 1536 | tf_op jit(solution)/shard_map/jit(remainder)/select_n | solution.py:439
  13.6 5.8 %all_gather.3 = bf16[64,3,512]{2,0,1:T(8,128)(2,1)S(1)} all-gather(bf16[16,3,512]{2,0,1:T(8,128)(2,1)} %param.7), channel_id=1, replica_groups=mesh['tm'=8,'roi'=4] {'roi'}, dimensions={0}, use_global_device_ids=true | all-gather | bytes 245760 | tf_op jit(solution)/shard_map/all_gather | solution.py:443
  19.4 0.7 %fusion.2 = pred[64,3]{0,1:T(4,128)(4,1)S(1)} fusion(s32[64,3]{0,1:T(4,128)} %param.8, s32[]{:T(128)} %axis_index.25, s32[64]{0:T(128)} %param.9), kind=kLoop, calls=%fused_computation.28 | loop fusion | flops 3456 | bytes 1220 | tf_op jit(solution)/shard_map/and | solution.py:437
  20.1 1.1 %constant_dynamic-slice_fusion.2 = (bf16[16,16,384]{2,1,0:T(8,128)(2,1)S(1)}, bf16[16,16,384]{2,1,0:T(8,128)(2,1)S(1)}) fusion(bf16[16,128,512]{2,1,0:T(8,128)(2,1)} %param.5, s32[]{:T(128)S(6)} %select_n.60, s32[]{:T(128)S(6)} %select_n.59), kind=kLoop, calls=%fused_computation.17 | loop fusion | bytes 786440 | tf_op jit(solution)/shard_map/dynamic_slice | solution.py:463
  21.2 0.0 collective-permute-done.4.rest_4_
  21.2 2.2 %collective-permute-start.5 = (bf16[256,384]{1,0:T(8,128)(2,1)S(1)}, bf16[256,384]{1,0:T(8,128)(2,1)S(1)}, u32[]{:S(2)}, u32[]{:S(2)}) collective-permute-start(bf16[256,384]{1,0:T(8,128)(2,1)S(1)} %bitcast.37), channel_id=1, source_target_pairs={{0,20},{4,16},{8,28},{12,24},{16,4},{20,0},{24,12},{28,8},{1,21},{... | collective-permute-start | bytes 589832 | tf_op jit(solution)/shard_map/ppermute | solution.py:471
  23.4 0.6 select_add_fusion.dense_ref
  24.1 0.1 slice.47.dense_ref
  24.2 3.1 %collective-permute-start.6 = (bf16[256,384]{1,0:T(8,128)(2,1)S(1)}, bf16[256,384]{1,0:T(8,128)(2,1)S(1)}, u32[]{:S(2)}, u32[]{:S(2)}) collective-permute-start(bf16[256,384]{1,0:T(8,128)(2,1)S(1)} %bitcast.36), channel_id=1, source_target_pairs={{0,16},{4,20},{8,24},{12,28},{16,0},{20,4},{24,8},{28,12},{1,17},{... | collective-permute-start | bytes 589832 | tf_op jit(solution)/shard_map/ppermute | solution.py:471
  27.4 0.9 %constant_dynamic-slice_fusion = (bf16[16,16,128]{2,1,0:T(8,128)(2,1)S(1)}, bf16[16,16,128]{2,1,0:T(8,128)(2,1)S(1)}) fusion(bf16[16,128,512]{2,1,0:T(8,128)(2,1)} %param.5, s32[]{:T(128)S(6)} %select_n.60, s32[]{:T(128)S(6)} %select_n.59), kind=kLoop, calls=%fused_computation.15 | loop fusion | bytes 262152 | tf_op jit(solution)/shard_map/dynamic_slice | solution.py:463
  28.2 0.0 collective-permute-done.1.rest_1_
  28.3 4.8 %collective-permute-start.7 = (bf16[256,128]{1,0:T(8,128)(2,1)S(1)}, bf16[256,128]{1,0:T(8,128)(2,1)S(1)}, u32[]{:S(2)}, u32[]{:S(2)}) collective-permute-start(bf16[256,128]{1,0:T(8,128)(2,1)S(1)} %bitcast.39), channel_id=1, source_target_pairs={{0,20},{4,16},{8,28},{12,24},{16,4},{20,0},{24,12},{28,8},{1,21},{... | collective-permute-start | bytes 196616 | tf_op jit(solution)/shard_map/ppermute | solution.py:471
  33.1 12.1 %collective-permute-done.5.rest_0_ = bf16[256,384]{1,0:T(8,128)(2,1)S(1)} collective-permute-done((bf16[256,384]{1,0:T(8,128)(2,1)S(1)}, bf16[256,384]{1,0:T(8,128)(2,1)S(1)}, u32[]{:S(2)}, u32[]{:S(2)}) %collective-permute-start.5) | collective-permute-done | bytes 196640 | tf_op jit(solution)/shard_map/ppermute | solution.py:471
  45.2 0.0 collective-permute-start.8
  45.2 0.1 pad_add_fusion.ids_ref
  45.2 3.9 %shard_map.68 = (f32[4,2304,128]{2,1,0:T(8,128)S(1)}, f32[4,2304,128]{2,1,0:T(8,128)S(1)}, f32[64,128]{1,0:T(8,128)S(1)}) custom-call(s32[2]{0:T(128)S(1)} %pad_add_fusion.ids_ref, bf16[5,16,512]{2,1,0:T(8,128)(2,1)S(1)} %copy-done, bf16[16,64,512]{2,1,0:T(8,128)(2,1)S(1)} %select_add_fusion.dense_ref, bf16[256,512]{1,0:T(8,128)(2,1)S(1)} %collective-permute-done.rest_0_, ...), custom_call_target="tpu_custom_call" | custom-call | flops 16777216 | bytes 4194304 | tf_op jit(solution)/shard_map/pallas_call | solution.py:316
  49.1 1.6 %collective-permute-done.6.rest_1_ = bf16[256,384]{1,0:T(8,128)(2,1)S(1)} collective-permute-done((bf16[256,384]{1,0:T(8,128)(2,1)S(1)}, bf16[256,384]{1,0:T(8,128)(2,1)S(1)}, u32[]{:S(2)}, u32[]{:S(2)}) %collective-permute-start.6) | collective-permute-done | bytes 196640 | tf_op jit(solution)/shard_map/ppermute | solution.py:471
  50.7 1.6 %shard_map.69 = (f32[4,2304,128]{2,1,0:T(8,128)S(1)}, f32[4,2304,128]{2,1,0:T(8,128)S(1)}, f32[64,128]{1,0:T(8,128)S(1)}) custom-call(s32[2]{0:T(128)S(1)} %pad_add_fusion.ids_ref, bf16[5,16,384]{2,1,0:T(8,128)(2,1)S(1)} %slice.38.coeff_ref, bf16[16,64,384]{2,1,0:T(8,128)(2,1)S(1)} %slice.47.dense_ref, ...), custom_call_target="tpu_custom_call", output_to_operand_aliasing={{0}: (4, {}), {1}: (5, {})} | custom-call | flops 12582912 | bytes 3145728 | tf_op jit(solution)/shard_map/pallas_call | solution.py:333
  52.3 0.3 collective-permute-done.8.rest_1_
  52.6 1.2 %shard_map.70 = (f32[4,2304,128]{2,1,0:T(8,128)S(1)}, f32[4,2304,128]{2,1,0:T(8,128)S(1)}, f32[16,128]{1,0:T(8,128)S(1)}, f32[16,128]{1,0:T(8,128)S(1)}, f32[16,128]{1,0:T(8,128)S(1)}, /*index=5*/f32[16,128]{1,0:T(8,128)S(1)}) custom-call(s32[2]{0:T(128)S(1)} %pad_add_fusion.ids_ref, ...), custom_call_target="tpu_custom_call", output_to_operand_aliasing={{0}: (4, {}), {1}: (5, {})} | custom-call | flops 4194304 | bytes 1048576 | tf_op jit(solution)/shard_map/pallas_call | solution.py:333
  53.8 0.4 collective-permute-start.9
  54.2 1.3 %collective-permute-start.10 = (f32[16,128]{1,0:T(8,128)S(1)}, f32[16,128]{1,0:T(8,128)S(1)}, u32[]{:S(2)}, u32[]{:S(2)}) collective-permute-start(f32[16,128]{1,0:T(8,128)S(1)} %get-tuple-element.36), channel_id=1, source_target_pairs={{0,2},{1,3},{2,0},{3,1},{4,6},{5,7},{6,4},{7,5},{8,10},{9,11},{10,... | collective-permute-start | bytes 24584 | tf_op jit(solution)/shard_map/ppermute | solution.py:513
  55.5 0.3 collective-permute-start.11
  55.8 2.1 %shard_map.71 = bf16[128,16,512]{2,1,0:T(8,128)(2,1)} custom-call(f32[128]{0:T(128)S(1)} %convert_divide_fusion.inv_ref, f32[4,2304,128]{2,1,0:T(8,128)S(1)} %get-tuple-element.33.filtered), custom_call_target="tpu_custom_call" | custom-call | flops 16777216 | bytes 4194304 | tf_op jit(solution)/shard_map/pallas_call | solution.py:349
  58.0 0.6 %add_add_fusion = f32[16,128]{1,0:T(8,128)} fusion(f32[16,128]{1,0:T(8,128)S(1)} %collective-permute-done.11, f32[16,128]{1,0:T(8,128)S(1)} %collective-permute-done.10, f32[16,128]{1,0:T(8,128)S(1)} %get-tuple-element.34, f32[16,128]{1,0:T(8,128)S(1)} %collective-permute-done.9), kind=kLoop, calls=%fused_computation.6 | loop fusion | flops 6144 | bytes 40960 | tf_op jit(solution)/shard_map/add | solution.py:513
  (16 shorter events, 0.1 us)
Async XLA Ops:
  0.6 23.4 %copy-start = (bf16[5,16,512]{2,1,0:T(8,128)(2,1)S(1)}, bf16[5,16,512]{2,1,0:T(8,128)(2,1)}, u32[]{:S(2)}) copy-start(bf16[5,16,512]{2,1,0:T(8,128)(2,1)} %coeff_ref.1) | copy-start | bytes 245764
  1.8 22.4 %collective-permute-start = (bf16[256,512]{1,0:T(8,128)(2,1)S(1)}, bf16[256,512]{1,0:T(8,128)(2,1)S(1)}, u32[]{:S(2)}, u32[]{:S(2)}) collective-permute-start(bf16[256,512]{1,0:T(8,128)(2,1)S(1)} %bitcast.32), channel_id=1, source_target_pairs={{0,28},{4,24},{8,20},{12,16},{16,12},{20,8},{24,4},{28,0},{1,29},{... | collective-permute-start | bytes 786440 | tf_op jit(solution)/shard_map/ppermute | solution.py:471
  7.8 20.4 %collective-permute-start.1 = (bf16[256,512]{1,0:T(8,128)(2,1)S(1)}, bf16[256,512]{1,0:T(8,128)(2,1)S(1)}, u32[]{:S(2)}, u32[]{:S(2)}) collective-permute-start(bf16[256,512]{1,0:T(8,128)(2,1)S(1)} %bitcast.31), channel_id=1, source_target_pairs={{0,24},{4,28},{8,16},{12,20},{16,8},{20,12},{24,0},{28,4},{1,25},{... | collective-permute-start | bytes 786440 | tf_op jit(solution)/shard_map/ppermute | solution.py:471
  9.3 11.9 %collective-permute-start.4 = (bf16[256,512]{1,0:T(8,128)(2,1)S(1)}, bf16[256,512]{1,0:T(8,128)(2,1)S(1)}, u32[]{:S(2)}, u32[]{:S(2)}) collective-permute-start(bf16[256,512]{1,0:T(8,128)(2,1)S(1)} %bitcast.35), channel_id=1, source_target_pairs={{0,4},{4,0},{8,12},{12,8},{16,20},{20,16},{24,28},{28,24},{1,5},{5... | collective-permute-start | bytes 786440 | tf_op jit(solution)/shard_map/ppermute | solution.py:471
  9.8 35.4 %collective-permute-start.3 = (bf16[256,512]{1,0:T(8,128)(2,1)S(1)}, bf16[256,512]{1,0:T(8,128)(2,1)S(1)}, u32[]{:S(2)}, u32[]{:S(2)}) collective-permute-start(bf16[256,512]{1,0:T(8,128)(2,1)S(1)} %bitcast.34), channel_id=1, source_target_pairs={{0,8},{4,12},{8,0},{12,4},{16,24},{20,28},{24,16},{28,20},{1,9},{5... | collective-permute-start | bytes 786440 | tf_op jit(solution)/shard_map/ppermute | solution.py:471
  9.8 35.4 %collective-permute-start.2 = (bf16[256,512]{1,0:T(8,128)(2,1)S(1)}, bf16[256,512]{1,0:T(8,128)(2,1)S(1)}, u32[]{:S(2)}, u32[]{:S(2)}) collective-permute-start(bf16[256,512]{1,0:T(8,128)(2,1)S(1)} %bitcast.33), channel_id=1, source_target_pairs={{0,12},{4,8},{8,4},{12,0},{16,28},{20,24},{24,20},{28,16},{1,13},{... | collective-permute-start | bytes 786440 | tf_op jit(solution)/shard_map/ppermute | solution.py:471
  21.2 23.9 %collective-permute-start.5 = (bf16[256,384]{1,0:T(8,128)(2,1)S(1)}, bf16[256,384]{1,0:T(8,128)(2,1)S(1)}, u32[]{:S(2)}, u32[]{:S(2)}) collective-permute-start(bf16[256,384]{1,0:T(8,128)(2,1)S(1)} %bitcast.37), channel_id=1, source_target_pairs={{0,20},{4,16},{8,28},{12,24},{16,4},{20,0},{24,12},{28,8},{1,21},{... | collective-permute-start | bytes 589832 | tf_op jit(solution)/shard_map/ppermute | solution.py:471
  24.2 26.5 %collective-permute-start.6 = (bf16[256,384]{1,0:T(8,128)(2,1)S(1)}, bf16[256,384]{1,0:T(8,128)(2,1)S(1)}, u32[]{:S(2)}, u32[]{:S(2)}) collective-permute-start(bf16[256,384]{1,0:T(8,128)(2,1)S(1)} %bitcast.36), channel_id=1, source_target_pairs={{0,16},{4,20},{8,24},{12,28},{16,0},{20,4},{24,8},{28,12},{1,17},{... | collective-permute-start | bytes 589832 | tf_op jit(solution)/shard_map/ppermute | solution.py:471
  28.3 24.1 %collective-permute-start.7 = (bf16[256,128]{1,0:T(8,128)(2,1)S(1)}, bf16[256,128]{1,0:T(8,128)(2,1)S(1)}, u32[]{:S(2)}, u32[]{:S(2)}) collective-permute-start(bf16[256,128]{1,0:T(8,128)(2,1)S(1)} %bitcast.39), channel_id=1, source_target_pairs={{0,20},{4,16},{8,28},{12,24},{16,4},{20,0},{24,12},{28,8},{1,21},{... | collective-permute-start | bytes 196616 | tf_op jit(solution)/shard_map/ppermute | solution.py:471
  45.2 7.5 %collective-permute-start.8 = (bf16[256,128]{1,0:T(8,128)(2,1)S(1)}, bf16[256,128]{1,0:T(8,128)(2,1)S(1)}, u32[]{:S(2)}, u32[]{:S(2)}) collective-permute-start(bf16[256,128]{1,0:T(8,128)(2,1)S(1)} %bitcast.38), channel_id=1, source_target_pairs={{0,16},{4,20},{8,24},{12,28},{16,0},{20,4},{24,8},{28,12},{1,17},{... | collective-permute-start | bytes 196616 | tf_op jit(solution)/shard_map/ppermute | solution.py:471
  53.8 4.1 %collective-permute-start.9 = (f32[16,128]{1,0:T(8,128)S(1)}, f32[16,128]{1,0:T(8,128)S(1)}, u32[]{:S(2)}, u32[]{:S(2)}) collective-permute-start(f32[16,128]{1,0:T(8,128)S(1)} %get-tuple-element.35), channel_id=1, source_target_pairs={{0,3},{1,2},{2,1},{3,0},{4,7},{5,6},{6,5},{7,4},{8,11},{9,10},{10,... | collective-permute-start | bytes 24584 | tf_op jit(solution)/shard_map/ppermute | solution.py:513
  54.2 3.7 %collective-permute-start.10 = (f32[16,128]{1,0:T(8,128)S(1)}, f32[16,128]{1,0:T(8,128)S(1)}, u32[]{:S(2)}, u32[]{:S(2)}) collective-permute-start(f32[16,128]{1,0:T(8,128)S(1)} %get-tuple-element.36), channel_id=1, source_target_pairs={{0,2},{1,3},{2,0},{3,1},{4,6},{5,7},{6,4},{7,5},{8,10},{9,11},{10,... | collective-permute-start | bytes 24584 | tf_op jit(solution)/shard_map/ppermute | solution.py:513
  55.5 2.5 %collective-permute-start.11 = (f32[16,128]{1,0:T(8,128)S(1)}, f32[16,128]{1,0:T(8,128)S(1)}, u32[]{:S(2)}, u32[]{:S(2)}) collective-permute-start(f32[16,128]{1,0:T(8,128)S(1)} %get-tuple-element.37), channel_id=1, source_target_pairs={{0,1},{1,0},{2,3},{3,2},{4,5},{5,4},{6,7},{7,6},{8,9},{9,8},{10,11... | collective-permute-start | bytes 24584 | tf_op jit(solution)/shard_map/ppermute | solution.py:513

commit v6 on v5

--- a/solution.py
+++ b/solution.py
@@ -155,25 +155,6 @@
         lax.fori_loop(0, frames // step, block_step, (zero,) * (taps - 1))
 
 
-def subtract_mean(filtered, packed, inv_ref, step):
-    tiles, frames, rows, _ = packed.shape
-
-    def block_step(index, running):
-        running = list(running)
-        for offset in range(step):
-            frame = index * step + offset
-            for tile in range(tiles):
-                value = filtered[tile, frame_rows(frame, rows), :]
-                running[tile] = running[tile] + value
-                packed[tile, frame] = (value - running[tile] * inv_ref[frame]).astype(
-                    jnp.bfloat16
-                )
-        return tuple(running)
-
-    zero = jnp.zeros((rows, LANES), jnp.float32)
-    lax.fori_loop(0, frames // step, block_step, (zero,) * tiles)
-
-
 def project(filtered, dense_ref, first, frames):
     rows = dense_ref.shape[0]
     total = 0.0
@@ -243,37 +224,41 @@
     total_ref[...] = project(filtered, dense_ref, 0, frames)
 
 
-def late_kernel(ids_ref, coeff_ref, dense_ref, total_ref, _px, _ft, *rest, late, tile, last):
+def late_kernel(ids_ref, coeff_ref, dense_ref, total_ref, pixels, *rest, late, first_tile, last):
     blocks = rest[: len(late)]
-    all_pixels, all_filtered, *outs, strip, partial = rest[len(late) :]
+    filtered, *outs, held, strip, partial = rest[len(late) :]
     here, position = ids_ref[0], ids_ref[1]
     taps, rows, width = coeff_ref.shape
     step = blocks[0].shape[0] // rows
-    tiles = width // LANES
     frames = total_ref.shape[1]
-    pixels = all_pixels.at[tile : tile + tiles]
-    filtered = all_filtered.at[tile : tile + tiles]
     first, length = late_frames(here, late, step)
-    fill(pixels, blocks, [(k, 0) for k in late], here, step, rows)
-    for tile in range(tiles):
+    for tile in range(width // LANES):
+        own = pixels.at[first_tile + tile]
+        for block, k in zip(blocks, late):
+            start = pl.multiple_of(((here ^ k) * step - first) * rows, step * rows)
+            held[pl.ds(start, step * rows), :] = block[
+                :, tile * LANES : (tile + 1) * LANES
+            ].astype(jnp.float32)
+        after = pl.multiple_of((first + length - REACH) * rows, step * rows)
+        held[(length - REACH) * rows :, :] = own[pl.ds(after, REACH * rows), :]
         weights = tap_weights(coeff_ref, tile)
         history = []
         for tap in range(1, taps):
-            earlier = pixels[tile, frame_rows(jnp.maximum(first - tap, 0), rows), :]
+            earlier = own[frame_rows(jnp.maximum(first - tap, 0), rows), :]
             history.append(jnp.where(first > 0, earlier, 0.0))
 
         def block_step(index, history):
             history = list(history)
             for offset in range(REACH):
-                at = frame_rows(first + index * REACH + offset, rows)
-                now = pixels[tile, at, :]
+                at = frame_rows(index * REACH + offset, rows)
+                now = held[at, :]
                 filtered[tile, at, :] = filtered_at(now, history, weights)
                 history = [now] + history[:-1]
             return tuple(history)
 
         lax.fori_loop(0, length // REACH, block_step, tuple(history))
     strip[...] = jnp.zeros(strip.shape, jnp.float32)
-    strip[:, :length] = project(filtered, dense_ref, first, length)
+    strip[:, :length] = project(filtered, dense_ref, 0, length)
     frame_ids = lax.broadcasted_iota(jnp.int32, strip.shape, 1)
     found = jnp.where(frame_ids < frames - first, strip[...], 0.0)
     total = total_ref[...] + pltpu.roll(found, first, 1)
@@ -285,11 +270,36 @@
         outs[0][...] = total
 
 
-def delta_kernel(inv_ref, filtered, out_ref, packed, sems, *, step):
+def delta_kernel(ids_ref, inv_ref, *rest, late, step):
+    *pieces, filtered, out_ref, packed, sems = rest
+    pieces = pieces[::-1]
+    tiles, frames, rows, _ = packed.shape
+    first, length = late_frames(ids_ref[0], late, step)
+    places = [(piece, tile) for piece in pieces for tile in range(piece.shape[0])]
     copies = []
-    for tile in range(packed.shape[0]):
-        at = pl.ds(tile, 1)
-        subtract_mean(filtered.at[at], packed.at[at], inv_ref, step)
+    for tile, (piece, its_tile) in enumerate(places):
+
+        def subtract_mean(source, low, high, running):
+            def block_step(index, running):
+                for offset in range(REACH):
+                    frame = index * REACH + offset
+                    value = source(frame)
+                    running = running + value
+                    packed[tile, frame] = (value - running * inv_ref[frame]).astype(jnp.bfloat16)
+                return running
+
+            return lax.fori_loop(low // REACH, high // REACH, block_step, running)
+
+        def early(frame):
+            return filtered[tile, frame_rows(frame, rows), :]
+
+        def middle(frame):
+            return piece[its_tile, frame_rows(frame - first, rows), :]
+
+        end = jnp.minimum(first + length, frames)
+        running = subtract_mean(early, 0, first, jnp.zeros((rows, LANES), jnp.float32))
+        running = subtract_mean(middle, first, end, running)
+        subtract_mean(early, end, frames, running)
         place = out_ref.at[:, :, pl.ds(tile * LANES, LANES)]
         copies.append(pltpu.make_async_copy(packed.at[tile], place, sems.at[tile]))
         copies[-1].start()
@@ -324,39 +334,40 @@
     )(ids, coeffs, dense, *blocks)
 
 
-def run_late(ids, coeffs, dense, total, pixels, filtered, late, owners, tile, last):
+def run_late(ids, coeffs, dense, total, pixels, late, owners, first_tile, last):
     _, rows, width = coeffs.shape
     rois, frames = total.shape
-    held = jax.ShapeDtypeStruct(pixels.shape, jnp.float32)
+    height = sum(block.shape[0] for block in late.values()) + REACH * rows
     parts = owners if last else 1
     part = jax.ShapeDtypeStruct((rois // parts, frames), jnp.float32)
     return pl.pallas_call(
-        functools.partial(late_kernel, late=tuple(late), tile=tile, last=last),
-        out_shape=[held, held] + [part] * parts,
-        in_specs=[SMEM] + [VMEM] * (5 + len(late)),
-        out_specs=[VMEM] * (2 + parts),
-        input_output_aliases={4: 0, 5: 1},
+        functools.partial(late_kernel, late=tuple(late), first_tile=first_tile, last=last),
+        out_shape=[jax.ShapeDtypeStruct((width // LANES, height, LANES), jnp.float32)]
+        + [part] * parts,
+        in_specs=[SMEM] + [VMEM] * (4 + len(late)),
+        out_specs=[VMEM] * (1 + parts),
         scratch_shapes=[
+            pltpu.VMEM((height, LANES), jnp.float32),
             pltpu.VMEM((rois, frames), jnp.float32),
             pltpu.VMEM((owners, rois // owners, frames), jnp.float32),
         ],
         **options(4, frames * rows * width),
-    )(ids, coeffs, dense, total, pixels, filtered, *late.values())
-
-
-def run_delta(inverse, filtered, rows, step):
+    )(ids, coeffs, dense, total, pixels, *late.values())
+
+
+def run_delta(ids, inverse, filtered, pieces, late, rows, step):
     tiles, frames = filtered.shape[0], inverse.shape[0]
     return pl.pallas_call(
-        functools.partial(delta_kernel, step=step),
+        functools.partial(delta_kernel, late=tuple(late), step=step),
         out_shape=jax.ShapeDtypeStruct((frames, rows, tiles * LANES), jnp.bfloat16),
-        in_specs=[SMEM, VMEM],
+        in_specs=[SMEM, SMEM] + [VMEM] * (1 + len(pieces)),
         out_specs=ANYWHERE,
         scratch_shapes=[
             pltpu.VMEM((tiles, frames, rows, LANES), jnp.bfloat16),
             pltpu.SemaphoreType.DMA((tiles,)),
         ],
         **options(4, frames * rows * tiles * LANES),
-    )(inverse, filtered)
+    )(ids, inverse, *pieces[::-1], filtered)
 
 
 def swaps(count, k):
@@ -456,7 +467,7 @@
         )
 
     far = list(range(devices - 1, devices // 2 - 1, -1))
-    near = list(range(devices // 2 - 1, 0, -1))
+    near = list(range(1, devices // 2))
     early, late = far[: len(far) // 2], far[len(far) // 2 :]
 
     def rows_of(source, k, low=0, high=slab_width):
@@ -474,7 +485,7 @@
     rest, *opening = lax.optimization_barrier((movie, *opening))
     whole = {k: send(block, k) for block, k in zip(opening, early)}
     whole |= {k: send(rows_of(rest, k), k) for k in near}
-    ties = [whole[near[-1]]] + [whole[k] for k in early]
+    ties = [whole[near[0]]] + [whole[k] for k in early]
     low = {k: send(rows_of(rest, k, 0, middle), k, tie) for k, tie in zip(late, ties)}
     ties = ties[len(late) :] + list(low.values())
     high = {k: send(rows_of(rest, k, middle), k, tie) for k, tie in zip(late, ties)}
@@ -484,34 +495,36 @@
     pixels, filtered, total = run_early(
         ids, coeffs, dense, list(whole.values()), list(whole), frames, late
     )
-    pixels, filtered, total = run_late(
+    lower, total = run_late(
         ids,
         coeffs[:, :, :middle],
         dense[:, :, :middle],
         total,
         pixels,
-        filtered,
         low,
         owners,
         0,
         False,
     )
-    _, filtered, *parts = run_late(
+    pixels, filtered, lower, total = lax.optimization_barrier(
+        (pixels, filtered, lower, total)
+    )
+    upper, *parts = run_late(
         ids,
         coeffs[:, :, middle:],
         dense[:, :, middle:],
         total,
         pixels,
-        filtered,
         high,
         owners,
         middle // LANES,
         True,
     )
     traces = parts[0]
-    for k in range(owners - 1, 0, -1):
+    for k in range(1, owners):
         traces = traces + lax.ppermute(parts[k], "roi", swaps(owners, k))
-    return run_delta(inverse, filtered, rows, step), traces
+    delta = run_delta(ids, inverse, filtered, [lower, upper], late, rows, step)
+    return delta, traces
 
 
 def solution(mesh):

time: 58.9 us -> 59.1 us (level)
  starting transfers between devices: 21.9 us -> 23.3 us
  other arithmetic: 2.66 us -> 1.29 us
    ppermute x9, starting transfers between devices: 20 us -> 21.4 us  [send(): return lax.ppermute(block, 'tm', swaps(devices, k))]
    and x1, other arithmetic: 0.7 us -> 0.02 us  [local(): live = live & (roi_blocks // rows == position)]
    select_n x1, other arithmetic: 0.69 us -> 0.01 us  [local(): roi_blocks % rows]
  transfers between devices with their start and end apart: 12 -> 12, of which waited for: 3 -> 4; matrix products, arithmetic and copies ran while one was open for 9% -> 7% of each run, Pallas kernels for 13% -> 13%
where the time goes in v6:
time: 59.1 us; the launch traced here: 58.9 us
  starting transfers between devices  23.3 us (39%)
  waiting for transfers between devices  14.1 us (24%)
  Pallas kernels  9.17 us (16%)
  blocking collectives  5.61 us (9%)
  local copies, waits for them, and re-layouts  4.53 us (8%)
  other arithmetic  1.29 us (2%)
  between operations  0.87 us (1%)
    ppermute x9, starting transfers between devices, send(): return lax.ppermute(block, 'tm', swaps(devices, k))  21.4 us
    ppermute x9, waiting for transfers between devices, send(): return lax.ppermute(block, 'tm', swaps(devices, k))  14.1 us
    all_gather x1, blocking collectives, dense_of(): gathered = lax.all_gather(footprint_w, 'roi', axis=0, tiled=True)  5.61 us
    dynamic_slice x4, local copies, waits for them, and re-layouts, rows_of(): lax.dynamic_slice(source, (0, (here ^ k) * rows, low), (step, rows, high...  4.34 us
    pallas_call x1, Pallas kernels, run_early(): pl.pallas_call(functools.partial(early_kernel, places=tuple(places), step...  3.88 us
    pallas_call x2, Pallas kernels, run_late(): pl.pallas_call(functools.partial(late_kernel, late=tuple(late), first_til...  2.85 us
    pallas_call x1, Pallas kernels, run_delta(): pl.pallas_call(functools.partial(delta_kernel, late=tuple(late), step=ste...  2.44 us
    ppermute x3, starting transfers between devices, local(): traces = traces + lax.ppermute(parts[k], 'roi', swaps(owners, k))  1.93 us
  transfers between devices with their start and end apart: 12, of which 4 were waited for; matrix products, arithmetic and copies ran while one was open for 7% of the time, Pallas kernels for 13%

profile of v6, /device:TPU:0, one launch (start us, length us, event | category | flops | bytes accessed | tf_op | source)
XLA Modules:
  0.0 58.9 jit_solution(13532619867703458670)
XLA Ops:
  0.7 1.1 %constant_dynamic-slice_fusion.8 = (bf16[16,16,512]{2,1,0:T(8,128)(2,1)S(1)}, bf16[16,16,512]{2,1,0:T(8,128)(2,1)S(1)}) fusion(bf16[16,128,512]{2,1,0:T(8,128)(2,1)} %param.5, s32[]{:T(128)S(6)} %select_n.54, s32[]{:T(128)S(6)} %select_n.53), kind=kLoop, calls=%fused_computation.23 | loop fusion | bytes 1048584 | tf_op jit(solution)/shard_map/dynamic_slice | solution.py:474
  1.8 6.1 %collective-permute-start = (bf16[256,512]{1,0:T(8,128)(2,1)S(1)}, bf16[256,512]{1,0:T(8,128)(2,1)S(1)}, u32[]{:S(2)}, u32[]{:S(2)}) collective-permute-start(bf16[256,512]{1,0:T(8,128)(2,1)S(1)} %bitcast.32), channel_id=1, source_target_pairs={{0,28},{4,24},{8,20},{12,16},{16,12},{20,8},{24,4},{28,0},{1,29},{... | collective-permute-start | bytes 786440 | tf_op jit(solution)/shard_map/ppermute | solution.py:482
  7.8 0.2 collective-permute-start.1
  8.1 1.3 %constant_dynamic-slice_fusion.4 = (bf16[16,16,512]{2,1,0:T(8,128)(2,1)S(1)}, bf16[16,16,512]{2,1,0:T(8,128)(2,1)S(1)}, bf16[16,16,512]{2,1,0:T(8,128)(2,1)S(1)}, bf16[16,16,512]{2,1,0:T(8,128)(2,1)S(1)}) fusion(bf16[16,128,512]{2,1,0:T(8,128)(2,1)} %param.5, s32[]{:T(128)S(6)} %select_n.58, s32[]{:T(128)S(6)} %select_n.57, s32[]{:T(128)S(6)} %select_n.56, ...), kind=kLoop, calls=%fused_computation.19 | loop fusion | bytes 2097168 | tf_op jit(solution)/shard_map/dynamic_slice | solution.py:474
  9.3 0.5 collective-permute-start.2
  9.8 0.0 collective-permute-start.3
  9.8 3.1 %collective-permute-start.4 = (bf16[256,512]{1,0:T(8,128)(2,1)S(1)}, bf16[256,512]{1,0:T(8,128)(2,1)S(1)}, u32[]{:S(2)}, u32[]{:S(2)}) collective-permute-start(bf16[256,512]{1,0:T(8,128)(2,1)S(1)} %bitcast.33), channel_id=1, source_target_pairs={{0,12},{4,8},{8,4},{12,0},{16,28},{20,24},{24,20},{28,16},{1,13},{... | collective-permute-start | bytes 786440 | tf_op jit(solution)/shard_map/ppermute | solution.py:482
  12.9 5.6 %all_gather.3 = bf16[64,3,512]{2,0,1:T(8,128)(2,1)S(1)} all-gather(bf16[16,3,512]{2,0,1:T(8,128)(2,1)S(1)} %copy-done.1), channel_id=1, replica_groups=mesh['tm'=8,'roi'=4] {'roi'}, dimensions={0}, use_global_device_ids=true | all-gather | bytes 245760 | tf_op jit(solution)/shard_map/all_gather | solution.py:454
  18.6 1.1 %constant_dynamic-slice_fusion.2 = (bf16[16,16,384]{2,1,0:T(8,128)(2,1)S(1)}, bf16[16,16,384]{2,1,0:T(8,128)(2,1)S(1)}) fusion(bf16[16,128,512]{2,1,0:T(8,128)(2,1)} %param.5, s32[]{:T(128)S(6)} %select_n.60, s32[]{:T(128)S(6)} %select_n.59), kind=kLoop, calls=%fused_computation.17 | loop fusion | bytes 786440 | tf_op jit(solution)/shard_map/dynamic_slice | solution.py:474
  19.7 0.1 collective-permute-done.2.rest_2_
  19.9 2.1 %collective-permute-start.5 = (bf16[256,384]{1,0:T(8,128)(2,1)S(1)}, bf16[256,384]{1,0:T(8,128)(2,1)S(1)}, u32[]{:S(2)}, u32[]{:S(2)}) collective-permute-start(bf16[256,384]{1,0:T(8,128)(2,1)S(1)} %bitcast.37), channel_id=1, source_target_pairs={{0,20},{4,16},{8,28},{12,24},{16,4},{20,0},{24,12},{28,8},{1,21},{... | collective-permute-start | bytes 589832 | tf_op jit(solution)/shard_map/ppermute | solution.py:482
  21.9 0.6 select_add_fusion.dense_ref
  22.6 0.1 slice.47.dense_ref
  22.7 0.0 collective-permute-done.rest_0_
  22.7 4.6 %collective-permute-start.6 = (bf16[256,384]{1,0:T(8,128)(2,1)S(1)}, bf16[256,384]{1,0:T(8,128)(2,1)S(1)}, u32[]{:S(2)}, u32[]{:S(2)}) collective-permute-start(bf16[256,384]{1,0:T(8,128)(2,1)S(1)} %bitcast.36), channel_id=1, source_target_pairs={{0,16},{4,20},{8,24},{12,28},{16,0},{20,4},{24,8},{28,12},{1,17},{... | collective-permute-start | bytes 589832 | tf_op jit(solution)/shard_map/ppermute | solution.py:482
  27.4 0.9 %constant_dynamic-slice_fusion = (bf16[16,16,128]{2,1,0:T(8,128)(2,1)S(1)}, bf16[16,16,128]{2,1,0:T(8,128)(2,1)S(1)}) fusion(bf16[16,128,512]{2,1,0:T(8,128)(2,1)} %param.5, s32[]{:T(128)S(6)} %select_n.60, s32[]{:T(128)S(6)} %select_n.59), kind=kLoop, calls=%fused_computation.15 | loop fusion | bytes 262152 | tf_op jit(solution)/shard_map/dynamic_slice | solution.py:474
  28.3 4.8 %collective-permute-start.7 = (bf16[256,128]{1,0:T(8,128)(2,1)S(1)}, bf16[256,128]{1,0:T(8,128)(2,1)S(1)}, u32[]{:S(2)}, u32[]{:S(2)}) collective-permute-start(bf16[256,128]{1,0:T(8,128)(2,1)S(1)} %bitcast.39), channel_id=1, source_target_pairs={{0,20},{4,16},{8,28},{12,24},{16,4},{20,0},{24,12},{28,8},{1,21},{... | collective-permute-start | bytes 196616 | tf_op jit(solution)/shard_map/ppermute | solution.py:482
  33.1 12.1 %collective-permute-done.5.rest_0_ = bf16[256,384]{1,0:T(8,128)(2,1)S(1)} collective-permute-done((bf16[256,384]{1,0:T(8,128)(2,1)S(1)}, bf16[256,384]{1,0:T(8,128)(2,1)S(1)}, u32[]{:S(2)}, u32[]{:S(2)}) %collective-permute-start.5) | collective-permute-done | bytes 196640 | tf_op jit(solution)/shard_map/ppermute | solution.py:482
  45.1 0.0 collective-permute-start.8
  45.1 0.1 pad_add_fusion.ids_ref
  45.2 0.0 collective-permute-done.3.rest_3_
  45.2 0.0 collective-permute-done.4.rest_4_
  45.2 3.9 %shard_map.68 = (f32[4,2304,128]{2,1,0:T(8,128)S(1)}, f32[4,2304,128]{2,1,0:T(8,128)S(1)}, f32[64,128]{1,0:T(8,128)S(1)}) custom-call(s32[2]{0:T(128)S(1)} %pad_add_fusion.ids_ref, bf16[5,16,512]{2,1,0:T(8,128)(2,1)S(1)} %copy-done, bf16[16,64,512]{2,1,0:T(8,128)(2,1)S(1)} %select_add_fusion.dense_ref, bf16[256,512]{1,0:T(8,128)(2,1)S(1)} %collective-permute-done.rest_0_, ...), custom_call_target="tpu_custom_call" | custom-call | flops 16777216 | bytes 4194304 | tf_op jit(solution)/shard_map/pallas_call | solution.py:326
  49.1 1.6 %collective-permute-done.6.rest_1_ = bf16[256,384]{1,0:T(8,128)(2,1)S(1)} collective-permute-done((bf16[256,384]{1,0:T(8,128)(2,1)S(1)}, bf16[256,384]{1,0:T(8,128)(2,1)S(1)}, u32[]{:S(2)}, u32[]{:S(2)}) %collective-permute-start.6) | collective-permute-done | bytes 196640 | tf_op jit(solution)/shard_map/ppermute | solution.py:482
  50.7 1.6 %shard_map.69 = (f32[3,640,128]{2,1,0:T(8,128)S(1)}, f32[64,128]{1,0:T(8,128)S(1)}) custom-call(s32[2]{0:T(128)S(1)} %pad_add_fusion.ids_ref, bf16[5,16,384]{2,1,0:T(8,128)(2,1)S(1)} %slice.38.coeff_ref, bf16[16,64,384]{2,1,0:T(8,128)(2,1)S(1)} %slice.47.dense_ref, f32[64,128]{1,0:T(8,128)S(1)} %get-tuple-element.28.total_ref, ...), custom_call_target="tpu_custom_call" | custom-call | flops 12582912 | bytes 3145728 | tf_op jit(solution)/shard_map/pallas_call | solution.py:343
  52.3 0.3 collective-permute-done.8.rest_1_
  52.6 1.2 %shard_map.70 = (f32[1,640,128]{2,1,0:T(8,128)S(1)}, f32[16,128]{1,0:T(8,128)S(1)}, f32[16,128]{1,0:T(8,128)S(1)}, f32[16,128]{1,0:T(8,128)S(1)}, f32[16,128]{1,0:T(8,128)S(1)}) custom-call(s32[2]{0:T(128)S(1)} %pad_add_fusion.ids_ref, bf16[5,16,128]{2,1,0:T(8,128)(2,1)S(1)} %slice.30.coeff_ref, bf16[16,64,128]{2,1,0:T(8,128)(2,1)S(1)} %slice.46.dense_ref, ...), custom_call_target="tpu_custom_call" | custom-call | flops 4194304 | bytes 1048576 | tf_op jit(solution)/shard_map/pallas_call | solution.py:343
  53.8 0.4 collective-permute-start.11
  54.2 1.3 %collective-permute-start.10 = (f32[16,128]{1,0:T(8,128)S(1)}, f32[16,128]{1,0:T(8,128)S(1)}, u32[]{:S(2)}, u32[]{:S(2)}) collective-permute-start(f32[16,128]{1,0:T(8,128)S(1)} %get-tuple-element.42), channel_id=1, source_target_pairs={{0,2},{1,3},{2,0},{3,1},{4,6},{5,7},{6,4},{7,5},{8,10},{9,11},{10,... | collective-permute-start | bytes 24584 | tf_op jit(solution)/shard_map/ppermute | solution.py:525
  55.5 0.3 collective-permute-start.9
  55.8 2.4 %shard_map.71 = bf16[128,16,512]{2,1,0:T(8,128)(2,1)} custom-call(s32[2]{0:T(128)S(1)} %pad_add_fusion.ids_ref, f32[128]{0:T(128)S(1)} %convert_divide_fusion.inv_ref, f32[1,640,128]{2,1,0:T(8,128)S(1)} %get-tuple-element.37.rest_0_, f32[3,640,128]{2,1,0:T(8,128)S(1)} %get-tuple-element.38.rest_1_, f32[4,2304,128]{2,1,0:T(8,128)S(1)} %get-tuple-element.39.rest_2_), custom_call_target="tpu_custom_call" | custom-call | flops 16777216 | bytes 4194304 | tf_op jit(solution)/shard_map/pallas_call | solution.py:360
  58.3 0.6 %add_add_fusion = f32[16,128]{1,0:T(8,128)} fusion(f32[16,128]{1,0:T(8,128)S(1)} %collective-permute-done.11, f32[16,128]{1,0:T(8,128)S(1)} %collective-permute-done.10, f32[16,128]{1,0:T(8,128)S(1)} %get-tuple-element.40, f32[16,128]{1,0:T(8,128)S(1)} %collective-permute-done.9), kind=kLoop, calls=%fused_computation.6 | loop fusion | flops 6144 | bytes 40960 | tf_op jit(solution)/shard_map/add | solution.py:525
  (22 shorter events, 0.2 us)
Async XLA Ops:
  0.6 12.3 %copy-start.2 = (s32[64,3]{0,1:T(4,128)S(1)}, s32[64,3]{0,1:T(4,128)}, u32[]{:S(2)}) copy-start(s32[64,3]{0,1:T(4,128)} %param.8) | copy-start | bytes 2308
  0.6 12.3 %copy-start.1 = (bf16[16,3,512]{2,0,1:T(8,128)(2,1)S(1)}, bf16[16,3,512]{2,0,1:T(8,128)(2,1)}, u32[]{:S(2)}) copy-start(bf16[16,3,512]{2,0,1:T(8,128)(2,1)} %param.7) | copy-start | bytes 147460
  0.7 17.9 %copy-start.3 = (s32[64]{0:T(128)S(1)}, s32[64]{0:T(128)}, u32[]{:S(2)}) copy-start(s32[64]{0:T(128)} %param.9) | copy-start | bytes 772
  1.8 20.9 %collective-permute-start = (bf16[256,512]{1,0:T(8,128)(2,1)S(1)}, bf16[256,512]{1,0:T(8,128)(2,1)S(1)}, u32[]{:S(2)}, u32[]{:S(2)}) collective-permute-start(bf16[256,512]{1,0:T(8,128)(2,1)S(1)} %bitcast.32), channel_id=1, source_target_pairs={{0,28},{4,24},{8,20},{12,16},{16,12},{20,8},{24,4},{28,0},{1,29},{... | collective-permute-start | bytes 786440 | tf_op jit(solution)/shard_map/ppermute | solution.py:482
  7.8 20.4 %collective-permute-start.1 = (bf16[256,512]{1,0:T(8,128)(2,1)S(1)}, bf16[256,512]{1,0:T(8,128)(2,1)S(1)}, u32[]{:S(2)}, u32[]{:S(2)}) collective-permute-start(bf16[256,512]{1,0:T(8,128)(2,1)S(1)} %bitcast.31), channel_id=1, source_target_pairs={{0,24},{4,28},{8,16},{12,20},{16,8},{20,12},{24,0},{28,4},{1,25},{... | collective-permute-start | bytes 786440 | tf_op jit(solution)/shard_map/ppermute | solution.py:482
  8.0 14.5 %copy-start = (bf16[5,16,512]{2,1,0:T(8,128)(2,1)S(1)}, bf16[5,16,512]{2,1,0:T(8,128)(2,1)}, u32[]{:S(2)}) copy-start(bf16[5,16,512]{2,1,0:T(8,128)(2,1)} %coeff_ref.1) | copy-start | bytes 245764
  9.3 10.5 %collective-permute-start.2 = (bf16[256,512]{1,0:T(8,128)(2,1)S(1)}, bf16[256,512]{1,0:T(8,128)(2,1)S(1)}, u32[]{:S(2)}, u32[]{:S(2)}) collective-permute-start(bf16[256,512]{1,0:T(8,128)(2,1)S(1)} %bitcast.35), channel_id=1, source_target_pairs={{0,4},{4,0},{8,12},{12,8},{16,20},{20,16},{24,28},{28,24},{1,5},{5... | collective-permute-start | bytes 786440 | tf_op jit(solution)/shard_map/ppermute | solution.py:482
  9.8 35.4 %collective-permute-start.3 = (bf16[256,512]{1,0:T(8,128)(2,1)S(1)}, bf16[256,512]{1,0:T(8,128)(2,1)S(1)}, u32[]{:S(2)}, u32[]{:S(2)}) collective-permute-start(bf16[256,512]{1,0:T(8,128)(2,1)S(1)} %bitcast.34), channel_id=1, source_target_pairs={{0,8},{4,12},{8,0},{12,4},{16,24},{20,28},{24,16},{28,20},{1,9},{5... | collective-permute-start | bytes 786440 | tf_op jit(solution)/shard_map/ppermute | solution.py:482
  9.8 35.4 %collective-permute-start.4 = (bf16[256,512]{1,0:T(8,128)(2,1)S(1)}, bf16[256,512]{1,0:T(8,128)(2,1)S(1)}, u32[]{:S(2)}, u32[]{:S(2)}) collective-permute-start(bf16[256,512]{1,0:T(8,128)(2,1)S(1)} %bitcast.33), channel_id=1, source_target_pairs={{0,12},{4,8},{8,4},{12,0},{16,28},{20,24},{24,20},{28,16},{1,13},{... | collective-permute-start | bytes 786440 | tf_op jit(solution)/shard_map/ppermute | solution.py:482
  19.9 25.3 %collective-permute-start.5 = (bf16[256,384]{1,0:T(8,128)(2,1)S(1)}, bf16[256,384]{1,0:T(8,128)(2,1)S(1)}, u32[]{:S(2)}, u32[]{:S(2)}) collective-permute-start(bf16[256,384]{1,0:T(8,128)(2,1)S(1)} %bitcast.37), channel_id=1, source_target_pairs={{0,20},{4,16},{8,28},{12,24},{16,4},{20,0},{24,12},{28,8},{1,21},{... | collective-permute-start | bytes 589832 | tf_op jit(solution)/shard_map/ppermute | solution.py:482
  22.7 28.0 %collective-permute-start.6 = (bf16[256,384]{1,0:T(8,128)(2,1)S(1)}, bf16[256,384]{1,0:T(8,128)(2,1)S(1)}, u32[]{:S(2)}, u32[]{:S(2)}) collective-permute-start(bf16[256,384]{1,0:T(8,128)(2,1)S(1)} %bitcast.36), channel_id=1, source_target_pairs={{0,16},{4,20},{8,24},{12,28},{16,0},{20,4},{24,8},{28,12},{1,17},{... | collective-permute-start | bytes 589832 | tf_op jit(solution)/shard_map/ppermute | solution.py:482
  28.3 24.1 %collective-permute-start.7 = (bf16[256,128]{1,0:T(8,128)(2,1)S(1)}, bf16[256,128]{1,0:T(8,128)(2,1)S(1)}, u32[]{:S(2)}, u32[]{:S(2)}) collective-permute-start(bf16[256,128]{1,0:T(8,128)(2,1)S(1)} %bitcast.39), channel_id=1, source_target_pairs={{0,20},{4,16},{8,28},{12,24},{16,4},{20,0},{24,12},{28,8},{1,21},{... | collective-permute-start | bytes 196616 | tf_op jit(solution)/shard_map/ppermute | solution.py:482
  45.1 7.5 %collective-permute-start.8 = (bf16[256,128]{1,0:T(8,128)(2,1)S(1)}, bf16[256,128]{1,0:T(8,128)(2,1)S(1)}, u32[]{:S(2)}, u32[]{:S(2)}) collective-permute-start(bf16[256,128]{1,0:T(8,128)(2,1)S(1)} %bitcast.38), channel_id=1, source_target_pairs={{0,16},{4,20},{8,24},{12,28},{16,0},{20,4},{24,8},{28,12},{1,17},{... | collective-permute-start | bytes 196616 | tf_op jit(solution)/shard_map/ppermute | solution.py:482
  53.8 4.4 %collective-permute-start.11 = (f32[16,128]{1,0:T(8,128)S(1)}, f32[16,128]{1,0:T(8,128)S(1)}, u32[]{:S(2)}, u32[]{:S(2)}) collective-permute-start(f32[16,128]{1,0:T(8,128)S(1)} %get-tuple-element.43), channel_id=1, source_target_pairs={{0,3},{1,2},{2,1},{3,0},{4,7},{5,6},{6,5},{7,4},{8,11},{9,10},{10,... | collective-permute-start | bytes 24584 | tf_op jit(solution)/shard_map/ppermute | solution.py:525
  54.2 4.0 %collective-permute-start.10 = (f32[16,128]{1,0:T(8,128)S(1)}, f32[16,128]{1,0:T(8,128)S(1)}, u32[]{:S(2)}, u32[]{:S(2)}) collective-permute-start(f32[16,128]{1,0:T(8,128)S(1)} %get-tuple-element.42), channel_id=1, source_target_pairs={{0,2},{1,3},{2,0},{3,1},{4,6},{5,7},{6,4},{7,5},{8,10},{9,11},{10,... | collective-permute-start | bytes 24584 | tf_op jit(solution)/shard_map/ppermute | solution.py:525
  55.5 2.8 %collective-permute-start.9 = (f32[16,128]{1,0:T(8,128)S(1)}, f32[16,128]{1,0:T(8,128)S(1)}, u32[]{:S(2)}, u32[]{:S(2)}) collective-permute-start(f32[16,128]{1,0:T(8,128)S(1)} %get-tuple-element.41), channel_id=1, source_target_pairs={{0,1},{1,0},{2,3},{3,2},{4,5},{5,4},{6,7},{7,6},{8,9},{9,8},{10,11... | collective-permute-start | bytes 24584 | tf_op jit(solution)/shard_map/ppermute | solution.py:525

commit v7 on v6

--- a/solution.py
+++ b/solution.py
@@ -207,11 +207,11 @@
     return total - running / jnp.minimum(frame_ids + 1, BASE_WIN).astype(jnp.float32)
 
 
-def early_kernel(ids_ref, coeff_ref, dense_ref, *rest, places, step, frames, late):
+def early_kernel(coeff_ref, dense_ref, *rest, places, step, frames, late):
     blocks = rest[: len(places)]
     pixels, filtered, total_ref = rest[len(places) :]
     rows = coeff_ref.shape[1]
-    here = ids_ref[0]
+    here = lax.axis_index("tm")
     first, length = late_frames(here, late, step)
     at = pl.ds(pl.multiple_of(first * rows, step * rows), length * rows)
     zeros = jnp.zeros((length * rows, LANES), jnp.float32)
@@ -224,10 +224,10 @@
     total_ref[...] = project(filtered, dense_ref, 0, frames)
 
 
-def late_kernel(ids_ref, coeff_ref, dense_ref, total_ref, pixels, *rest, late, first_tile, last):
+def late_kernel(coeff_ref, dense_ref, total_ref, pixels, *rest, late, first_tile, last):
     blocks = rest[: len(late)]
     filtered, *outs, held, strip, partial = rest[len(late) :]
-    here, position = ids_ref[0], ids_ref[1]
+    here, position = lax.axis_index("tm"), lax.axis_index("roi")
     taps, rows, width = coeff_ref.shape
     step = blocks[0].shape[0] // rows
     frames = total_ref.shape[1]
@@ -270,39 +270,48 @@
         outs[0][...] = total
 
 
-def delta_kernel(ids_ref, inv_ref, *rest, late, step):
-    *pieces, filtered, out_ref, packed, sems = rest
-    pieces = pieces[::-1]
+def delta_kernel(*rest, late, step):
+    *pieces, filtered, out_ref, inv_ref, packed, sems = rest
     tiles, frames, rows, _ = packed.shape
-    first, length = late_frames(ids_ref[0], late, step)
-    places = [(piece, tile) for piece in pieces for tile in range(piece.shape[0])]
+    first, length = late_frames(lax.axis_index("tm"), late, step)
+    end = jnp.minimum(first + length, frames)
+    counts = lax.broadcasted_iota(jnp.int32, (frames, LANES), 0) + 1
+    inv_ref[...] = 1.0 / jnp.minimum(counts, BASE_WIN).astype(jnp.float32)
+    places = [(piece, tile) for piece in pieces[::-1] for tile in range(piece.shape[0])]
     copies = []
-    for tile, (piece, its_tile) in enumerate(places):
+    for tile in range(0, tiles, 2):
+        several = range(tile, min(tile + 2, tiles))
 
         def subtract_mean(source, low, high, running):
             def block_step(index, running):
+                running = list(running)
                 for offset in range(REACH):
                     frame = index * REACH + offset
-                    value = source(frame)
-                    running = running + value
-                    packed[tile, frame] = (value - running * inv_ref[frame]).astype(jnp.bfloat16)
-                return running
+                    for turn, one in enumerate(several):
+                        value = source(one, frame)
+                        running[turn] = running[turn] + value
+                        packed[one, frame] = (value - running[turn] * inv_ref[pl.ds(frame, 1), :]).astype(
+                            jnp.bfloat16
+                        )
+                return tuple(running)
 
             return lax.fori_loop(low // REACH, high // REACH, block_step, running)
 
-        def early(frame):
-            return filtered[tile, frame_rows(frame, rows), :]
-
-        def middle(frame):
+        def early(one, frame):
+            return filtered[one, frame_rows(frame, rows), :]
+
+        def middle(one, frame):
+            piece, its_tile = places[one]
             return piece[its_tile, frame_rows(frame - first, rows), :]
 
-        end = jnp.minimum(first + length, frames)
-        running = subtract_mean(early, 0, first, jnp.zeros((rows, LANES), jnp.float32))
+        zero = jnp.zeros((rows, LANES), jnp.float32)
+        running = subtract_mean(early, 0, first, (zero,) * len(several))
         running = subtract_mean(middle, first, end, running)
         subtract_mean(early, end, frames, running)
-        place = out_ref.at[:, :, pl.ds(tile * LANES, LANES)]
-        copies.append(pltpu.make_async_copy(packed.at[tile], place, sems.at[tile]))
-        copies[-1].start()
+        for one in several:
+            place = out_ref.at[:, :, pl.ds(one * LANES, LANES)]
+            copies.append(pltpu.make_async_copy(packed.at[one], place, sems.at[one]))
+            copies[-1].start()
     for copy in copies:
         copy.wait()
 
@@ -319,7 +328,7 @@
     )
 
 
-def run_early(ids, coeffs, dense, blocks, places, frames, late):
+def run_early(coeffs, dense, blocks, places, frames, late):
     _, rows, width = coeffs.shape
     step = blocks[0].shape[0] // rows
     held = jax.ShapeDtypeStruct((width // LANES, (frames + 2 * REACH) * rows, LANES), jnp.float32)
@@ -328,13 +337,13 @@
             early_kernel, places=tuple(places), step=step, frames=frames, late=tuple(late)
         ),
         out_shape=[held, held, jax.ShapeDtypeStruct((dense.shape[1], frames), jnp.float32)],
-        in_specs=[SMEM] + [VMEM] * (2 + len(blocks)),
+        in_specs=[VMEM] * (2 + len(blocks)),
         out_specs=[VMEM] * 3,
         **options(4, frames * rows * width),
-    )(ids, coeffs, dense, *blocks)
-
-
-def run_late(ids, coeffs, dense, total, pixels, late, owners, first_tile, last):
+    )(coeffs, dense, *blocks)
+
+
+def run_late(coeffs, dense, total, pixels, late, owners, first_tile, last):
     _, rows, width = coeffs.shape
     rois, frames = total.shape
     height = sum(block.shape[0] for block in late.values()) + REACH * rows
@@ -344,7 +353,7 @@
         functools.partial(late_kernel, late=tuple(late), first_tile=first_tile, last=last),
         out_shape=[jax.ShapeDtypeStruct((width // LANES, height, LANES), jnp.float32)]
         + [part] * parts,
-        in_specs=[SMEM] + [VMEM] * (4 + len(late)),
+        in_specs=[VMEM] * (4 + len(late)),
         out_specs=[VMEM] * (1 + parts),
         scratch_shapes=[
             pltpu.VMEM((height, LANES), jnp.float32),
@@ -352,22 +361,23 @@
             pltpu.VMEM((owners, rois // owners, frames), jnp.float32),
         ],
         **options(4, frames * rows * width),
-    )(ids, coeffs, dense, total, pixels, *late.values())
-
-
-def run_delta(ids, inverse, filtered, pieces, late, rows, step):
-    tiles, frames = filtered.shape[0], inverse.shape[0]
+    )(coeffs, dense, total, pixels, *late.values())
+
+
+def run_delta(filtered, pieces, late, rows, step):
+    tiles, frames = filtered.shape[0], filtered.shape[1] // rows - 2 * REACH
     return pl.pallas_call(
         functools.partial(delta_kernel, late=tuple(late), step=step),
         out_shape=jax.ShapeDtypeStruct((frames, rows, tiles * LANES), jnp.bfloat16),
-        in_specs=[SMEM, SMEM] + [VMEM] * (1 + len(pieces)),
+        in_specs=[VMEM] * (1 + len(pieces)),
         out_specs=ANYWHERE,
         scratch_shapes=[
+            pltpu.VMEM((frames, LANES), jnp.float32),
             pltpu.VMEM((tiles, frames, rows, LANES), jnp.bfloat16),
             pltpu.SemaphoreType.DMA((tiles,)),
         ],
         **options(4, frames * rows * tiles * LANES),
-    )(ids, inverse, *pieces[::-1], filtered)
+    )(*pieces[::-1], filtered)
 
 
 def swaps(count, k):
@@ -481,9 +491,10 @@
             block, *_ = lax.optimization_barrier((block, *after))
         return lax.ppermute(block, "tm", swaps(devices, k))
 
-    opening = [rows_of(movie, k) for k in early]
-    rest, *opening = lax.optimization_barrier((movie, *opening))
-    whole = {k: send(block, k) for block, k in zip(opening, early)}
+    opening = rows_of(movie, early[0])
+    rest, opening = lax.optimization_barrier((movie, opening))
+    whole = {early[0]: send(opening, early[0])}
+    whole |= {k: send(rows_of(rest, k), k) for k in early[1:]}
     whole |= {k: send(rows_of(rest, k), k) for k in near}
     ties = [whole[near[0]]] + [whole[k] for k in early]
     low = {k: send(rows_of(rest, k, 0, middle), k, tie) for k, tie in zip(late, ties)}
@@ -493,10 +504,9 @@
     dense = dense_of()
 
     pixels, filtered, total = run_early(
-        ids, coeffs, dense, list(whole.values()), list(whole), frames, late
+        coeffs, dense, list(whole.values()), list(whole), frames, late
     )
     lower, total = run_late(
-        ids,
         coeffs[:, :, :middle],
         dense[:, :, :middle],
         total,
@@ -510,7 +520,6 @@
         (pixels, filtered, lower, total)
     )
     upper, *parts = run_late(
-        ids,
         coeffs[:, :, middle:],
         dense[:, :, middle:],
         total,
@@ -523,7 +532,7 @@
     traces = parts[0]
     for k in range(1, owners):
         traces = traces + lax.ppermute(parts[k], "roi", swaps(owners, k))
-    delta = run_delta(ids, inverse, filtered, [lower, upper], late, rows, step)
+    delta = run_delta(filtered, [lower, upper], late, rows, step)
     return delta, traces
 
 

time: 59.1 us -> 58.1 us (0.983)
  Pallas kernels: 9.17 us -> 6.83 us
  starting transfers between devices: 23.3 us -> 24.1 us
  waiting for transfers between devices: 14.1 us -> 14.7 us
    pallas_call x2, Pallas kernels: 2.85 us -> 1.77 us  [run_late(): pl.pallas_call(functools.partial(late_kernel, late=tuple(late), first_til...]
    ppermute x9, starting transfers between devices: 21.4 us -> 22.1 us  [send(): return lax.ppermute(block, 'tm', swaps(devices, k))]
    pallas_call x1, Pallas kernels: 2.44 us -> 1.71 us  [run_delta(): pl.pallas_call(functools.partial(delta_kernel, late=tuple(late), step=ste...]
  transfers between devices with their start and end apart: 12 -> 12, of which waited for: 4 -> 5; matrix products, arithmetic and copies ran while one was open for 7% -> 7% of each run, Pallas kernels for 13% -> 11%
where the time goes in v7:
time: 58.1 us; the launch traced here: 57.8 us
  starting transfers between devices  24.1 us (41%)
  waiting for transfers between devices  14.7 us (25%)
  Pallas kernels  6.83 us (12%)
  blocking collectives  5.61 us (10%)
  local copies, waits for them, and re-layouts  4.54 us (8%)
  other arithmetic  1.21 us (2%)
  between operations  0.86 us (1%)
    ppermute x9, starting transfers between devices, send(): return lax.ppermute(block, 'tm', swaps(devices, k))  22.1 us
    ppermute x9, waiting for transfers between devices, send(): return lax.ppermute(block, 'tm', swaps(devices, k))  14.4 us
    all_gather x1, blocking collectives, dense_of(): gathered = lax.all_gather(footprint_w, 'roi', axis=0, tiled=True)  5.61 us
    dynamic_slice x4, local copies, waits for them, and re-layouts, rows_of(): lax.dynamic_slice(source, (0, (here ^ k) * rows, low), (step, rows, high...  4.35 us
    pallas_call x1, Pallas kernels, run_early(): pl.pallas_call(functools.partial(early_kernel, places=tuple(places), step...  3.35 us
    ppermute x3, starting transfers between devices, local(): traces = traces + lax.ppermute(parts[k], 'roi', swaps(owners, k))  1.93 us
    pallas_call x2, Pallas kernels, run_late(): pl.pallas_call(functools.partial(late_kernel, late=tuple(late), first_til...  1.77 us
    pallas_call x1, Pallas kernels, run_delta(): pl.pallas_call(functools.partial(delta_kernel, late=tuple(late), step=ste...  1.71 us
  transfers between devices with their start and end apart: 12, of which 5 were waited for; matrix products, arithmetic and copies ran while one was open for 7% of the time, Pallas kernels for 11%

profile of v7, /device:TPU:0, one launch (start us, length us, event | category | flops | bytes accessed | tf_op | source)
XLA Modules:
  0.0 57.8 jit_solution(11989007628838882366)
XLA Ops:
  0.7 1.0 %constant_dynamic-slice_fusion.9 = bf16[16,16,512]{2,1,0:T(8,128)(2,1)S(1)} fusion(bf16[16,128,512]{2,1,0:T(8,128)(2,1)} %param.5, s32[]{:T(128)S(6)} %select_n.53), kind=kLoop, calls=%fused_computation.24 | loop fusion | bytes 524292 | tf_op jit(solution)/shard_map/dynamic_slice | solution.py:484
  1.7 6.1 %collective-permute-start = (bf16[256,512]{1,0:T(8,128)(2,1)S(1)}, bf16[256,512]{1,0:T(8,128)(2,1)S(1)}, u32[]{:S(2)}, u32[]{:S(2)}) collective-permute-start(bf16[256,512]{1,0:T(8,128)(2,1)S(1)} %bitcast.33), channel_id=1, source_target_pairs={{0,28},{4,24},{8,20},{12,16},{16,12},{20,8},{24,4},{28,0},{1,29},{... | collective-permute-start | bytes 786440 | tf_op jit(solution)/shard_map/ppermute | solution.py:492
  7.7 1.4 %constant_dynamic-slice_fusion.4 = (bf16[16,16,512]{2,1,0:T(8,128)(2,1)S(1)}, bf16[16,16,512]{2,1,0:T(8,128)(2,1)S(1)}, bf16[16,16,512]{2,1,0:T(8,128)(2,1)S(1)}...) fusion(bf16[16,128,512]{2,1,0:T(8,128)(2,1)} %param.5, s32[]{:T(128)S(6)} %select_n.58, s32[]{:T(128)S(6)} %select_n.57, ...), kind=kLoop, calls=%fused_computation.19 | loop fusion | bytes 2621460 | tf_op jit(solution)/shard_map/dynamic_slice | solution.py:484
  9.1 0.0 copy-start
  9.2 0.3 collective-permute-start.1
  9.4 0.4 collective-permute-start.2
  9.8 3.1 %collective-permute-start.4 = (bf16[256,512]{1,0:T(8,128)(2,1)S(1)}, bf16[256,512]{1,0:T(8,128)(2,1)S(1)}, u32[]{:S(2)}, u32[]{:S(2)}) collective-permute-start(bf16[256,512]{1,0:T(8,128)(2,1)S(1)} %bitcast.29), channel_id=1, source_target_pairs={{0,12},{4,8},{8,4},{12,0},{16,28},{20,24},{24,20},{28,16},{1,13},{... | collective-permute-start | bytes 786440 | tf_op jit(solution)/shard_map/ppermute | solution.py:492
  13.0 1.1 %constant_dynamic-slice_fusion.2 = (bf16[16,16,384]{2,1,0:T(8,128)(2,1)S(1)}, bf16[16,16,384]{2,1,0:T(8,128)(2,1)S(1)}) fusion(bf16[16,128,512]{2,1,0:T(8,128)(2,1)} %param.5, s32[]{:T(128)S(6)} %select_n.60, s32[]{:T(128)S(6)} %select_n.59), kind=kLoop, calls=%fused_computation.17 | loop fusion | bytes 786440 | tf_op jit(solution)/shard_map/dynamic_slice | solution.py:484
  14.1 5.6 %all_gather.3 = bf16[64,3,512]{2,0,1:T(8,128)(2,1)S(1)} all-gather(bf16[16,3,512]{2,0,1:T(8,128)(2,1)S(1)} %copy-done.1), channel_id=1, replica_groups=mesh['tm'=8,'roi'=4] {'roi'}, dimensions={0}, use_global_device_ids=true | all-gather | bytes 245760 | tf_op jit(solution)/shard_map/all_gather | solution.py:464
  19.7 0.0 collective-permute-done.2.rest_2_
  19.8 2.2 %collective-permute-start.5 = (bf16[256,384]{1,0:T(8,128)(2,1)S(1)}, bf16[256,384]{1,0:T(8,128)(2,1)S(1)}, u32[]{:S(2)}, u32[]{:S(2)}) collective-permute-start(bf16[256,384]{1,0:T(8,128)(2,1)S(1)} %bitcast.35), channel_id=1, source_target_pairs={{0,20},{4,16},{8,28},{12,24},{16,4},{20,0},{24,12},{28,8},{1,21},{... | collective-permute-start | bytes 589832 | tf_op jit(solution)/shard_map/ppermute | solution.py:492
  21.9 0.9 %constant_dynamic-slice_fusion = (bf16[16,16,128]{2,1,0:T(8,128)(2,1)S(1)}, bf16[16,16,128]{2,1,0:T(8,128)(2,1)S(1)}) fusion(bf16[16,128,512]{2,1,0:T(8,128)(2,1)} %param.5, s32[]{:T(128)S(6)} %select_n.60, s32[]{:T(128)S(6)} %select_n.59), kind=kLoop, calls=%fused_computation.15 | loop fusion | bytes 262152 | tf_op jit(solution)/shard_map/dynamic_slice | solution.py:484
  22.8 4.4 %collective-permute-start.6 = (bf16[256,384]{1,0:T(8,128)(2,1)S(1)}, bf16[256,384]{1,0:T(8,128)(2,1)S(1)}, u32[]{:S(2)}, u32[]{:S(2)}) collective-permute-start(bf16[256,384]{1,0:T(8,128)(2,1)S(1)} %bitcast.34), channel_id=1, source_target_pairs={{0,16},{4,20},{8,24},{12,28},{16,0},{20,4},{24,8},{28,12},{1,17},{... | collective-permute-start | bytes 589832 | tf_op jit(solution)/shard_map/ppermute | solution.py:492
  27.3 0.0 collective-permute-done.1.rest_1_
  27.3 5.7 %collective-permute-start.7 = (bf16[256,128]{1,0:T(8,128)(2,1)S(1)}, bf16[256,128]{1,0:T(8,128)(2,1)S(1)}, u32[]{:S(2)}, u32[]{:S(2)}) collective-permute-start(bf16[256,128]{1,0:T(8,128)(2,1)S(1)} %bitcast.37), channel_id=1, source_target_pairs={{0,20},{4,16},{8,28},{12,24},{16,4},{20,0},{24,12},{28,8},{1,21},{... | collective-permute-start | bytes 196616 | tf_op jit(solution)/shard_map/ppermute | solution.py:492
  33.0 12.1 %collective-permute-done.5.rest_0_ = bf16[256,384]{1,0:T(8,128)(2,1)S(1)} collective-permute-done((bf16[256,384]{1,0:T(8,128)(2,1)S(1)}, bf16[256,384]{1,0:T(8,128)(2,1)S(1)}, u32[]{:S(2)}, u32[]{:S(2)}) %collective-permute-start.5) | collective-permute-done | bytes 196640 | tf_op jit(solution)/shard_map/ppermute | solution.py:492
  45.0 0.6 select_add_fusion.dense_ref
  45.7 0.1 slice.47.dense_ref
  45.8 0.0 collective-permute-done.4.rest_4_
  45.8 3.4 %shard_map.68 = (f32[4,2304,128]{2,1,0:T(8,128)S(1)}, f32[4,2304,128]{2,1,0:T(8,128)S(1)}, f32[64,128]{1,0:T(8,128)S(1)}) custom-call(bf16[5,16,512]{2,1,0:T(8,128)(2,1)S(1)} %copy-done, bf16[16,64,512]{2,1,0:T(8,128)(2,1)S(1)} %select_add_fusion.dense_ref, bf16[256,512]{1,0:T(8,128)(2,1)S(1)} %collective-permute-done.rest_0_, ...), custom_call_target="tpu_custom_call" | custom-call | flops 16777216 | bytes 4194304 | tf_op jit(solution)/shard_map/pallas_call | solution.py:335
  49.2 1.4 %collective-permute-done.6.rest_1_ = bf16[256,384]{1,0:T(8,128)(2,1)S(1)} collective-permute-done((bf16[256,384]{1,0:T(8,128)(2,1)S(1)}, bf16[256,384]{1,0:T(8,128)(2,1)S(1)}, u32[]{:S(2)}, u32[]{:S(2)}) %collective-permute-start.6) | collective-permute-done | bytes 196640 | tf_op jit(solution)/shard_map/ppermute | solution.py:492
  50.6 1.1 %shard_map.69 = (f32[3,640,128]{2,1,0:T(8,128)S(1)}, f32[64,128]{1,0:T(8,128)S(1)}) custom-call(bf16[5,16,384]{2,1,0:T(8,128)(2,1)S(1)} %slice.38.coeff_ref, bf16[16,64,384]{2,1,0:T(8,128)(2,1)S(1)} %slice.47.dense_ref, f32[64,128]{1,0:T(8,128)S(1)} %get-tuple-element.26.total_ref, f32[4,2304,128]{2,1,0:T(8,128)S(1)} %get-tuple-element.32.pixels, ...), custom_call_target="tpu_custom_call" | custom-call | flops 12582912 | bytes 3145728 | tf_op jit(solution)/shard_map/pallas_call | solution.py:352
  51.7 0.1 collective-permute-done.7.rest_0_
  51.7 0.8 %collective-permute-done.8.rest_1_ = bf16[256,128]{1,0:T(8,128)(2,1)S(1)} collective-permute-done((bf16[256,128]{1,0:T(8,128)(2,1)S(1)}, bf16[256,128]{1,0:T(8,128)(2,1)S(1)}, u32[]{:S(2)}, u32[]{:S(2)}) %collective-permute-start.8) | collective-permute-done | bytes 65568 | tf_op jit(solution)/shard_map/ppermute | solution.py:492
  52.5 0.7 %shard_map.70 = (f32[1,640,128]{2,1,0:T(8,128)S(1)}, f32[16,128]{1,0:T(8,128)S(1)}, f32[16,128]{1,0:T(8,128)S(1)}, f32[16,128]{1,0:T(8,128)S(1)}, f32[16,128]{1,0:T(8,128)S(1)}) custom-call(bf16[5,16,128]{2,1,0:T(8,128)(2,1)S(1)} %slice.30.coeff_ref, bf16[16,64,128]{2,1,0:T(8,128)(2,1)S(1)} %slice.46.dense_ref, f32[64,128]{1,0:T(8,128)S(1)} %get-tuple-element.31.total_ref, ...), custom_call_target="tpu_custom_call" | custom-call | flops 4194304 | bytes 1048576 | tf_op jit(solution)/shard_map/pallas_call | solution.py:352
  53.2 0.4 collective-permute-start.11
  53.6 1.3 %collective-permute-start.10 = (f32[16,128]{1,0:T(8,128)S(1)}, f32[16,128]{1,0:T(8,128)S(1)}, u32[]{:S(2)}, u32[]{:S(2)}) collective-permute-start(f32[16,128]{1,0:T(8,128)S(1)} %get-tuple-element.40), channel_id=1, source_target_pairs={{0,2},{1,3},{2,0},{3,1},{4,6},{5,7},{6,4},{7,5},{8,10},{9,11},{10,... | collective-permute-start | bytes 24584 | tf_op jit(solution)/shard_map/ppermute | solution.py:534
  54.8 0.3 collective-permute-start.9
  55.1 1.7 %shard_map.71 = bf16[128,16,512]{2,1,0:T(8,128)(2,1)} custom-call(f32[1,640,128]{2,1,0:T(8,128)S(1)} %get-tuple-element.35.rest_0_, f32[3,640,128]{2,1,0:T(8,128)S(1)} %get-tuple-element.36.rest_1_, f32[4,2304,128]{2,1,0:T(8,128)S(1)} %get-tuple-element.37.rest_2_), custom_call_target="tpu_custom_call" | custom-call | flops 16777216 | bytes 4194304 | tf_op jit(solution)/shard_map/pallas_call | solution.py:369
  56.9 0.0 collective-permute-done.11
  56.9 0.4 collective-permute-done.10
  57.2 0.6 %add_add_fusion = f32[16,128]{1,0:T(8,128)} fusion(f32[16,128]{1,0:T(8,128)S(1)} %collective-permute-done.11, f32[16,128]{1,0:T(8,128)S(1)} %collective-permute-done.10, f32[16,128]{1,0:T(8,128)S(1)} %get-tuple-element.38, f32[16,128]{1,0:T(8,128)S(1)} %collective-permute-done.9), kind=kLoop, calls=%fused_computation.6 | loop fusion | flops 6144 | bytes 40960 | tf_op jit(solution)/shard_map/add | solution.py:534
  (20 shorter events, 0.1 us)
Async XLA Ops:
  0.6 12.3 %copy-start.2 = (s32[64,3]{0,1:T(4,128)S(1)}, s32[64,3]{0,1:T(4,128)}, u32[]{:S(2)}) copy-start(s32[64,3]{0,1:T(4,128)} %param.8) | copy-start | bytes 2308
  0.6 12.3 %copy-start.3 = (s32[64]{0:T(128)S(1)}, s32[64]{0:T(128)}, u32[]{:S(2)}) copy-start(s32[64]{0:T(128)} %param.9) | copy-start | bytes 772
  0.7 13.4 %copy-start.1 = (bf16[16,3,512]{2,0,1:T(8,128)(2,1)S(1)}, bf16[16,3,512]{2,0,1:T(8,128)(2,1)}, u32[]{:S(2)}) copy-start(bf16[16,3,512]{2,0,1:T(8,128)(2,1)} %param.7) | copy-start | bytes 147460
  1.7 21.2 %collective-permute-start = (bf16[256,512]{1,0:T(8,128)(2,1)S(1)}, bf16[256,512]{1,0:T(8,128)(2,1)S(1)}, u32[]{:S(2)}, u32[]{:S(2)}) collective-permute-start(bf16[256,512]{1,0:T(8,128)(2,1)S(1)} %bitcast.33), channel_id=1, source_target_pairs={{0,28},{4,24},{8,20},{12,16},{16,12},{20,8},{24,4},{28,0},{1,29},{... | collective-permute-start | bytes 786440 | tf_op jit(solution)/shard_map/ppermute | solution.py:492
  9.1 36.5 %copy-start = (bf16[5,16,512]{2,1,0:T(8,128)(2,1)S(1)}, bf16[5,16,512]{2,1,0:T(8,128)(2,1)}, u32[]{:S(2)}) copy-start(bf16[5,16,512]{2,1,0:T(8,128)(2,1)} %coeff_ref.1) | copy-start | bytes 245764
  9.2 18.1 %collective-permute-start.1 = (bf16[256,512]{1,0:T(8,128)(2,1)S(1)}, bf16[256,512]{1,0:T(8,128)(2,1)S(1)}, u32[]{:S(2)}, u32[]{:S(2)}) collective-permute-start(bf16[256,512]{1,0:T(8,128)(2,1)S(1)} %bitcast.31), channel_id=1, source_target_pairs={{0,24},{4,28},{8,16},{12,20},{16,8},{20,12},{24,0},{28,4},{1,25},{... | collective-permute-start | bytes 786440 | tf_op jit(solution)/shard_map/ppermute | solution.py:492
  9.4 10.3 %collective-permute-start.2 = (bf16[256,512]{1,0:T(8,128)(2,1)S(1)}, bf16[256,512]{1,0:T(8,128)(2,1)S(1)}, u32[]{:S(2)}, u32[]{:S(2)}) collective-permute-start(bf16[256,512]{1,0:T(8,128)(2,1)S(1)} %bitcast.32), channel_id=1, source_target_pairs={{0,4},{4,0},{8,12},{12,8},{16,20},{20,16},{24,28},{28,24},{1,5},{5... | collective-permute-start | bytes 786440 | tf_op jit(solution)/shard_map/ppermute | solution.py:492
  9.8 36.0 %collective-permute-start.3 = (bf16[256,512]{1,0:T(8,128)(2,1)S(1)}, bf16[256,512]{1,0:T(8,128)(2,1)S(1)}, u32[]{:S(2)}, u32[]{:S(2)}) collective-permute-start(bf16[256,512]{1,0:T(8,128)(2,1)S(1)} %bitcast.30), channel_id=1, source_target_pairs={{0,8},{4,12},{8,0},{12,4},{16,24},{20,28},{24,16},{28,20},{1,9},{5... | collective-permute-start | bytes 786440 | tf_op jit(solution)/shard_map/ppermute | solution.py:492
  9.8 36.0 %collective-permute-start.4 = (bf16[256,512]{1,0:T(8,128)(2,1)S(1)}, bf16[256,512]{1,0:T(8,128)(2,1)S(1)}, u32[]{:S(2)}, u32[]{:S(2)}) collective-permute-start(bf16[256,512]{1,0:T(8,128)(2,1)S(1)} %bitcast.29), channel_id=1, source_target_pairs={{0,12},{4,8},{8,4},{12,0},{16,28},{20,24},{24,20},{28,16},{1,13},{... | collective-permute-start | bytes 786440 | tf_op jit(solution)/shard_map/ppermute | solution.py:492
  19.8 25.3 %collective-permute-start.5 = (bf16[256,384]{1,0:T(8,128)(2,1)S(1)}, bf16[256,384]{1,0:T(8,128)(2,1)S(1)}, u32[]{:S(2)}, u32[]{:S(2)}) collective-permute-start(bf16[256,384]{1,0:T(8,128)(2,1)S(1)} %bitcast.35), channel_id=1, source_target_pairs={{0,20},{4,16},{8,28},{12,24},{16,4},{20,0},{24,12},{28,8},{1,21},{... | collective-permute-start | bytes 589832 | tf_op jit(solution)/shard_map/ppermute | solution.py:492
  22.8 27.8 %collective-permute-start.6 = (bf16[256,384]{1,0:T(8,128)(2,1)S(1)}, bf16[256,384]{1,0:T(8,128)(2,1)S(1)}, u32[]{:S(2)}, u32[]{:S(2)}) collective-permute-start(bf16[256,384]{1,0:T(8,128)(2,1)S(1)} %bitcast.34), channel_id=1, source_target_pairs={{0,16},{4,20},{8,24},{12,28},{16,0},{20,4},{24,8},{28,12},{1,17},{... | collective-permute-start | bytes 589832 | tf_op jit(solution)/shard_map/ppermute | solution.py:492
  27.3 24.5 %collective-permute-start.7 = (bf16[256,128]{1,0:T(8,128)(2,1)S(1)}, bf16[256,128]{1,0:T(8,128)(2,1)S(1)}, u32[]{:S(2)}, u32[]{:S(2)}) collective-permute-start(bf16[256,128]{1,0:T(8,128)(2,1)S(1)} %bitcast.37), channel_id=1, source_target_pairs={{0,20},{4,16},{8,28},{12,24},{16,4},{20,0},{24,12},{28,8},{1,21},{... | collective-permute-start | bytes 196616 | tf_op jit(solution)/shard_map/ppermute | solution.py:492
  45.0 7.5 %collective-permute-start.8 = (bf16[256,128]{1,0:T(8,128)(2,1)S(1)}, bf16[256,128]{1,0:T(8,128)(2,1)S(1)}, u32[]{:S(2)}, u32[]{:S(2)}) collective-permute-start(bf16[256,128]{1,0:T(8,128)(2,1)S(1)} %bitcast.36), channel_id=1, source_target_pairs={{0,16},{4,20},{8,24},{12,28},{16,0},{20,4},{24,8},{28,12},{1,17},{... | collective-permute-start | bytes 196616 | tf_op jit(solution)/shard_map/ppermute | solution.py:492
  53.2 3.6 %collective-permute-start.11 = (f32[16,128]{1,0:T(8,128)S(1)}, f32[16,128]{1,0:T(8,128)S(1)}, u32[]{:S(2)}, u32[]{:S(2)}) collective-permute-start(f32[16,128]{1,0:T(8,128)S(1)} %get-tuple-element.41), channel_id=1, source_target_pairs={{0,3},{1,2},{2,1},{3,0},{4,7},{5,6},{6,5},{7,4},{8,11},{9,10},{10,... | collective-permute-start | bytes 24584 | tf_op jit(solution)/shard_map/ppermute | solution.py:534
  53.6 3.7 %collective-permute-start.10 = (f32[16,128]{1,0:T(8,128)S(1)}, f32[16,128]{1,0:T(8,128)S(1)}, u32[]{:S(2)}, u32[]{:S(2)}) collective-permute-start(f32[16,128]{1,0:T(8,128)S(1)} %get-tuple-element.40), channel_id=1, source_target_pairs={{0,2},{1,3},{2,0},{3,1},{4,6},{5,7},{6,4},{7,5},{8,10},{9,11},{10,... | collective-permute-start | bytes 24584 | tf_op jit(solution)/shard_map/ppermute | solution.py:534
  54.8 2.4 %collective-permute-start.9 = (f32[16,128]{1,0:T(8,128)S(1)}, f32[16,128]{1,0:T(8,128)S(1)}, u32[]{:S(2)}, u32[]{:S(2)}) collective-permute-start(f32[16,128]{1,0:T(8,128)S(1)} %get-tuple-element.39), channel_id=1, source_target_pairs={{0,1},{1,0},{2,3},{3,2},{4,5},{5,4},{6,7},{7,6},{8,9},{9,8},{10,11... | collective-permute-start | bytes 24584 | tf_op jit(solution)/shard_map/ppermute | solution.py:534

commit v8 on v7

--- a/solution.py
+++ b/solution.py
@@ -106,7 +106,7 @@
         scratch_shapes=[
             pltpu.VMEM((frames, rows, width), jnp.bfloat16),
             pltpu.VMEM((held, rows, width), jnp.bfloat16),
-            pltpu.VMEM((width // LANES, frames * rows, LANES), jnp.float32),
+            pltpu.VMEM((width // LANES, (frames + 1) * rows, LANES), jnp.float32),
             pltpu.VMEM((owners, rois // owners, frames), jnp.float32),
         ],
         compiler_params=pltpu.CompilerParams(vmem_limit_bytes=24 * 1024 * 1024),
@@ -240,7 +240,7 @@
                 :, tile * LANES : (tile + 1) * LANES
             ].astype(jnp.float32)
         after = pl.multiple_of((first + length - REACH) * rows, step * rows)
-        held[(length - REACH) * rows :, :] = own[pl.ds(after, REACH * rows), :]
+        held[pl.ds((length - REACH) * rows, REACH * rows), :] = own[pl.ds(after, REACH * rows), :]
         weights = tap_weights(coeff_ref, tile)
         history = []
         for tap in range(1, taps):
@@ -346,7 +346,7 @@
 def run_late(coeffs, dense, total, pixels, late, owners, first_tile, last):
     _, rows, width = coeffs.shape
     rois, frames = total.shape
-    height = sum(block.shape[0] for block in late.values()) + REACH * rows
+    height = sum(block.shape[0] for block in late.values()) + (REACH + 1) * rows
     parts = owners if last else 1
     part = jax.ShapeDtypeStruct((rois // parts, frames), jnp.float32)
     return pl.pallas_call(

time: 58.1 us -> 58.1 us (level)
  no operation moved by 1% of the time
where the time goes in v8:
time: 58.1 us; the launch traced here: 57.8 us
  starting transfers between devices  24.1 us (41%)
  waiting for transfers between devices  14.7 us (25%)
  Pallas kernels  6.83 us (12%)
  blocking collectives  5.61 us (10%)
  local copies, waits for them, and re-layouts  4.54 us (8%)
  other arithmetic  1.21 us (2%)
  between operations  0.86 us (1%)
    ppermute x9, starting transfers between devices, send(): return lax.ppermute(block, 'tm', swaps(devices, k))  22.1 us
    ppermute x9, waiting for transfers between devices, send(): return lax.ppermute(block, 'tm', swaps(devices, k))  14.4 us
    all_gather x1, blocking collectives, dense_of(): gathered = lax.all_gather(footprint_w, 'roi', axis=0, tiled=True)  5.61 us
    dynamic_slice x4, local copies, waits for them, and re-layouts, rows_of(): lax.dynamic_slice(source, (0, (here ^ k) * rows, low), (step, rows, high...  4.35 us
    pallas_call x1, Pallas kernels, run_early(): pl.pallas_call(functools.partial(early_kernel, places=tuple(places), step...  3.35 us
    ppermute x3, starting transfers between devices, local(): traces = traces + lax.ppermute(parts[k], 'roi', swaps(owners, k))  1.93 us
    pallas_call x2, Pallas kernels, run_late(): pl.pallas_call(functools.partial(late_kernel, late=tuple(late), first_til...  1.77 us
    pallas_call x1, Pallas kernels, run_delta(): pl.pallas_call(functools.partial(delta_kernel, late=tuple(late), step=ste...  1.71 us
  transfers between devices with their start and end apart: 12, of which 5 were waited for; matrix products, arithmetic and copies ran while one was open for 7% of the time, Pallas kernels for 11%

profile of v8, /device:TPU:0, one launch (start us, length us, event | category | flops | bytes accessed | tf_op | source)
XLA Modules:
  0.0 57.8 jit_solution(11442345583475117199)
XLA Ops:
  0.7 1.0 %constant_dynamic-slice_fusion.9 = bf16[16,16,512]{2,1,0:T(8,128)(2,1)S(1)} fusion(bf16[16,128,512]{2,1,0:T(8,128)(2,1)} %param.5, s32[]{:T(128)S(6)} %select_n.53), kind=kLoop, calls=%fused_computation.24 | loop fusion | bytes 524292 | tf_op jit(solution)/shard_map/dynamic_slice | solution.py:484
  1.7 6.1 %collective-permute-start = (bf16[256,512]{1,0:T(8,128)(2,1)S(1)}, bf16[256,512]{1,0:T(8,128)(2,1)S(1)}, u32[]{:S(2)}, u32[]{:S(2)}) collective-permute-start(bf16[256,512]{1,0:T(8,128)(2,1)S(1)} %bitcast.33), channel_id=1, source_target_pairs={{0,28},{4,24},{8,20},{12,16},{16,12},{20,8},{24,4},{28,0},{1,29},{... | collective-permute-start | bytes 786440 | tf_op jit(solution)/shard_map/ppermute | solution.py:492
  7.7 1.4 %constant_dynamic-slice_fusion.4 = (bf16[16,16,512]{2,1,0:T(8,128)(2,1)S(1)}, bf16[16,16,512]{2,1,0:T(8,128)(2,1)S(1)}, bf16[16,16,512]{2,1,0:T(8,128)(2,1)S(1)}...) fusion(bf16[16,128,512]{2,1,0:T(8,128)(2,1)} %param.5, s32[]{:T(128)S(6)} %select_n.58, s32[]{:T(128)S(6)} %select_n.57, ...), kind=kLoop, calls=%fused_computation.19 | loop fusion | bytes 2621460 | tf_op jit(solution)/shard_map/dynamic_slice | solution.py:484
  9.1 0.0 copy-start
  9.2 0.3 collective-permute-start.1
  9.4 0.4 collective-permute-start.2
  9.8 3.1 %collective-permute-start.4 = (bf16[256,512]{1,0:T(8,128)(2,1)S(1)}, bf16[256,512]{1,0:T(8,128)(2,1)S(1)}, u32[]{:S(2)}, u32[]{:S(2)}) collective-permute-start(bf16[256,512]{1,0:T(8,128)(2,1)S(1)} %bitcast.29), channel_id=1, source_target_pairs={{0,12},{4,8},{8,4},{12,0},{16,28},{20,24},{24,20},{28,16},{1,13},{... | collective-permute-start | bytes 786440 | tf_op jit(solution)/shard_map/ppermute | solution.py:492
  13.0 1.1 %constant_dynamic-slice_fusion.2 = (bf16[16,16,384]{2,1,0:T(8,128)(2,1)S(1)}, bf16[16,16,384]{2,1,0:T(8,128)(2,1)S(1)}) fusion(bf16[16,128,512]{2,1,0:T(8,128)(2,1)} %param.5, s32[]{:T(128)S(6)} %select_n.60, s32[]{:T(128)S(6)} %select_n.59), kind=kLoop, calls=%fused_computation.17 | loop fusion | bytes 786440 | tf_op jit(solution)/shard_map/dynamic_slice | solution.py:484
  14.1 5.6 %all_gather.3 = bf16[64,3,512]{2,0,1:T(8,128)(2,1)S(1)} all-gather(bf16[16,3,512]{2,0,1:T(8,128)(2,1)S(1)} %copy-done.1), channel_id=1, replica_groups=mesh['tm'=8,'roi'=4] {'roi'}, dimensions={0}, use_global_device_ids=true | all-gather | bytes 245760 | tf_op jit(solution)/shard_map/all_gather | solution.py:464
  19.7 0.0 collective-permute-done.2.rest_2_
  19.8 2.2 %collective-permute-start.5 = (bf16[256,384]{1,0:T(8,128)(2,1)S(1)}, bf16[256,384]{1,0:T(8,128)(2,1)S(1)}, u32[]{:S(2)}, u32[]{:S(2)}) collective-permute-start(bf16[256,384]{1,0:T(8,128)(2,1)S(1)} %bitcast.35), channel_id=1, source_target_pairs={{0,20},{4,16},{8,28},{12,24},{16,4},{20,0},{24,12},{28,8},{1,21},{... | collective-permute-start | bytes 589832 | tf_op jit(solution)/shard_map/ppermute | solution.py:492
  21.9 0.9 %constant_dynamic-slice_fusion = (bf16[16,16,128]{2,1,0:T(8,128)(2,1)S(1)}, bf16[16,16,128]{2,1,0:T(8,128)(2,1)S(1)}) fusion(bf16[16,128,512]{2,1,0:T(8,128)(2,1)} %param.5, s32[]{:T(128)S(6)} %select_n.60, s32[]{:T(128)S(6)} %select_n.59), kind=kLoop, calls=%fused_computation.15 | loop fusion | bytes 262152 | tf_op jit(solution)/shard_map/dynamic_slice | solution.py:484
  22.8 4.4 %collective-permute-start.6 = (bf16[256,384]{1,0:T(8,128)(2,1)S(1)}, bf16[256,384]{1,0:T(8,128)(2,1)S(1)}, u32[]{:S(2)}, u32[]{:S(2)}) collective-permute-start(bf16[256,384]{1,0:T(8,128)(2,1)S(1)} %bitcast.34), channel_id=1, source_target_pairs={{0,16},{4,20},{8,24},{12,28},{16,0},{20,4},{24,8},{28,12},{1,17},{... | collective-permute-start | bytes 589832 | tf_op jit(solution)/shard_map/ppermute | solution.py:492
  27.3 0.0 collective-permute-done.1.rest_1_
  27.3 5.7 %collective-permute-start.7 = (bf16[256,128]{1,0:T(8,128)(2,1)S(1)}, bf16[256,128]{1,0:T(8,128)(2,1)S(1)}, u32[]{:S(2)}, u32[]{:S(2)}) collective-permute-start(bf16[256,128]{1,0:T(8,128)(2,1)S(1)} %bitcast.37), channel_id=1, source_target_pairs={{0,20},{4,16},{8,28},{12,24},{16,4},{20,0},{24,12},{28,8},{1,21},{... | collective-permute-start | bytes 196616 | tf_op jit(solution)/shard_map/ppermute | solution.py:492
  33.0 12.1 %collective-permute-done.5.rest_0_ = bf16[256,384]{1,0:T(8,128)(2,1)S(1)} collective-permute-done((bf16[256,384]{1,0:T(8,128)(2,1)S(1)}, bf16[256,384]{1,0:T(8,128)(2,1)S(1)}, u32[]{:S(2)}, u32[]{:S(2)}) %collective-permute-start.5) | collective-permute-done | bytes 196640 | tf_op jit(solution)/shard_map/ppermute | solution.py:492
  45.0 0.6 select_add_fusion.dense_ref
  45.7 0.1 slice.47.dense_ref
  45.8 0.0 collective-permute-done.4.rest_4_
  45.8 3.4 %shard_map.68 = (f32[4,2304,128]{2,1,0:T(8,128)S(1)}, f32[4,2304,128]{2,1,0:T(8,128)S(1)}, f32[64,128]{1,0:T(8,128)S(1)}) custom-call(bf16[5,16,512]{2,1,0:T(8,128)(2,1)S(1)} %copy-done, bf16[16,64,512]{2,1,0:T(8,128)(2,1)S(1)} %select_add_fusion.dense_ref, bf16[256,512]{1,0:T(8,128)(2,1)S(1)} %collective-permute-done.rest_0_, ...), custom_call_target="tpu_custom_call" | custom-call | flops 16777216 | bytes 4194304 | tf_op jit(solution)/shard_map/pallas_call | solution.py:335
  49.2 1.4 %collective-permute-done.6.rest_1_ = bf16[256,384]{1,0:T(8,128)(2,1)S(1)} collective-permute-done((bf16[256,384]{1,0:T(8,128)(2,1)S(1)}, bf16[256,384]{1,0:T(8,128)(2,1)S(1)}, u32[]{:S(2)}, u32[]{:S(2)}) %collective-permute-start.6) | collective-permute-done | bytes 196640 | tf_op jit(solution)/shard_map/ppermute | solution.py:492
  50.6 1.1 %shard_map.69 = (f32[3,656,128]{2,1,0:T(8,128)S(1)}, f32[64,128]{1,0:T(8,128)S(1)}) custom-call(bf16[5,16,384]{2,1,0:T(8,128)(2,1)S(1)} %slice.38.coeff_ref, bf16[16,64,384]{2,1,0:T(8,128)(2,1)S(1)} %slice.47.dense_ref, f32[64,128]{1,0:T(8,128)S(1)} %get-tuple-element.26.total_ref, f32[4,2304,128]{2,1,0:T(8,128)S(1)} %get-tuple-element.32.pixels, ...), custom_call_target="tpu_custom_call" | custom-call | flops 12582912 | bytes 3145728 | tf_op jit(solution)/shard_map/pallas_call | solution.py:352
  51.7 0.1 collective-permute-done.7.rest_0_
  51.7 0.8 %collective-permute-done.8.rest_1_ = bf16[256,128]{1,0:T(8,128)(2,1)S(1)} collective-permute-done((bf16[256,128]{1,0:T(8,128)(2,1)S(1)}, bf16[256,128]{1,0:T(8,128)(2,1)S(1)}, u32[]{:S(2)}, u32[]{:S(2)}) %collective-permute-start.8) | collective-permute-done | bytes 65568 | tf_op jit(solution)/shard_map/ppermute | solution.py:492
  52.5 0.7 %shard_map.70 = (f32[1,656,128]{2,1,0:T(8,128)S(1)}, f32[16,128]{1,0:T(8,128)S(1)}, f32[16,128]{1,0:T(8,128)S(1)}, f32[16,128]{1,0:T(8,128)S(1)}, f32[16,128]{1,0:T(8,128)S(1)}) custom-call(bf16[5,16,128]{2,1,0:T(8,128)(2,1)S(1)} %slice.30.coeff_ref, bf16[16,64,128]{2,1,0:T(8,128)(2,1)S(1)} %slice.46.dense_ref, f32[64,128]{1,0:T(8,128)S(1)} %get-tuple-element.31.total_ref, ...), custom_call_target="tpu_custom_call" | custom-call | flops 4194304 | bytes 1048576 | tf_op jit(solution)/shard_map/pallas_call | solution.py:352
  53.2 0.4 collective-permute-start.11
  53.6 1.3 %collective-permute-start.10 = (f32[16,128]{1,0:T(8,128)S(1)}, f32[16,128]{1,0:T(8,128)S(1)}, u32[]{:S(2)}, u32[]{:S(2)}) collective-permute-start(f32[16,128]{1,0:T(8,128)S(1)} %get-tuple-element.40), channel_id=1, source_target_pairs={{0,2},{1,3},{2,0},{3,1},{4,6},{5,7},{6,4},{7,5},{8,10},{9,11},{10,... | collective-permute-start | bytes 24584 | tf_op jit(solution)/shard_map/ppermute | solution.py:534
  54.8 0.3 collective-permute-start.9
  55.1 1.7 %shard_map.71 = bf16[128,16,512]{2,1,0:T(8,128)(2,1)} custom-call(f32[1,656,128]{2,1,0:T(8,128)S(1)} %get-tuple-element.35.rest_0_, f32[3,656,128]{2,1,0:T(8,128)S(1)} %get-tuple-element.36.rest_1_, f32[4,2304,128]{2,1,0:T(8,128)S(1)} %get-tuple-element.37.rest_2_), custom_call_target="tpu_custom_call" | custom-call | flops 16777216 | bytes 4194304 | tf_op jit(solution)/shard_map/pallas_call | solution.py:369
  56.9 0.0 collective-permute-done.11
  56.9 0.4 collective-permute-done.10
  57.2 0.6 %add_add_fusion = f32[16,128]{1,0:T(8,128)} fusion(f32[16,128]{1,0:T(8,128)S(1)} %collective-permute-done.11, f32[16,128]{1,0:T(8,128)S(1)} %collective-permute-done.10, f32[16,128]{1,0:T(8,128)S(1)} %get-tuple-element.38, f32[16,128]{1,0:T(8,128)S(1)} %collective-permute-done.9), kind=kLoop, calls=%fused_computation.6 | loop fusion | flops 6144 | bytes 40960 | tf_op jit(solution)/shard_map/add | solution.py:534
  (20 shorter events, 0.1 us)
Async XLA Ops:
  0.6 12.3 %copy-start.2 = (s32[64,3]{0,1:T(4,128)S(1)}, s32[64,3]{0,1:T(4,128)}, u32[]{:S(2)}) copy-start(s32[64,3]{0,1:T(4,128)} %param.8) | copy-start | bytes 2308
  0.6 12.3 %copy-start.3 = (s32[64]{0:T(128)S(1)}, s32[64]{0:T(128)}, u32[]{:S(2)}) copy-start(s32[64]{0:T(128)} %param.9) | copy-start | bytes 772
  0.7 13.4 %copy-start.1 = (bf16[16,3,512]{2,0,1:T(8,128)(2,1)S(1)}, bf16[16,3,512]{2,0,1:T(8,128)(2,1)}, u32[]{:S(2)}) copy-start(bf16[16,3,512]{2,0,1:T(8,128)(2,1)} %param.7) | copy-start | bytes 147460
  1.7 21.2 %collective-permute-start = (bf16[256,512]{1,0:T(8,128)(2,1)S(1)}, bf16[256,512]{1,0:T(8,128)(2,1)S(1)}, u32[]{:S(2)}, u32[]{:S(2)}) collective-permute-start(bf16[256,512]{1,0:T(8,128)(2,1)S(1)} %bitcast.33), channel_id=1, source_target_pairs={{0,28},{4,24},{8,20},{12,16},{16,12},{20,8},{24,4},{28,0},{1,29},{... | collective-permute-start | bytes 786440 | tf_op jit(solution)/shard_map/ppermute | solution.py:492
  9.1 36.5 %copy-start = (bf16[5,16,512]{2,1,0:T(8,128)(2,1)S(1)}, bf16[5,16,512]{2,1,0:T(8,128)(2,1)}, u32[]{:S(2)}) copy-start(bf16[5,16,512]{2,1,0:T(8,128)(2,1)} %coeff_ref.1) | copy-start | bytes 245764
  9.2 18.1 %collective-permute-start.1 = (bf16[256,512]{1,0:T(8,128)(2,1)S(1)}, bf16[256,512]{1,0:T(8,128)(2,1)S(1)}, u32[]{:S(2)}, u32[]{:S(2)}) collective-permute-start(bf16[256,512]{1,0:T(8,128)(2,1)S(1)} %bitcast.31), channel_id=1, source_target_pairs={{0,24},{4,28},{8,16},{12,20},{16,8},{20,12},{24,0},{28,4},{1,25},{... | collective-permute-start | bytes 786440 | tf_op jit(solution)/shard_map/ppermute | solution.py:492
  9.4 10.3 %collective-permute-start.2 = (bf16[256,512]{1,0:T(8,128)(2,1)S(1)}, bf16[256,512]{1,0:T(8,128)(2,1)S(1)}, u32[]{:S(2)}, u32[]{:S(2)}) collective-permute-start(bf16[256,512]{1,0:T(8,128)(2,1)S(1)} %bitcast.32), channel_id=1, source_target_pairs={{0,4},{4,0},{8,12},{12,8},{16,20},{20,16},{24,28},{28,24},{1,5},{5... | collective-permute-start | bytes 786440 | tf_op jit(solution)/shard_map/ppermute | solution.py:492
  9.8 36.0 %collective-permute-start.3 = (bf16[256,512]{1,0:T(8,128)(2,1)S(1)}, bf16[256,512]{1,0:T(8,128)(2,1)S(1)}, u32[]{:S(2)}, u32[]{:S(2)}) collective-permute-start(bf16[256,512]{1,0:T(8,128)(2,1)S(1)} %bitcast.30), channel_id=1, source_target_pairs={{0,8},{4,12},{8,0},{12,4},{16,24},{20,28},{24,16},{28,20},{1,9},{5... | collective-permute-start | bytes 786440 | tf_op jit(solution)/shard_map/ppermute | solution.py:492
  9.8 36.0 %collective-permute-start.4 = (bf16[256,512]{1,0:T(8,128)(2,1)S(1)}, bf16[256,512]{1,0:T(8,128)(2,1)S(1)}, u32[]{:S(2)}, u32[]{:S(2)}) collective-permute-start(bf16[256,512]{1,0:T(8,128)(2,1)S(1)} %bitcast.29), channel_id=1, source_target_pairs={{0,12},{4,8},{8,4},{12,0},{16,28},{20,24},{24,20},{28,16},{1,13},{... | collective-permute-start | bytes 786440 | tf_op jit(solution)/shard_map/ppermute | solution.py:492
  19.8 25.3 %collective-permute-start.5 = (bf16[256,384]{1,0:T(8,128)(2,1)S(1)}, bf16[256,384]{1,0:T(8,128)(2,1)S(1)}, u32[]{:S(2)}, u32[]{:S(2)}) collective-permute-start(bf16[256,384]{1,0:T(8,128)(2,1)S(1)} %bitcast.35), channel_id=1, source_target_pairs={{0,20},{4,16},{8,28},{12,24},{16,4},{20,0},{24,12},{28,8},{1,21},{... | collective-permute-start | bytes 589832 | tf_op jit(solution)/shard_map/ppermute | solution.py:492
  22.8 27.8 %collective-permute-start.6 = (bf16[256,384]{1,0:T(8,128)(2,1)S(1)}, bf16[256,384]{1,0:T(8,128)(2,1)S(1)}, u32[]{:S(2)}, u32[]{:S(2)}) collective-permute-start(bf16[256,384]{1,0:T(8,128)(2,1)S(1)} %bitcast.34), channel_id=1, source_target_pairs={{0,16},{4,20},{8,24},{12,28},{16,0},{20,4},{24,8},{28,12},{1,17},{... | collective-permute-start | bytes 589832 | tf_op jit(solution)/shard_map/ppermute | solution.py:492
  27.3 24.5 %collective-permute-start.7 = (bf16[256,128]{1,0:T(8,128)(2,1)S(1)}, bf16[256,128]{1,0:T(8,128)(2,1)S(1)}, u32[]{:S(2)}, u32[]{:S(2)}) collective-permute-start(bf16[256,128]{1,0:T(8,128)(2,1)S(1)} %bitcast.37), channel_id=1, source_target_pairs={{0,20},{4,16},{8,28},{12,24},{16,4},{20,0},{24,12},{28,8},{1,21},{... | collective-permute-start | bytes 196616 | tf_op jit(solution)/shard_map/ppermute | solution.py:492
  45.0 7.5 %collective-permute-start.8 = (bf16[256,128]{1,0:T(8,128)(2,1)S(1)}, bf16[256,128]{1,0:T(8,128)(2,1)S(1)}, u32[]{:S(2)}, u32[]{:S(2)}) collective-permute-start(bf16[256,128]{1,0:T(8,128)(2,1)S(1)} %bitcast.36), channel_id=1, source_target_pairs={{0,16},{4,20},{8,24},{12,28},{16,0},{20,4},{24,8},{28,12},{1,17},{... | collective-permute-start | bytes 196616 | tf_op jit(solution)/shard_map/ppermute | solution.py:492
  53.2 3.6 %collective-permute-start.11 = (f32[16,128]{1,0:T(8,128)S(1)}, f32[16,128]{1,0:T(8,128)S(1)}, u32[]{:S(2)}, u32[]{:S(2)}) collective-permute-start(f32[16,128]{1,0:T(8,128)S(1)} %get-tuple-element.41), channel_id=1, source_target_pairs={{0,3},{1,2},{2,1},{3,0},{4,7},{5,6},{6,5},{7,4},{8,11},{9,10},{10,... | collective-permute-start | bytes 24584 | tf_op jit(solution)/shard_map/ppermute | solution.py:534
  53.6 3.7 %collective-permute-start.10 = (f32[16,128]{1,0:T(8,128)S(1)}, f32[16,128]{1,0:T(8,128)S(1)}, u32[]{:S(2)}, u32[]{:S(2)}) collective-permute-start(f32[16,128]{1,0:T(8,128)S(1)} %get-tuple-element.40), channel_id=1, source_target_pairs={{0,2},{1,3},{2,0},{3,1},{4,6},{5,7},{6,4},{7,5},{8,10},{9,11},{10,... | collective-permute-start | bytes 24584 | tf_op jit(solution)/shard_map/ppermute | solution.py:534
  54.8 2.4 %collective-permute-start.9 = (f32[16,128]{1,0:T(8,128)S(1)}, f32[16,128]{1,0:T(8,128)S(1)}, u32[]{:S(2)}, u32[]{:S(2)}) collective-permute-start(f32[16,128]{1,0:T(8,128)S(1)} %get-tuple-element.39), channel_id=1, source_target_pairs={{0,1},{1,0},{2,3},{3,2},{4,5},{5,4},{6,7},{7,6},{8,9},{9,8},{10,11... | collective-permute-start | bytes 24584 | tf_op jit(solution)/shard_map/ppermute | solution.py:534

commit v9 on v8

--- a/solution.py
+++ b/solution.py
@@ -156,21 +156,19 @@
 
 
 def project(filtered, dense_ref, first, frames):
-    rows = dense_ref.shape[0]
+    rows, tiles = dense_ref.shape[0], filtered.shape[0]
+    joined = max(1, 256 // (tiles * LANES))
     total = 0.0
-    for row in range(rows):
-        picked = jnp.concatenate(
-            [
-                filtered[tile, pl.ds(first * rows + row, frames, stride=rows), :].astype(
-                    jnp.bfloat16
-                )
-                for tile in range(filtered.shape[0])
-            ],
-            axis=1,
-        )
+    for row in range(0, rows, joined):
+        several = range(row, min(row + joined, rows))
+        picked = [
+            filtered[tile, pl.ds(first * rows + one, frames, stride=rows), :].astype(jnp.bfloat16)
+            for one in several
+            for tile in range(tiles)
+        ]
         total = total + lax.dot_general(
-            dense_ref[row],
-            picked,
+            jnp.concatenate([dense_ref[one] for one in several], axis=1),
+            jnp.concatenate(picked, axis=1),
             (((1,), (1,)), ((), ())),
             preferred_element_type=jnp.float32,
         )

time: 58.1 us -> 58.1 us (level)
  no operation moved by 1% of the time
where the time goes in v9:
time: 58.1 us; the launch traced here: 57.8 us
  starting transfers between devices  24.1 us (41%)
  waiting for transfers between devices  14.7 us (25%)
  Pallas kernels  6.81 us (12%)
  blocking collectives  5.61 us (10%)
  local copies, waits for them, and re-layouts  4.54 us (8%)
  other arithmetic  1.21 us (2%)
  between operations  0.85 us (1%)
    ppermute x9, starting transfers between devices, send(): return lax.ppermute(block, 'tm', swaps(devices, k))  22.1 us
    ppermute x9, waiting for transfers between devices, send(): return lax.ppermute(block, 'tm', swaps(devices, k))  14.4 us
    all_gather x1, blocking collectives, dense_of(): gathered = lax.all_gather(footprint_w, 'roi', axis=0, tiled=True)  5.61 us
    dynamic_slice x4, local copies, waits for them, and re-layouts, rows_of(): lax.dynamic_slice(source, (0, (here ^ k) * rows, low), (step, rows, high...  4.35 us
    pallas_call x1, Pallas kernels, run_early(): pl.pallas_call(functools.partial(early_kernel, places=tuple(places), step...  3.35 us
    ppermute x3, starting transfers between devices, local(): traces = traces + lax.ppermute(parts[k], 'roi', swaps(owners, k))  1.93 us
    pallas_call x2, Pallas kernels, run_late(): pl.pallas_call(functools.partial(late_kernel, late=tuple(late), first_til...  1.75 us
    pallas_call x1, Pallas kernels, run_delta(): pl.pallas_call(functools.partial(delta_kernel, late=tuple(late), step=ste...  1.71 us
  transfers between devices with their start and end apart: 12, of which 5 were waited for; matrix products, arithmetic and copies ran while one was open for 7% of the time, Pallas kernels for 11%

profile of v9, /device:TPU:0, one launch (start us, length us, event | category | flops | bytes accessed | tf_op | source)
XLA Modules:
  0.0 57.8 jit_solution(16138299705279470120)
XLA Ops:
  0.7 1.0 %constant_dynamic-slice_fusion.9 = bf16[16,16,512]{2,1,0:T(8,128)(2,1)S(1)} fusion(bf16[16,128,512]{2,1,0:T(8,128)(2,1)} %param.5, s32[]{:T(128)S(6)} %select_n.53), kind=kLoop, calls=%fused_computation.24 | loop fusion | bytes 524292 | tf_op jit(solution)/shard_map/dynamic_slice | solution.py:482
  1.7 6.1 %collective-permute-start = (bf16[256,512]{1,0:T(8,128)(2,1)S(1)}, bf16[256,512]{1,0:T(8,128)(2,1)S(1)}, u32[]{:S(2)}, u32[]{:S(2)}) collective-permute-start(bf16[256,512]{1,0:T(8,128)(2,1)S(1)} %bitcast.33), channel_id=1, source_target_pairs={{0,28},{4,24},{8,20},{12,16},{16,12},{20,8},{24,4},{28,0},{1,29},{... | collective-permute-start | bytes 786440 | tf_op jit(solution)/shard_map/ppermute | solution.py:490
  7.7 1.4 %constant_dynamic-slice_fusion.4 = (bf16[16,16,512]{2,1,0:T(8,128)(2,1)S(1)}, bf16[16,16,512]{2,1,0:T(8,128)(2,1)S(1)}, bf16[16,16,512]{2,1,0:T(8,128)(2,1)S(1)}...) fusion(bf16[16,128,512]{2,1,0:T(8,128)(2,1)} %param.5, s32[]{:T(128)S(6)} %select_n.58, s32[]{:T(128)S(6)} %select_n.57, ...), kind=kLoop, calls=%fused_computation.19 | loop fusion | bytes 2621460 | tf_op jit(solution)/shard_map/dynamic_slice | solution.py:482
  9.1 0.0 copy-start
  9.2 0.3 collective-permute-start.1
  9.4 0.4 collective-permute-start.2
  9.8 0.0 collective-permute-start.3
  9.8 3.1 %collective-permute-start.4 = (bf16[256,512]{1,0:T(8,128)(2,1)S(1)}, bf16[256,512]{1,0:T(8,128)(2,1)S(1)}, u32[]{:S(2)}, u32[]{:S(2)}) collective-permute-start(bf16[256,512]{1,0:T(8,128)(2,1)S(1)} %bitcast.29), channel_id=1, source_target_pairs={{0,12},{4,8},{8,4},{12,0},{16,28},{20,24},{24,20},{28,16},{1,13},{... | collective-permute-start | bytes 786440 | tf_op jit(solution)/shard_map/ppermute | solution.py:490
  13.0 1.1 %constant_dynamic-slice_fusion.2 = (bf16[16,16,384]{2,1,0:T(8,128)(2,1)S(1)}, bf16[16,16,384]{2,1,0:T(8,128)(2,1)S(1)}) fusion(bf16[16,128,512]{2,1,0:T(8,128)(2,1)} %param.5, s32[]{:T(128)S(6)} %select_n.60, s32[]{:T(128)S(6)} %select_n.59), kind=kLoop, calls=%fused_computation.17 | loop fusion | bytes 786440 | tf_op jit(solution)/shard_map/dynamic_slice | solution.py:482
  14.1 5.6 %all_gather.3 = bf16[64,3,512]{2,0,1:T(8,128)(2,1)S(1)} all-gather(bf16[16,3,512]{2,0,1:T(8,128)(2,1)S(1)} %copy-done.1), channel_id=1, replica_groups=mesh['tm'=8,'roi'=4] {'roi'}, dimensions={0}, use_global_device_ids=true | all-gather | bytes 245760 | tf_op jit(solution)/shard_map/all_gather | solution.py:462
  19.7 0.0 collective-permute-done.2.rest_2_
  19.8 2.2 %collective-permute-start.5 = (bf16[256,384]{1,0:T(8,128)(2,1)S(1)}, bf16[256,384]{1,0:T(8,128)(2,1)S(1)}, u32[]{:S(2)}, u32[]{:S(2)}) collective-permute-start(bf16[256,384]{1,0:T(8,128)(2,1)S(1)} %bitcast.35), channel_id=1, source_target_pairs={{0,20},{4,16},{8,28},{12,24},{16,4},{20,0},{24,12},{28,8},{1,21},{... | collective-permute-start | bytes 589832 | tf_op jit(solution)/shard_map/ppermute | solution.py:490
  21.9 0.9 %constant_dynamic-slice_fusion = (bf16[16,16,128]{2,1,0:T(8,128)(2,1)S(1)}, bf16[16,16,128]{2,1,0:T(8,128)(2,1)S(1)}) fusion(bf16[16,128,512]{2,1,0:T(8,128)(2,1)} %param.5, s32[]{:T(128)S(6)} %select_n.60, s32[]{:T(128)S(6)} %select_n.59), kind=kLoop, calls=%fused_computation.15 | loop fusion | bytes 262152 | tf_op jit(solution)/shard_map/dynamic_slice | solution.py:482
  22.8 0.0 collective-permute-done.rest_0_
  22.8 4.4 %collective-permute-start.6 = (bf16[256,384]{1,0:T(8,128)(2,1)S(1)}, bf16[256,384]{1,0:T(8,128)(2,1)S(1)}, u32[]{:S(2)}, u32[]{:S(2)}) collective-permute-start(bf16[256,384]{1,0:T(8,128)(2,1)S(1)} %bitcast.34), channel_id=1, source_target_pairs={{0,16},{4,20},{8,24},{12,28},{16,0},{20,4},{24,8},{28,12},{1,17},{... | collective-permute-start | bytes 589832 | tf_op jit(solution)/shard_map/ppermute | solution.py:490
  27.3 5.7 %collective-permute-start.7 = (bf16[256,128]{1,0:T(8,128)(2,1)S(1)}, bf16[256,128]{1,0:T(8,128)(2,1)S(1)}, u32[]{:S(2)}, u32[]{:S(2)}) collective-permute-start(bf16[256,128]{1,0:T(8,128)(2,1)S(1)} %bitcast.37), channel_id=1, source_target_pairs={{0,20},{4,16},{8,28},{12,24},{16,4},{20,0},{24,12},{28,8},{1,21},{... | collective-permute-start | bytes 196616 | tf_op jit(solution)/shard_map/ppermute | solution.py:490
  33.0 12.1 %collective-permute-done.5.rest_0_ = bf16[256,384]{1,0:T(8,128)(2,1)S(1)} collective-permute-done((bf16[256,384]{1,0:T(8,128)(2,1)S(1)}, bf16[256,384]{1,0:T(8,128)(2,1)S(1)}, u32[]{:S(2)}, u32[]{:S(2)}) %collective-permute-start.5) | collective-permute-done | bytes 196640 | tf_op jit(solution)/shard_map/ppermute | solution.py:490
  45.0 0.0 collective-permute-start.8
  45.0 0.6 select_add_fusion.dense_ref
  45.7 0.1 slice.47.dense_ref
  45.8 3.4 %shard_map.68 = (f32[4,2304,128]{2,1,0:T(8,128)S(1)}, f32[4,2304,128]{2,1,0:T(8,128)S(1)}, f32[64,128]{1,0:T(8,128)S(1)}) custom-call(bf16[5,16,512]{2,1,0:T(8,128)(2,1)S(1)} %copy-done, bf16[16,64,512]{2,1,0:T(8,128)(2,1)S(1)} %select_add_fusion.dense_ref, bf16[256,512]{1,0:T(8,128)(2,1)S(1)} %collective-permute-done.rest_0_, ...), custom_call_target="tpu_custom_call" | custom-call | flops 16777216 | bytes 4194304 | tf_op jit(solution)/shard_map/pallas_call | solution.py:333
  49.2 1.4 %collective-permute-done.6.rest_1_ = bf16[256,384]{1,0:T(8,128)(2,1)S(1)} collective-permute-done((bf16[256,384]{1,0:T(8,128)(2,1)S(1)}, bf16[256,384]{1,0:T(8,128)(2,1)S(1)}, u32[]{:S(2)}, u32[]{:S(2)}) %collective-permute-start.6) | collective-permute-done | bytes 196640 | tf_op jit(solution)/shard_map/ppermute | solution.py:490
  50.6 1.1 %shard_map.69 = (f32[3,656,128]{2,1,0:T(8,128)S(1)}, f32[64,128]{1,0:T(8,128)S(1)}) custom-call(bf16[5,16,384]{2,1,0:T(8,128)(2,1)S(1)} %slice.38.coeff_ref, bf16[16,64,384]{2,1,0:T(8,128)(2,1)S(1)} %slice.47.dense_ref, f32[64,128]{1,0:T(8,128)S(1)} %get-tuple-element.26.total_ref, f32[4,2304,128]{2,1,0:T(8,128)S(1)} %get-tuple-element.32.pixels, ...), custom_call_target="tpu_custom_call" | custom-call | flops 12582912 | bytes 3145728 | tf_op jit(solution)/shard_map/pallas_call | solution.py:350
  51.7 0.1 collective-permute-done.7.rest_0_
  51.7 0.8 %collective-permute-done.8.rest_1_ = bf16[256,128]{1,0:T(8,128)(2,1)S(1)} collective-permute-done((bf16[256,128]{1,0:T(8,128)(2,1)S(1)}, bf16[256,128]{1,0:T(8,128)(2,1)S(1)}, u32[]{:S(2)}, u32[]{:S(2)}) %collective-permute-start.8) | collective-permute-done | bytes 65568 | tf_op jit(solution)/shard_map/ppermute | solution.py:490
  52.5 0.7 %shard_map.70 = (f32[1,656,128]{2,1,0:T(8,128)S(1)}, f32[16,128]{1,0:T(8,128)S(1)}, f32[16,128]{1,0:T(8,128)S(1)}, f32[16,128]{1,0:T(8,128)S(1)}, f32[16,128]{1,0:T(8,128)S(1)}) custom-call(bf16[5,16,128]{2,1,0:T(8,128)(2,1)S(1)} %slice.30.coeff_ref, bf16[16,64,128]{2,1,0:T(8,128)(2,1)S(1)} %slice.46.dense_ref, f32[64,128]{1,0:T(8,128)S(1)} %get-tuple-element.31.total_ref, ...), custom_call_target="tpu_custom_call" | custom-call | flops 4194304 | bytes 1048576 | tf_op jit(solution)/shard_map/pallas_call | solution.py:350
  53.2 0.4 collective-permute-start.11
  53.6 1.3 %collective-permute-start.10 = (f32[16,128]{1,0:T(8,128)S(1)}, f32[16,128]{1,0:T(8,128)S(1)}, u32[]{:S(2)}, u32[]{:S(2)}) collective-permute-start(f32[16,128]{1,0:T(8,128)S(1)} %get-tuple-element.40), channel_id=1, source_target_pairs={{0,2},{1,3},{2,0},{3,1},{4,6},{5,7},{6,4},{7,5},{8,10},{9,11},{10,... | collective-permute-start | bytes 24584 | tf_op jit(solution)/shard_map/ppermute | solution.py:532
  54.8 0.3 collective-permute-start.9
  55.1 1.7 %shard_map.71 = bf16[128,16,512]{2,1,0:T(8,128)(2,1)} custom-call(f32[1,656,128]{2,1,0:T(8,128)S(1)} %get-tuple-element.35.rest_0_, f32[3,656,128]{2,1,0:T(8,128)S(1)} %get-tuple-element.36.rest_1_, f32[4,2304,128]{2,1,0:T(8,128)S(1)} %get-tuple-element.37.rest_2_), custom_call_target="tpu_custom_call" | custom-call | flops 16777216 | bytes 4194304 | tf_op jit(solution)/shard_map/pallas_call | solution.py:367
  56.8 0.4 collective-permute-done.10
  57.2 0.6 %add_add_fusion = f32[16,128]{1,0:T(8,128)} fusion(f32[16,128]{1,0:T(8,128)S(1)} %collective-permute-done.11, f32[16,128]{1,0:T(8,128)S(1)} %collective-permute-done.10, f32[16,128]{1,0:T(8,128)S(1)} %get-tuple-element.38, f32[16,128]{1,0:T(8,128)S(1)} %collective-permute-done.9), kind=kLoop, calls=%fused_computation.6 | loop fusion | flops 6144 | bytes 40960 | tf_op jit(solution)/shard_map/add | solution.py:532
  (20 shorter events, 0.1 us)
Async XLA Ops:
  0.6 12.3 %copy-start.2 = (s32[64,3]{0,1:T(4,128)S(1)}, s32[64,3]{0,1:T(4,128)}, u32[]{:S(2)}) copy-start(s32[64,3]{0,1:T(4,128)} %param.8) | copy-start | bytes 2308
  0.6 12.3 %copy-start.3 = (s32[64]{0:T(128)S(1)}, s32[64]{0:T(128)}, u32[]{:S(2)}) copy-start(s32[64]{0:T(128)} %param.9) | copy-start | bytes 772
  0.7 13.4 %copy-start.1 = (bf16[16,3,512]{2,0,1:T(8,128)(2,1)S(1)}, bf16[16,3,512]{2,0,1:T(8,128)(2,1)}, u32[]{:S(2)}) copy-start(bf16[16,3,512]{2,0,1:T(8,128)(2,1)} %param.7) | copy-start | bytes 147460
  1.7 21.2 %collective-permute-start = (bf16[256,512]{1,0:T(8,128)(2,1)S(1)}, bf16[256,512]{1,0:T(8,128)(2,1)S(1)}, u32[]{:S(2)}, u32[]{:S(2)}) collective-permute-start(bf16[256,512]{1,0:T(8,128)(2,1)S(1)} %bitcast.33), channel_id=1, source_target_pairs={{0,28},{4,24},{8,20},{12,16},{16,12},{20,8},{24,4},{28,0},{1,29},{... | collective-permute-start | bytes 786440 | tf_op jit(solution)/shard_map/ppermute | solution.py:490
  9.1 36.5 %copy-start = (bf16[5,16,512]{2,1,0:T(8,128)(2,1)S(1)}, bf16[5,16,512]{2,1,0:T(8,128)(2,1)}, u32[]{:S(2)}) copy-start(bf16[5,16,512]{2,1,0:T(8,128)(2,1)} %coeff_ref.1) | copy-start | bytes 245764
  9.2 18.1 %collective-permute-start.1 = (bf16[256,512]{1,0:T(8,128)(2,1)S(1)}, bf16[256,512]{1,0:T(8,128)(2,1)S(1)}, u32[]{:S(2)}, u32[]{:S(2)}) collective-permute-start(bf16[256,512]{1,0:T(8,128)(2,1)S(1)} %bitcast.31), channel_id=1, source_target_pairs={{0,24},{4,28},{8,16},{12,20},{16,8},{20,12},{24,0},{28,4},{1,25},{... | collective-permute-start | bytes 786440 | tf_op jit(solution)/shard_map/ppermute | solution.py:490
  9.4 10.3 %collective-permute-start.2 = (bf16[256,512]{1,0:T(8,128)(2,1)S(1)}, bf16[256,512]{1,0:T(8,128)(2,1)S(1)}, u32[]{:S(2)}, u32[]{:S(2)}) collective-permute-start(bf16[256,512]{1,0:T(8,128)(2,1)S(1)} %bitcast.32), channel_id=1, source_target_pairs={{0,4},{4,0},{8,12},{12,8},{16,20},{20,16},{24,28},{28,24},{1,5},{5... | collective-permute-start | bytes 786440 | tf_op jit(solution)/shard_map/ppermute | solution.py:490
  9.8 36.0 %collective-permute-start.3 = (bf16[256,512]{1,0:T(8,128)(2,1)S(1)}, bf16[256,512]{1,0:T(8,128)(2,1)S(1)}, u32[]{:S(2)}, u32[]{:S(2)}) collective-permute-start(bf16[256,512]{1,0:T(8,128)(2,1)S(1)} %bitcast.30), channel_id=1, source_target_pairs={{0,8},{4,12},{8,0},{12,4},{16,24},{20,28},{24,16},{28,20},{1,9},{5... | collective-permute-start | bytes 786440 | tf_op jit(solution)/shard_map/ppermute | solution.py:490
  9.8 36.0 %collective-permute-start.4 = (bf16[256,512]{1,0:T(8,128)(2,1)S(1)}, bf16[256,512]{1,0:T(8,128)(2,1)S(1)}, u32[]{:S(2)}, u32[]{:S(2)}) collective-permute-start(bf16[256,512]{1,0:T(8,128)(2,1)S(1)} %bitcast.29), channel_id=1, source_target_pairs={{0,12},{4,8},{8,4},{12,0},{16,28},{20,24},{24,20},{28,16},{1,13},{... | collective-permute-start | bytes 786440 | tf_op jit(solution)/shard_map/ppermute | solution.py:490
  19.8 25.3 %collective-permute-start.5 = (bf16[256,384]{1,0:T(8,128)(2,1)S(1)}, bf16[256,384]{1,0:T(8,128)(2,1)S(1)}, u32[]{:S(2)}, u32[]{:S(2)}) collective-permute-start(bf16[256,384]{1,0:T(8,128)(2,1)S(1)} %bitcast.35), channel_id=1, source_target_pairs={{0,20},{4,16},{8,28},{12,24},{16,4},{20,0},{24,12},{28,8},{1,21},{... | collective-permute-start | bytes 589832 | tf_op jit(solution)/shard_map/ppermute | solution.py:490
  22.8 27.8 %collective-permute-start.6 = (bf16[256,384]{1,0:T(8,128)(2,1)S(1)}, bf16[256,384]{1,0:T(8,128)(2,1)S(1)}, u32[]{:S(2)}, u32[]{:S(2)}) collective-permute-start(bf16[256,384]{1,0:T(8,128)(2,1)S(1)} %bitcast.34), channel_id=1, source_target_pairs={{0,16},{4,20},{8,24},{12,28},{16,0},{20,4},{24,8},{28,12},{1,17},{... | collective-permute-start | bytes 589832 | tf_op jit(solution)/shard_map/ppermute | solution.py:490
  27.3 24.5 %collective-permute-start.7 = (bf16[256,128]{1,0:T(8,128)(2,1)S(1)}, bf16[256,128]{1,0:T(8,128)(2,1)S(1)}, u32[]{:S(2)}, u32[]{:S(2)}) collective-permute-start(bf16[256,128]{1,0:T(8,128)(2,1)S(1)} %bitcast.37), channel_id=1, source_target_pairs={{0,20},{4,16},{8,28},{12,24},{16,4},{20,0},{24,12},{28,8},{1,21},{... | collective-permute-start | bytes 196616 | tf_op jit(solution)/shard_map/ppermute | solution.py:490
  45.0 7.5 %collective-permute-start.8 = (bf16[256,128]{1,0:T(8,128)(2,1)S(1)}, bf16[256,128]{1,0:T(8,128)(2,1)S(1)}, u32[]{:S(2)}, u32[]{:S(2)}) collective-permute-start(bf16[256,128]{1,0:T(8,128)(2,1)S(1)} %bitcast.36), channel_id=1, source_target_pairs={{0,16},{4,20},{8,24},{12,28},{16,0},{20,4},{24,8},{28,12},{1,17},{... | collective-permute-start | bytes 196616 | tf_op jit(solution)/shard_map/ppermute | solution.py:490
  53.2 3.6 %collective-permute-start.11 = (f32[16,128]{1,0:T(8,128)S(1)}, f32[16,128]{1,0:T(8,128)S(1)}, u32[]{:S(2)}, u32[]{:S(2)}) collective-permute-start(f32[16,128]{1,0:T(8,128)S(1)} %get-tuple-element.41), channel_id=1, source_target_pairs={{0,3},{1,2},{2,1},{3,0},{4,7},{5,6},{6,5},{7,4},{8,11},{9,10},{10,... | collective-permute-start | bytes 24584 | tf_op jit(solution)/shard_map/ppermute | solution.py:532
  53.6 3.7 %collective-permute-start.10 = (f32[16,128]{1,0:T(8,128)S(1)}, f32[16,128]{1,0:T(8,128)S(1)}, u32[]{:S(2)}, u32[]{:S(2)}) collective-permute-start(f32[16,128]{1,0:T(8,128)S(1)} %get-tuple-element.40), channel_id=1, source_target_pairs={{0,2},{1,3},{2,0},{3,1},{4,6},{5,7},{6,4},{7,5},{8,10},{9,11},{10,... | collective-permute-start | bytes 24584 | tf_op jit(solution)/shard_map/ppermute | solution.py:532
  54.8 2.4 %collective-permute-start.9 = (f32[16,128]{1,0:T(8,128)S(1)}, f32[16,128]{1,0:T(8,128)S(1)}, u32[]{:S(2)}, u32[]{:S(2)}) collective-permute-start(f32[16,128]{1,0:T(8,128)S(1)} %get-tuple-element.39), channel_id=1, source_target_pairs={{0,1},{1,0},{2,3},{3,2},{4,5},{5,4},{6,7},{7,6},{8,9},{9,8},{10,11... | collective-permute-start | bytes 24584 | tf_op jit(solution)/shard_map/ppermute | solution.py:532

commit v10 on v9

--- a/solution.py
+++ b/solution.py
@@ -198,9 +198,10 @@
     rest = total - high.astype(jnp.float32)
     middle = rest.astype(jnp.bfloat16)
     low = (rest - middle.astype(jnp.float32)).astype(jnp.bfloat16)
-    running = sum(
-        jnp.dot(term, upto, preferred_element_type=jnp.float32) for term in (low, middle, high)
-    )
+    terms = jnp.concatenate([low, middle, high], axis=0)
+    sums = jnp.dot(terms, upto, preferred_element_type=jnp.float32)
+    height = total.shape[0]
+    running = sums[:height] + sums[height : 2 * height] + sums[2 * height :]
     frame_ids = lax.broadcasted_iota(jnp.int32, total.shape, 1)
     return total - running / jnp.minimum(frame_ids + 1, BASE_WIN).astype(jnp.float32)
 

time: 58.1 us -> 58.1 us (level)
  no operation moved by 1% of the time
where the time goes in v10:
time: 58.1 us; the launch traced here: 57.8 us
  starting transfers between devices  24.1 us (41%)
  waiting for transfers between devices  14.7 us (25%)
  Pallas kernels  6.81 us (12%)
  blocking collectives  5.61 us (10%)
  local copies, waits for them, and re-layouts  4.54 us (8%)
  other arithmetic  1.21 us (2%)
  between operations  0.86 us (1%)
    ppermute x9, starting transfers between devices, send(): return lax.ppermute(block, 'tm', swaps(devices, k))  22.1 us
    ppermute x9, waiting for transfers between devices, send(): return lax.ppermute(block, 'tm', swaps(devices, k))  14.4 us
    all_gather x1, blocking collectives, dense_of(): gathered = lax.all_gather(footprint_w, 'roi', axis=0, tiled=True)  5.61 us
    dynamic_slice x4, local copies, waits for them, and re-layouts, rows_of(): lax.dynamic_slice(source, (0, (here ^ k) * rows, low), (step, rows, high...  4.35 us
    pallas_call x1, Pallas kernels, run_early(): pl.pallas_call(functools.partial(early_kernel, places=tuple(places), step...  3.35 us
    ppermute x3, starting transfers between devices, local(): traces = traces + lax.ppermute(parts[k], 'roi', swaps(owners, k))  1.93 us
    pallas_call x2, Pallas kernels, run_late(): pl.pallas_call(functools.partial(late_kernel, late=tuple(late), first_til...  1.75 us
    pallas_call x1, Pallas kernels, run_delta(): pl.pallas_call(functools.partial(delta_kernel, late=tuple(late), step=ste...  1.71 us
  transfers between devices with their start and end apart: 12, of which 5 were waited for; matrix products, arithmetic and copies ran while one was open for 7% of the time, Pallas kernels for 11%

profile of v10, /device:TPU:0, one launch (start us, length us, event | category | flops | bytes accessed | tf_op | source)
XLA Modules:
  0.0 57.8 jit_solution(11031030281836491571)
XLA Ops:
  0.7 1.0 %constant_dynamic-slice_fusion.9 = bf16[16,16,512]{2,1,0:T(8,128)(2,1)S(1)} fusion(bf16[16,128,512]{2,1,0:T(8,128)(2,1)} %param.5, s32[]{:T(128)S(6)} %select_n.53), kind=kLoop, calls=%fused_computation.24 | loop fusion | bytes 524292 | tf_op jit(solution)/shard_map/dynamic_slice | solution.py:483
  1.7 6.1 %collective-permute-start = (bf16[256,512]{1,0:T(8,128)(2,1)S(1)}, bf16[256,512]{1,0:T(8,128)(2,1)S(1)}, u32[]{:S(2)}, u32[]{:S(2)}) collective-permute-start(bf16[256,512]{1,0:T(8,128)(2,1)S(1)} %bitcast.33), channel_id=1, source_target_pairs={{0,28},{4,24},{8,20},{12,16},{16,12},{20,8},{24,4},{28,0},{1,29},{... | collective-permute-start | bytes 786440 | tf_op jit(solution)/shard_map/ppermute | solution.py:491
  7.7 1.4 %constant_dynamic-slice_fusion.4 = (bf16[16,16,512]{2,1,0:T(8,128)(2,1)S(1)}, bf16[16,16,512]{2,1,0:T(8,128)(2,1)S(1)}, bf16[16,16,512]{2,1,0:T(8,128)(2,1)S(1)}...) fusion(bf16[16,128,512]{2,1,0:T(8,128)(2,1)} %param.5, s32[]{:T(128)S(6)} %select_n.58, s32[]{:T(128)S(6)} %select_n.57, ...), kind=kLoop, calls=%fused_computation.19 | loop fusion | bytes 2621460 | tf_op jit(solution)/shard_map/dynamic_slice | solution.py:483
  9.1 0.0 copy-start
  9.2 0.3 collective-permute-start.1
  9.4 0.4 collective-permute-start.2
  9.8 0.0 collective-permute-start.3
  9.8 3.1 %collective-permute-start.4 = (bf16[256,512]{1,0:T(8,128)(2,1)S(1)}, bf16[256,512]{1,0:T(8,128)(2,1)S(1)}, u32[]{:S(2)}, u32[]{:S(2)}) collective-permute-start(bf16[256,512]{1,0:T(8,128)(2,1)S(1)} %bitcast.29), channel_id=1, source_target_pairs={{0,12},{4,8},{8,4},{12,0},{16,28},{20,24},{24,20},{28,16},{1,13},{... | collective-permute-start | bytes 786440 | tf_op jit(solution)/shard_map/ppermute | solution.py:491
  13.0 1.1 %constant_dynamic-slice_fusion.2 = (bf16[16,16,384]{2,1,0:T(8,128)(2,1)S(1)}, bf16[16,16,384]{2,1,0:T(8,128)(2,1)S(1)}) fusion(bf16[16,128,512]{2,1,0:T(8,128)(2,1)} %param.5, s32[]{:T(128)S(6)} %select_n.60, s32[]{:T(128)S(6)} %select_n.59), kind=kLoop, calls=%fused_computation.17 | loop fusion | bytes 786440 | tf_op jit(solution)/shard_map/dynamic_slice | solution.py:483
  14.1 5.6 %all_gather.3 = bf16[64,3,512]{2,0,1:T(8,128)(2,1)S(1)} all-gather(bf16[16,3,512]{2,0,1:T(8,128)(2,1)S(1)} %copy-done.1), channel_id=1, replica_groups=mesh['tm'=8,'roi'=4] {'roi'}, dimensions={0}, use_global_device_ids=true | all-gather | bytes 245760 | tf_op jit(solution)/shard_map/all_gather | solution.py:463
  19.7 0.0 collective-permute-done.2.rest_2_
  19.8 2.2 %collective-permute-start.5 = (bf16[256,384]{1,0:T(8,128)(2,1)S(1)}, bf16[256,384]{1,0:T(8,128)(2,1)S(1)}, u32[]{:S(2)}, u32[]{:S(2)}) collective-permute-start(bf16[256,384]{1,0:T(8,128)(2,1)S(1)} %bitcast.35), channel_id=1, source_target_pairs={{0,20},{4,16},{8,28},{12,24},{16,4},{20,0},{24,12},{28,8},{1,21},{... | collective-permute-start | bytes 589832 | tf_op jit(solution)/shard_map/ppermute | solution.py:491
  21.9 0.9 %constant_dynamic-slice_fusion = (bf16[16,16,128]{2,1,0:T(8,128)(2,1)S(1)}, bf16[16,16,128]{2,1,0:T(8,128)(2,1)S(1)}) fusion(bf16[16,128,512]{2,1,0:T(8,128)(2,1)} %param.5, s32[]{:T(128)S(6)} %select_n.60, s32[]{:T(128)S(6)} %select_n.59), kind=kLoop, calls=%fused_computation.15 | loop fusion | bytes 262152 | tf_op jit(solution)/shard_map/dynamic_slice | solution.py:483
  22.8 0.0 collective-permute-done.rest_0_
  22.8 4.4 %collective-permute-start.6 = (bf16[256,384]{1,0:T(8,128)(2,1)S(1)}, bf16[256,384]{1,0:T(8,128)(2,1)S(1)}, u32[]{:S(2)}, u32[]{:S(2)}) collective-permute-start(bf16[256,384]{1,0:T(8,128)(2,1)S(1)} %bitcast.34), channel_id=1, source_target_pairs={{0,16},{4,20},{8,24},{12,28},{16,0},{20,4},{24,8},{28,12},{1,17},{... | collective-permute-start | bytes 589832 | tf_op jit(solution)/shard_map/ppermute | solution.py:491
  27.3 5.7 %collective-permute-start.7 = (bf16[256,128]{1,0:T(8,128)(2,1)S(1)}, bf16[256,128]{1,0:T(8,128)(2,1)S(1)}, u32[]{:S(2)}, u32[]{:S(2)}) collective-permute-start(bf16[256,128]{1,0:T(8,128)(2,1)S(1)} %bitcast.37), channel_id=1, source_target_pairs={{0,20},{4,16},{8,28},{12,24},{16,4},{20,0},{24,12},{28,8},{1,21},{... | collective-permute-start | bytes 196616 | tf_op jit(solution)/shard_map/ppermute | solution.py:491
  33.0 12.1 %collective-permute-done.5.rest_0_ = bf16[256,384]{1,0:T(8,128)(2,1)S(1)} collective-permute-done((bf16[256,384]{1,0:T(8,128)(2,1)S(1)}, bf16[256,384]{1,0:T(8,128)(2,1)S(1)}, u32[]{:S(2)}, u32[]{:S(2)}) %collective-permute-start.5) | collective-permute-done | bytes 196640 | tf_op jit(solution)/shard_map/ppermute | solution.py:491
  45.0 0.0 collective-permute-start.8
  45.0 0.6 select_add_fusion.dense_ref
  45.7 0.1 slice.47.dense_ref
  45.8 3.4 %shard_map.68 = (f32[4,2304,128]{2,1,0:T(8,128)S(1)}, f32[4,2304,128]{2,1,0:T(8,128)S(1)}, f32[64,128]{1,0:T(8,128)S(1)}) custom-call(bf16[5,16,512]{2,1,0:T(8,128)(2,1)S(1)} %copy-done, bf16[16,64,512]{2,1,0:T(8,128)(2,1)S(1)} %select_add_fusion.dense_ref, bf16[256,512]{1,0:T(8,128)(2,1)S(1)} %collective-permute-done.rest_0_, ...), custom_call_target="tpu_custom_call" | custom-call | flops 16777216 | bytes 4194304 | tf_op jit(solution)/shard_map/pallas_call | solution.py:334
  49.2 1.4 %collective-permute-done.6.rest_1_ = bf16[256,384]{1,0:T(8,128)(2,1)S(1)} collective-permute-done((bf16[256,384]{1,0:T(8,128)(2,1)S(1)}, bf16[256,384]{1,0:T(8,128)(2,1)S(1)}, u32[]{:S(2)}, u32[]{:S(2)}) %collective-permute-start.6) | collective-permute-done | bytes 196640 | tf_op jit(solution)/shard_map/ppermute | solution.py:491
  50.6 1.1 %shard_map.69 = (f32[3,656,128]{2,1,0:T(8,128)S(1)}, f32[64,128]{1,0:T(8,128)S(1)}) custom-call(bf16[5,16,384]{2,1,0:T(8,128)(2,1)S(1)} %slice.38.coeff_ref, bf16[16,64,384]{2,1,0:T(8,128)(2,1)S(1)} %slice.47.dense_ref, f32[64,128]{1,0:T(8,128)S(1)} %get-tuple-element.26.total_ref, f32[4,2304,128]{2,1,0:T(8,128)S(1)} %get-tuple-element.32.pixels, ...), custom_call_target="tpu_custom_call" | custom-call | flops 12582912 | bytes 3145728 | tf_op jit(solution)/shard_map/pallas_call | solution.py:351
  51.7 0.1 collective-permute-done.7.rest_0_
  51.7 0.8 %collective-permute-done.8.rest_1_ = bf16[256,128]{1,0:T(8,128)(2,1)S(1)} collective-permute-done((bf16[256,128]{1,0:T(8,128)(2,1)S(1)}, bf16[256,128]{1,0:T(8,128)(2,1)S(1)}, u32[]{:S(2)}, u32[]{:S(2)}) %collective-permute-start.8) | collective-permute-done | bytes 65568 | tf_op jit(solution)/shard_map/ppermute | solution.py:491
  52.5 0.7 %shard_map.70 = (f32[1,656,128]{2,1,0:T(8,128)S(1)}, f32[16,128]{1,0:T(8,128)S(1)}, f32[16,128]{1,0:T(8,128)S(1)}, f32[16,128]{1,0:T(8,128)S(1)}, f32[16,128]{1,0:T(8,128)S(1)}) custom-call(bf16[5,16,128]{2,1,0:T(8,128)(2,1)S(1)} %slice.30.coeff_ref, bf16[16,64,128]{2,1,0:T(8,128)(2,1)S(1)} %slice.46.dense_ref, f32[64,128]{1,0:T(8,128)S(1)} %get-tuple-element.31.total_ref, ...), custom_call_target="tpu_custom_call" | custom-call | flops 4194304 | bytes 1048576 | tf_op jit(solution)/shard_map/pallas_call | solution.py:351
  53.2 0.4 collective-permute-start.11
  53.6 1.3 %collective-permute-start.10 = (f32[16,128]{1,0:T(8,128)S(1)}, f32[16,128]{1,0:T(8,128)S(1)}, u32[]{:S(2)}, u32[]{:S(2)}) collective-permute-start(f32[16,128]{1,0:T(8,128)S(1)} %get-tuple-element.40), channel_id=1, source_target_pairs={{0,2},{1,3},{2,0},{3,1},{4,6},{5,7},{6,4},{7,5},{8,10},{9,11},{10,... | collective-permute-start | bytes 24584 | tf_op jit(solution)/shard_map/ppermute | solution.py:533
  54.8 0.3 collective-permute-start.9
  55.1 1.7 %shard_map.71 = bf16[128,16,512]{2,1,0:T(8,128)(2,1)} custom-call(f32[1,656,128]{2,1,0:T(8,128)S(1)} %get-tuple-element.35.rest_0_, f32[3,656,128]{2,1,0:T(8,128)S(1)} %get-tuple-element.36.rest_1_, f32[4,2304,128]{2,1,0:T(8,128)S(1)} %get-tuple-element.37.rest_2_), custom_call_target="tpu_custom_call" | custom-call | flops 16777216 | bytes 4194304 | tf_op jit(solution)/shard_map/pallas_call | solution.py:368
  56.8 0.4 collective-permute-done.10
  57.2 0.6 %add_add_fusion = f32[16,128]{1,0:T(8,128)} fusion(f32[16,128]{1,0:T(8,128)S(1)} %collective-permute-done.11, f32[16,128]{1,0:T(8,128)S(1)} %collective-permute-done.10, f32[16,128]{1,0:T(8,128)S(1)} %get-tuple-element.38, f32[16,128]{1,0:T(8,128)S(1)} %collective-permute-done.9), kind=kLoop, calls=%fused_computation.6 | loop fusion | flops 6144 | bytes 40960 | tf_op jit(solution)/shard_map/add | solution.py:533
  (20 shorter events, 0.1 us)
Async XLA Ops:
  0.6 12.3 %copy-start.2 = (s32[64,3]{0,1:T(4,128)S(1)}, s32[64,3]{0,1:T(4,128)}, u32[]{:S(2)}) copy-start(s32[64,3]{0,1:T(4,128)} %param.8) | copy-start | bytes 2308
  0.6 12.3 %copy-start.3 = (s32[64]{0:T(128)S(1)}, s32[64]{0:T(128)}, u32[]{:S(2)}) copy-start(s32[64]{0:T(128)} %param.9) | copy-start | bytes 772
  0.7 13.4 %copy-start.1 = (bf16[16,3,512]{2,0,1:T(8,128)(2,1)S(1)}, bf16[16,3,512]{2,0,1:T(8,128)(2,1)}, u32[]{:S(2)}) copy-start(bf16[16,3,512]{2,0,1:T(8,128)(2,1)} %param.7) | copy-start | bytes 147460
  1.7 21.2 %collective-permute-start = (bf16[256,512]{1,0:T(8,128)(2,1)S(1)}, bf16[256,512]{1,0:T(8,128)(2,1)S(1)}, u32[]{:S(2)}, u32[]{:S(2)}) collective-permute-start(bf16[256,512]{1,0:T(8,128)(2,1)S(1)} %bitcast.33), channel_id=1, source_target_pairs={{0,28},{4,24},{8,20},{12,16},{16,12},{20,8},{24,4},{28,0},{1,29},{... | collective-permute-start | bytes 786440 | tf_op jit(solution)/shard_map/ppermute | solution.py:491
  9.1 36.5 %copy-start = (bf16[5,16,512]{2,1,0:T(8,128)(2,1)S(1)}, bf16[5,16,512]{2,1,0:T(8,128)(2,1)}, u32[]{:S(2)}) copy-start(bf16[5,16,512]{2,1,0:T(8,128)(2,1)} %coeff_ref.1) | copy-start | bytes 245764
  9.2 18.1 %collective-permute-start.1 = (bf16[256,512]{1,0:T(8,128)(2,1)S(1)}, bf16[256,512]{1,0:T(8,128)(2,1)S(1)}, u32[]{:S(2)}, u32[]{:S(2)}) collective-permute-start(bf16[256,512]{1,0:T(8,128)(2,1)S(1)} %bitcast.31), channel_id=1, source_target_pairs={{0,24},{4,28},{8,16},{12,20},{16,8},{20,12},{24,0},{28,4},{1,25},{... | collective-permute-start | bytes 786440 | tf_op jit(solution)/shard_map/ppermute | solution.py:491
  9.4 10.3 %collective-permute-start.2 = (bf16[256,512]{1,0:T(8,128)(2,1)S(1)}, bf16[256,512]{1,0:T(8,128)(2,1)S(1)}, u32[]{:S(2)}, u32[]{:S(2)}) collective-permute-start(bf16[256,512]{1,0:T(8,128)(2,1)S(1)} %bitcast.32), channel_id=1, source_target_pairs={{0,4},{4,0},{8,12},{12,8},{16,20},{20,16},{24,28},{28,24},{1,5},{5... | collective-permute-start | bytes 786440 | tf_op jit(solution)/shard_map/ppermute | solution.py:491
  9.8 36.0 %collective-permute-start.3 = (bf16[256,512]{1,0:T(8,128)(2,1)S(1)}, bf16[256,512]{1,0:T(8,128)(2,1)S(1)}, u32[]{:S(2)}, u32[]{:S(2)}) collective-permute-start(bf16[256,512]{1,0:T(8,128)(2,1)S(1)} %bitcast.30), channel_id=1, source_target_pairs={{0,8},{4,12},{8,0},{12,4},{16,24},{20,28},{24,16},{28,20},{1,9},{5... | collective-permute-start | bytes 786440 | tf_op jit(solution)/shard_map/ppermute | solution.py:491
  9.8 36.0 %collective-permute-start.4 = (bf16[256,512]{1,0:T(8,128)(2,1)S(1)}, bf16[256,512]{1,0:T(8,128)(2,1)S(1)}, u32[]{:S(2)}, u32[]{:S(2)}) collective-permute-start(bf16[256,512]{1,0:T(8,128)(2,1)S(1)} %bitcast.29), channel_id=1, source_target_pairs={{0,12},{4,8},{8,4},{12,0},{16,28},{20,24},{24,20},{28,16},{1,13},{... | collective-permute-start | bytes 786440 | tf_op jit(solution)/shard_map/ppermute | solution.py:491
  19.8 25.3 %collective-permute-start.5 = (bf16[256,384]{1,0:T(8,128)(2,1)S(1)}, bf16[256,384]{1,0:T(8,128)(2,1)S(1)}, u32[]{:S(2)}, u32[]{:S(2)}) collective-permute-start(bf16[256,384]{1,0:T(8,128)(2,1)S(1)} %bitcast.35), channel_id=1, source_target_pairs={{0,20},{4,16},{8,28},{12,24},{16,4},{20,0},{24,12},{28,8},{1,21},{... | collective-permute-start | bytes 589832 | tf_op jit(solution)/shard_map/ppermute | solution.py:491
  22.8 27.8 %collective-permute-start.6 = (bf16[256,384]{1,0:T(8,128)(2,1)S(1)}, bf16[256,384]{1,0:T(8,128)(2,1)S(1)}, u32[]{:S(2)}, u32[]{:S(2)}) collective-permute-start(bf16[256,384]{1,0:T(8,128)(2,1)S(1)} %bitcast.34), channel_id=1, source_target_pairs={{0,16},{4,20},{8,24},{12,28},{16,0},{20,4},{24,8},{28,12},{1,17},{... | collective-permute-start | bytes 589832 | tf_op jit(solution)/shard_map/ppermute | solution.py:491
  27.3 24.5 %collective-permute-start.7 = (bf16[256,128]{1,0:T(8,128)(2,1)S(1)}, bf16[256,128]{1,0:T(8,128)(2,1)S(1)}, u32[]{:S(2)}, u32[]{:S(2)}) collective-permute-start(bf16[256,128]{1,0:T(8,128)(2,1)S(1)} %bitcast.37), channel_id=1, source_target_pairs={{0,20},{4,16},{8,28},{12,24},{16,4},{20,0},{24,12},{28,8},{1,21},{... | collective-permute-start | bytes 196616 | tf_op jit(solution)/shard_map/ppermute | solution.py:491
  45.0 7.5 %collective-permute-start.8 = (bf16[256,128]{1,0:T(8,128)(2,1)S(1)}, bf16[256,128]{1,0:T(8,128)(2,1)S(1)}, u32[]{:S(2)}, u32[]{:S(2)}) collective-permute-start(bf16[256,128]{1,0:T(8,128)(2,1)S(1)} %bitcast.36), channel_id=1, source_target_pairs={{0,16},{4,20},{8,24},{12,28},{16,0},{20,4},{24,8},{28,12},{1,17},{... | collective-permute-start | bytes 196616 | tf_op jit(solution)/shard_map/ppermute | solution.py:491
  53.2 3.6 %collective-permute-start.11 = (f32[16,128]{1,0:T(8,128)S(1)}, f32[16,128]{1,0:T(8,128)S(1)}, u32[]{:S(2)}, u32[]{:S(2)}) collective-permute-start(f32[16,128]{1,0:T(8,128)S(1)} %get-tuple-element.41), channel_id=1, source_target_pairs={{0,3},{1,2},{2,1},{3,0},{4,7},{5,6},{6,5},{7,4},{8,11},{9,10},{10,... | collective-permute-start | bytes 24584 | tf_op jit(solution)/shard_map/ppermute | solution.py:533
  53.6 3.7 %collective-permute-start.10 = (f32[16,128]{1,0:T(8,128)S(1)}, f32[16,128]{1,0:T(8,128)S(1)}, u32[]{:S(2)}, u32[]{:S(2)}) collective-permute-start(f32[16,128]{1,0:T(8,128)S(1)} %get-tuple-element.40), channel_id=1, source_target_pairs={{0,2},{1,3},{2,0},{3,1},{4,6},{5,7},{6,4},{7,5},{8,10},{9,11},{10,... | collective-permute-start | bytes 24584 | tf_op jit(solution)/shard_map/ppermute | solution.py:533
  54.8 2.4 %collective-permute-start.9 = (f32[16,128]{1,0:T(8,128)S(1)}, f32[16,128]{1,0:T(8,128)S(1)}, u32[]{:S(2)}, u32[]{:S(2)}) collective-permute-start(f32[16,128]{1,0:T(8,128)S(1)} %get-tuple-element.39), channel_id=1, source_target_pairs={{0,1},{1,0},{2,3},{3,2},{4,5},{5,4},{6,7},{7,6},{8,9},{9,8},{10,11... | collective-permute-start | bytes 24584 | tf_op jit(solution)/shard_map/ppermute | solution.py:533
